TPU v7x, 32 devices: a whole 2x2x4 slice. The times are simulated.
32 devices in a mesh: dp: 2 (over core), ctx: 16 (over z, y, x).
Axes of the slice: x: 2, y: 2, z: 4, core: 2. Of those that a mesh axis runs over, the one named last changes fastest.
Arguments:
- tokens: bfloat16 [2, 2048, 1024], P('dp', 'ctx'), may hold values from -6 to 6
- cotangent: bfloat16 [2, 2048, 1024], P('dp', 'ctx'), may hold values from -6 to 6
- block_order: int32 [32], replicated, may hold values from 0 to 31, each once
- doc_lengths: int32 [2, 8], P('dp'), may hold values from 1 to 1024, 2048 in all within a row
- routes: int32 [2, 2048, 1], P('dp', 'ctx'), may hold values from 0 to 15; in each aligned block of 128 rows (0 to 127, 128 to 255, ..., all dimensions but the last counted through in order) at most 16 rows name the same one
- w_qkv: float32 [1024, 3072], P(('dp', 'ctx')), may hold values from -0.1875 to 0.1875
- w_out: float32 [1024, 1024], P(('dp', 'ctx')), may hold values from -3 to 3
- w_up: float32 [1024, 4096], P(('dp', 'ctx')), may hold values from -0.1875 to 0.1875
- w_down: float32 [4096, 1024], P(('dp', 'ctx')), may hold values from -0.09375 to 0.09375
- router: float32 [1024, 18], P(('dp', 'ctx')), may hold values from -0.09375 to 0.09375
- norm_gains: float32 [2, 1024], P(None, ('dp', 'ctx')), may hold values from 0.5 to 1.5
- norm_biases: float32 [2, 1024], P(None, ('dp', 'ctx')), may hold values from -1 to 1
- expert_up: bfloat16 [16, 1024, 4096], P('ctx', None, 'dp'), may hold values from -0.1875 to 0.1875
- expert_down: bfloat16 [16, 4096, 1024], P('ctx', 'dp'), may hold values from -8 to 8
Outputs:
- layer_out: bfloat16 [2, 2048, 1024], P('dp', 'ctx')
- grad_tokens: bfloat16 [2, 2048, 1024], P('dp', 'ctx')
- grad_w_qkv: float32 [1024, 3072], P(('dp', 'ctx'))
- grad_w_out: float32 [1024, 1024], P(('dp', 'ctx'))
- grad_w_up: float32 [1024, 4096], P(('dp', 'ctx'))
- grad_w_down: float32 [4096, 1024], P(('dp', 'ctx'))
- grad_router: float32 [1024, 18], P(('dp', 'ctx'))
- grad_norm_gains: float32 [2, 1024], P(None, ('dp', 'ctx'))
- grad_norm_biases: float32 [2, 1024], P(None, ('dp', 'ctx'))
- grad_expert_up: float32 [16, 1024, 4096], P('ctx', None, 'dp')
- grad_expert_down: float32 [16, 4096, 1024], P('ctx', 'dp')
Inputs may be any that keep to these rules, and one draw needn't show every extreme that they name: `block_order`: each value appears once; entry i is the initial block place, in blocks of 64 tokens, of rows i * 64 to (i + 1) * 64 - 1 of every packed sequence. `doc_lengths`: A packed sequence's document lengths sum to 2048; the longest is exactly 1024. `routes`: among the 128 rows of a packed sequence that one index of ctx holds, no expert is named more than 16 times, a bound that some block reaches.
All inputs are finite; a program needn't handle non-finite values.
Results may differ from a plain program's by a relative error of at most 0.014.
Values may be sent and summed in bfloat16 or wider, within the bound.
A program may use at most 320 MiB of HBM per device.

v0:
```python
import functools
import math

import jax
import jax.numpy as jnp
from jax import lax
from jax.experimental import pallas as pl
from jax.experimental.pallas import tpu as pltpu
from jax.sharding import PartitionSpec as P

HEADS = 16
HEAD_DIM = 64

EPS = 1e-05
NEG = -1e30
SCALE = 0.125
TILE = 256
BF = jnp.bfloat16
F32 = jnp.float32
MESH = pl.DeviceIdType.MESH


def layer_norm(values, gain, shift):
    center = values - jnp.mean(values, axis=-1, keepdims=True)
    spread = jnp.mean(center * center, axis=-1, keepdims=True)
    return center * lax.rsqrt(spread + EPS) * gain + shift


def gelu_tanh(values):
    return jax.nn.gelu(values, approximate=True)


def router_heads(router_logits, route_hot, experts):
    chances = jax.nn.softmax(router_logits[:, :experts], axis=-1)
    gate = jnp.sum(chances * route_hot, axis=-1)
    mixing = jax.nn.softmax(router_logits[:, experts:], axis=-1)
    return (gate, mixing[:, 0], mixing[:, 1])


def dot_f32(left, right):
    return jnp.dot(left, right, preferred_element_type=F32)


def contract_rows(left, right):
    return lax.dot_general(left, right, (((0,), (0,)), ((), ())), preferred_element_type=F32)


def contract_cols(left, right):
    return lax.dot_general(left, right, (((1,), (1,)), ((), ())), preferred_element_type=F32)


def span(i, size):
    return pl.ds(pl.multiple_of(i * size, size), size)


class Move:
    def __init__(self, step, src, dst, after=None):
        self.step, self.src, self.dst, self.after = step, src, dst, after


def exchange(name, cid, sizes, ins, outs, build, micros=20):
    two, groups, team = sizes

    def kernel(*refs):
        in_refs, out_refs = refs[: len(ins)], refs[len(ins) : len(ins) + len(outs)]
        send_sem, recv_sem, local_sem = refs[len(ins) + len(outs) :]
        c = lax.axis_index("dp")
        i = lax.axis_index("ctx")
        g, t = lax.div(i, team), lax.rem(i, team)

        def device(step):
            dc, dg, dt = step
            return (
                lax.rem(c + dc, two),
                lax.rem(g + dg, groups) * team + lax.rem(t + dt, team),
            )

        locals_, moves = build((c, g, t), in_refs, out_refs)
        steps = sorted({m.step for m in moves})
        greet = sorted(
            set(steps) | {((-a) % two, (-b) % groups, (-d) % team) for a, b, d in steps}
        )
        barrier = pltpu.get_barrier_semaphore()
        for step in greet:
            pl.semaphore_signal(barrier, inc=1, device_id=device(step), device_id_type=MESH)
        pl.semaphore_wait(barrier, len(greet))

        copies = {}
        arrived = set()
        for k, (src, dst) in enumerate(locals_):
            copies[("local", k)] = pltpu.make_async_copy(src, dst, local_sem.at[k])
        for k, m in enumerate(moves):
            copies[k] = pltpu.make_async_remote_copy(
                src_ref=m.src,
                dst_ref=m.dst,
                send_sem=send_sem.at[k],
                recv_sem=recv_sem.at[k],
                device_id=device(m.step),
                device_id_type=MESH,
            )
        for k, m in enumerate(moves):
            if m.after is None:
                copies[k].start()
        for k in range(len(locals_)):
            copies[("local", k)].start()
        for k, m in enumerate(moves):
            if m.after is not None:
                if m.after not in arrived:
                    arrived.add(m.after)
                    if isinstance(m.after, tuple):
                        copies[m.after].wait()
                    else:
                        copies[m.after].wait_recv()
                copies[k].start()
        for k in range(len(locals_)):
            if ("local", k) not in arrived:
                copies[("local", k)].wait()
        for k in range(len(moves)):
            if k not in arrived:
                copies[k].wait_recv()
        for k in range(len(moves)):
            copies[k].wait_send()

    count = []

    def trace_counts():
        class Probe:
            def __getattr__(self, name):
                return self

            def __getitem__(self, index):
                return self

        locals_, moves = build((0, 0, 0), [Probe() for _ in ins], [Probe() for _ in outs])
        count.extend((len(locals_), len(moves)))

    trace_counts()
    return pl.pallas_call(
        kernel,
        name=name,
        out_shape=tuple(jax.ShapeDtypeStruct(s, d) for s, d in outs),
        in_specs=[pl.BlockSpec(memory_space=pl.ANY)] * len(ins),
        out_specs=tuple(pl.BlockSpec(memory_space=pl.ANY) for _ in outs),
        scratch_shapes=[
            pltpu.SemaphoreType.DMA((max(1, count[1]),)),
            pltpu.SemaphoreType.DMA((max(1, count[1]),)),
            pltpu.SemaphoreType.DMA((max(1, count[0]),)),
        ],
        compiler_params=pltpu.CompilerParams(collective_id=cid, has_side_effects=True),
        cost_estimate=pl.CostEstimate(
            flops=0, bytes_accessed=int(micros * 3.0e6), transcendentals=0
        ),
    )(*ins)


def mask_of(kt, key_place, query_place, query_low):
    return (key_place <= query_place) & (key_place >= query_low)


def key_places(sorted_rows, kt, place_ref):
    if sorted_rows:
        return lax.broadcasted_iota(jnp.int32, (TILE, TILE), 0) + kt * TILE
    return place_ref[pl.ds(pl.multiple_of(kt * TILE, TILE), TILE), :]


def attend_kernel(
    sorted_rows, bounds, meta_ref, place_ref, q_ref, rows_ref, kvt_ref, out_ref, lse_ref
):
    step = pl.program_id(0)
    queries = q_ref[...]
    place, low = meta_ref[0:1, :], meta_ref[1:2, :]

    def body(kt, carry):
        peak, total, acc = carry
        at = pl.ds(pl.multiple_of(kt * TILE, TILE), TILE)
        scores = dot_f32(rows_ref[at, :], queries)
        allowed = mask_of(kt, key_places(sorted_rows, kt, place_ref), place, low)
        scores = jnp.where(allowed, scores, NEG)
        new_peak = jnp.maximum(peak, jnp.max(scores, axis=0, keepdims=True))
        weights = jnp.exp(scores - new_peak)
        fade = jnp.exp(peak - new_peak)
        total = total * fade + jnp.sum(weights, axis=0, keepdims=True)
        acc = acc * fade + dot_f32(kvt_ref[HEAD_DIM:, at], weights.astype(BF))
        return new_peak, total, acc

    start = (
        jnp.full((1, TILE), NEG, F32),
        jnp.zeros((1, TILE), F32),
        jnp.zeros((HEAD_DIM, TILE), F32),
    )
    peak, total, acc = lax.fori_loop(bounds[step, 0], bounds[step, 1], body, start)
    out_ref[...] = acc / total
    lse_ref[...] = peak + jnp.log(total)


def attend_back_kernel(
    sorted_rows,
    tiles,
    bounds,
    meta_ref,
    place_ref,
    q_ref,
    do_ref,
    out_ref,
    lse_ref,
    rows_ref,
    kvt_ref,
    dq_ref,
    dkv_ref,
    acc_ref,
):
    step = pl.program_id(0)

    @pl.when(step == 0)
    def _():
        acc_ref[...] = jnp.zeros_like(acc_ref)

    queries, flows = q_ref[...], do_ref[...]
    place, low = meta_ref[0:1, :], meta_ref[1:2, :]
    log_total = lse_ref[...]
    delta = jnp.sum(flows[HEAD_DIM:, :].astype(F32) * out_ref[...], axis=0, keepdims=True)

    def body(kt, dq):
        at = pl.ds(pl.multiple_of(kt * TILE, TILE), TILE)
        rows = rows_ref[at, :]
        scores = dot_f32(rows, queries)
        allowed = mask_of(kt, key_places(sorted_rows, kt, place_ref), place, low)
        chances = jnp.exp(jnp.where(allowed, scores - log_total, NEG))
        flow = dot_f32(rows, flows)
        score_grad = (chances * (flow - delta)).astype(BF)
        dq = dq + dot_f32(kvt_ref[:HEAD_DIM, at], score_grad)
        acc_ref[:HEAD_DIM, at] += contract_cols(queries[:HEAD_DIM, :], score_grad)
        acc_ref[HEAD_DIM:, at] += contract_cols(flows[HEAD_DIM:, :], chances.astype(BF))
        return dq

    dq = lax.fori_loop(
        bounds[step, 0], bounds[step, 1], body, jnp.zeros((HEAD_DIM, TILE), F32)
    )
    dq_ref[...] = (dq * SCALE).astype(BF)

    @pl.when(step == tiles - 1)
    def _():
        dkv_ref[...] = acc_ref[...].astype(BF)


def attention_specs(length, query_length):
    def whole(shape):
        return pl.BlockSpec(shape, lambda i: (0, 0))

    def tile(rows):
        return pl.BlockSpec((rows, TILE), lambda i: (0, i))

    return whole, tile


def attend(sorted_rows, bounds, meta, place_col, q_pad, kv_rows, kv_t):
    length, query_length = kv_rows.shape[0], q_pad.shape[1]
    whole, tile = attention_specs(length, query_length)
    return pl.pallas_call(
        functools.partial(attend_kernel, sorted_rows),
        name="attend",
        grid=(query_length // TILE,),
        in_specs=[
            pl.BlockSpec(memory_space=pltpu.SMEM),
            tile(8),
            whole(place_col.shape),
            tile(2 * HEAD_DIM),
            whole((length, 2 * HEAD_DIM)),
            whole((2 * HEAD_DIM, length)),
        ],
        out_specs=(tile(HEAD_DIM), tile(1)),
        out_shape=(
            jax.ShapeDtypeStruct((HEAD_DIM, query_length), F32),
            jax.ShapeDtypeStruct((1, query_length), F32),
        ),
        compiler_params=pltpu.CompilerParams(vmem_limit_bytes=40 * 2**20),
    )(bounds, meta, place_col, q_pad, kv_rows, kv_t)


def attend_back(sorted_rows, bounds, meta, place_col, q_pad, do_pad, out, lse, kv_rows, kv_t):
    length, query_length = kv_rows.shape[0], q_pad.shape[1]
    whole, tile = attention_specs(length, query_length)
    return pl.pallas_call(
        functools.partial(attend_back_kernel, sorted_rows, query_length // TILE),
        name="attend_back",
        grid=(query_length // TILE,),
        in_specs=[
            pl.BlockSpec(memory_space=pltpu.SMEM),
            tile(8),
            whole(place_col.shape),
            tile(2 * HEAD_DIM),
            tile(2 * HEAD_DIM),
            tile(HEAD_DIM),
            tile(1),
            whole((length, 2 * HEAD_DIM)),
            whole((2 * HEAD_DIM, length)),
        ],
        out_specs=(tile(HEAD_DIM), whole((2 * HEAD_DIM, length))),
        out_shape=(
            jax.ShapeDtypeStruct((HEAD_DIM, query_length), BF),
            jax.ShapeDtypeStruct((2 * HEAD_DIM, length), BF),
        ),
        scratch_shapes=[pltpu.VMEM((2 * HEAD_DIM, length), F32)],
        compiler_params=pltpu.CompilerParams(vmem_limit_bytes=40 * 2**20),
    )(bounds, meta, place_col, q_pad, do_pad, out, lse, kv_rows, kv_t)


BLOCK = 64


def pick_pair(load, table, d):
    first, second = table[2 * d], table[2 * d + 1]
    left = load(lax.div(first, 2))
    right = load(lax.div(second, 2))
    lane = lax.broadcasted_iota(jnp.int32, left.shape, 1)
    left = jnp.where(lax.rem(first, 2) == 0, left, pltpu.roll(left, BLOCK, 1))
    right = jnp.where(lax.rem(second, 2) == 1, right, pltpu.roll(right, BLOCK, 1))
    return jnp.where(lane < BLOCK, left, right)


def column_block(ref, k, per):
    return ref[lax.div(k, per), :, span(lax.rem(k, per), 128)].astype(F32)


def sorted_attend_kernel(
    bounds, inverse, order, meta_ref, parts_ref,
    low_ref, out_ref, lse_ref, q_ref, kvt_ref, rows_ref,
):
    step = pl.program_id(0)
    length = q_ref.shape[1]
    per = parts_ref.shape[2] // 128

    @pl.when(step == 0)
    def _():
        def place(d, carry):
            tile = pick_pair(lambda k: column_block(parts_ref, k, per), inverse, d)
            at = span(d, 128)
            q_ref[:HEAD_DIM, at] = (tile[:HEAD_DIM] * SCALE).astype(BF)
            q_ref[HEAD_DIM:, at] = jnp.zeros((HEAD_DIM, 128), BF)
            kvt_ref[:, at] = tile[HEAD_DIM:].astype(BF)
            rows_ref[at, :] = tile[HEAD_DIM:].T.astype(BF)
            return carry

        lax.fori_loop(0, length // 128, place, 0)

    here = span(step, TILE)
    queries = q_ref[:, here]
    place, low = meta_ref[0:1, :], meta_ref[1:2, :]

    def body(kt, carry):
        peak, total, acc = carry
        at = span(kt, TILE)
        scores = dot_f32(rows_ref[at, :], queries)
        allowed = mask_of(kt, key_places(True, kt, None), place, low)
        scores = jnp.where(allowed, scores, NEG)
        new_peak = jnp.maximum(peak, jnp.max(scores, axis=0, keepdims=True))
        weights = jnp.exp(scores - new_peak)
        fade = jnp.exp(peak - new_peak)
        total = total * fade + jnp.sum(weights, axis=0, keepdims=True)
        acc = acc * fade + dot_f32(kvt_ref[HEAD_DIM:, at], weights.astype(BF))
        return new_peak, total, acc

    start = (
        jnp.full((1, TILE), NEG, F32),
        jnp.zeros((1, TILE), F32),
        jnp.zeros((HEAD_DIM, TILE), F32),
    )
    peak, total, acc = lax.fori_loop(bounds[step, 0], bounds[step, 1], body, start)
    out_ref[:, here] = acc / total
    lse_ref[:, here] = peak + jnp.log(total)

    @pl.when(step == length // TILE - 1)
    def _():
        def home(d, carry):
            tile = pick_pair(lambda k: out_ref[:, span(k, 128)], order, d)
            low_ref[lax.div(d, per), :, span(lax.rem(d, per), 128)] = tile.astype(BF)
            return carry

        lax.fori_loop(0, length // 128, home, 0)


def sorted_back_kernel(
    bounds, inverse, order, meta_ref, flow_ref, out_ref, lse_ref, q_ref, kvt_ref, rows_ref,
    grad_ref, do_ref, dq_ref, acc_ref,
):
    step = pl.program_id(0)
    length = q_ref.shape[1]
    per = grad_ref.shape[3] // 128

    @pl.when(step == 0)
    def _():
        acc_ref[...] = jnp.zeros_like(acc_ref)

        def place(d, carry):
            tile = pick_pair(lambda k: flow_ref[k].astype(F32), inverse, d)
            at = span(d, 128)
            do_ref[:HEAD_DIM, at] = jnp.zeros((HEAD_DIM, 128), BF)
            do_ref[HEAD_DIM:, at] = tile.astype(BF)
            return carry

        lax.fori_loop(0, length // 128, place, 0)

    here = span(step, TILE)
    queries, flows = q_ref[:, here], do_ref[:, here]
    place, low = meta_ref[0:1, :], meta_ref[1:2, :]
    log_total = lse_ref[:, here]
    delta = jnp.sum(flows[HEAD_DIM:, :].astype(F32) * out_ref[:, here], axis=0, keepdims=True)

    def body(kt, dq):
        at = span(kt, TILE)
        rows = rows_ref[at, :]
        scores = dot_f32(rows, queries)
        allowed = mask_of(kt, key_places(True, kt, None), place, low)
        chances = jnp.exp(jnp.where(allowed, scores - log_total, NEG))
        flow = dot_f32(rows, flows)
        score_grad = (chances * (flow - delta)).astype(BF)
        dq = dq + dot_f32(kvt_ref[:HEAD_DIM, at], score_grad)
        acc_ref[:HEAD_DIM, at] += contract_cols(queries[:HEAD_DIM, :], score_grad)
        acc_ref[HEAD_DIM:, at] += contract_cols(flows[HEAD_DIM:, :], chances.astype(BF))
        return dq

    dq = lax.fori_loop(
        bounds[step, 0], bounds[step, 1], body, jnp.zeros((HEAD_DIM, TILE), F32)
    )
    dq_ref[:, here] = dq * SCALE

    @pl.when(step == length // TILE - 1)
    def _():
        def home(d, carry):
            at = span(lax.rem(d, per), 128)
            tile = pick_pair(lambda k: dq_ref[:, span(k, 128)], order, d)
            grad_ref[lax.div(d, per), 0, :, at] = tile.astype(BF)
            tile = pick_pair(lambda k: acc_ref[:, span(k, 128)], order, d).astype(BF)
            grad_ref[lax.div(d, per), 1, :, at] = tile[:HEAD_DIM]
            grad_ref[lax.div(d, per), 2, :, at] = tile[HEAD_DIM:]
            return carry

        lax.fori_loop(0, length // 128, home, 0)


def fixed(shape):
    return pl.BlockSpec(shape, lambda i: (0,) * len(shape))


def sorted_attend(bounds, inverse, order, meta, parts):
    groups, _, columns = parts.shape
    length = groups * columns
    shapes = (
        ((groups, HEAD_DIM, columns), BF),
        ((HEAD_DIM, length), F32),
        ((1, length), F32),
        ((2 * HEAD_DIM, length), BF),
        ((2 * HEAD_DIM, length), BF),
        ((length, 2 * HEAD_DIM), BF),
    )
    return pl.pallas_call(
        sorted_attend_kernel,
        name="attend",
        grid=(length // TILE,),
        in_specs=[pl.BlockSpec(memory_space=pltpu.SMEM)] * 3
        + [pl.BlockSpec((8, TILE), lambda i: (0, i)), fixed(parts.shape)],
        out_specs=tuple(fixed(s) for s, _ in shapes),
        out_shape=tuple(jax.ShapeDtypeStruct(s, d) for s, d in shapes),
        compiler_params=pltpu.CompilerParams(vmem_limit_bytes=40 * 2**20),
    )(bounds, inverse, order, meta, parts)


def sorted_back(bounds, inverse, order, meta, flow, out, lse, q_pad, kv_t, kv_rows, groups):
    length = out.shape[1]
    grad = (groups, 3, HEAD_DIM, length // groups)
    return pl.pallas_call(
        sorted_back_kernel,
        name="attend_back",
        grid=(length // TILE,),
        in_specs=[pl.BlockSpec(memory_space=pltpu.SMEM)] * 3
        + [pl.BlockSpec((8, TILE), lambda i: (0, i))]
        + [fixed(a.shape) for a in (flow, out, lse, q_pad, kv_t, kv_rows)],
        out_specs=fixed(grad),
        out_shape=jax.ShapeDtypeStruct(grad, BF),
        scratch_shapes=[
            pltpu.VMEM((2 * HEAD_DIM, length), BF),
            pltpu.VMEM((HEAD_DIM, length), F32),
            pltpu.VMEM((2 * HEAD_DIM, length), F32),
        ],
        compiler_params=pltpu.CompilerParams(vmem_limit_bytes=40 * 2**20),
    )(bounds, inverse, order, meta, flow, out, lse, q_pad, kv_t, kv_rows)


def normalize(values):
    center = values - jnp.mean(values, axis=-1, keepdims=True)
    spread = jnp.mean(center * center, axis=-1, keepdims=True)
    scale = lax.rsqrt(spread + EPS)
    return center * scale, scale


def mid_kernel(
    experts, team, member, att, wo, x, vec, rw, route, cot,
    second, dgrad, send_s, send_g, sel, mixes, middle_own, prob_own, hot_own, second_own, att_own,
    egrad,
):
    rows = middle_own.shape[0]
    slots = send_s.shape[1]
    groups = send_s.shape[0]
    capacity = slots // team
    lane = lax.broadcasted_iota(jnp.int32, (rows, 128), 1)
    row = lax.broadcasted_iota(jnp.int32, (rows, rows), 0)
    col = lax.broadcasted_iota(jnp.int32, (rows, rows), 1)
    me = member[0]

    def block(b, carry):
        at = span(b, rows)
        part = att[:, at]
        middle = x[at, :].astype(F32) + contract_rows(part, wo[...])
        hat, _ = normalize(middle)
        low = (hat * vec[1:2, :] + vec[3:4, :]).astype(BF)
        second[at, :] = low
        logits = dot_f32(low, rw[...])
        is_expert = lane < experts
        is_mix = (lane >= experts) & (lane < experts + 2)
        pe = jnp.where(is_expert, logits, NEG)
        pe = jnp.exp(pe - jnp.max(pe, axis=1, keepdims=True))
        pe = pe / jnp.sum(pe, axis=1, keepdims=True)
        pm = jnp.where(is_mix, logits, NEG)
        pm = jnp.exp(pm - jnp.max(pm, axis=1, keepdims=True))
        pm = pm / jnp.sum(pm, axis=1, keepdims=True)
        route_row = jnp.broadcast_to(route[b][0:1, :], (rows, rows))
        route_col = jnp.sum(jnp.where(row == col, route_row, 0), axis=1, keepdims=True)
        hot = lane == route_col
        gate = jnp.sum(jnp.where(hot, pe, 0.0), axis=1, keepdims=True)
        mix0 = jnp.sum(jnp.where(lane == experts, pm, 0.0), axis=1, keepdims=True)
        mix1 = jnp.sum(jnp.where(lane == experts + 1, pm, 0.0), axis=1, keepdims=True)
        scaled = mix1 * gate
        flow = cot[at, :].astype(F32)
        dgrad[at, :] = (flow * mix0).astype(BF)
        egrad[at, :] = (flow * scaled).astype(BF)
        mixes[at, :] = jnp.where(lane == 0, mix0, jnp.where(lane == 1, scaled, 0.0))
        same = (route_row == route_col) & (col < row)
        rank = jnp.sum(jnp.where(same, 1, 0), axis=1, keepdims=True)
        group = lax.div(route_col, team)
        mine = lax.rem(route_col, team) == me
        target = jnp.where(mine, group * slots + b * capacity + rank, groups * slots)
        slot = lax.broadcasted_iota(jnp.int32, (rows, groups * slots), 1)
        sel[at, :] = jnp.where(slot == target, 1.0, 0.0).astype(BF)

        @pl.when(b == me)
        def _():
            middle_own[...] = middle
            prob_own[...] = jnp.where(is_expert, pe, jnp.where(is_mix, pm, 0.0))
            hot_own[...] = jnp.where(hot, 1.0, 0.0)
            second_own[...] = low
            att_own[...] = part

        return carry

    lax.fori_loop(0, team, block, 0)
    send_s[...] = contract_rows(sel[...], second[...]).astype(BF).reshape(send_s.shape)
    send_g[...] = contract_rows(sel[...], egrad[...]).astype(BF).reshape(send_g.shape)


def between(experts, sizes, slots, member, att, wo, x, vec, rw, route, cot):
    two, groups, team = sizes
    group_rows, width = x.shape
    rows = group_rows // team
    shapes = (
        ((group_rows, width), BF),
        ((group_rows, width), BF),
        ((groups, slots, width), BF),
        ((groups, slots, width), BF),
        ((group_rows, groups * slots), BF),
        ((group_rows, 128), F32),
        ((rows, width), F32),
        ((rows, 128), F32),
        ((rows, 128), F32),
        ((rows, width), BF),
        ((width, rows), BF),
    )
    inside = pl.BlockSpec(memory_space=pltpu.VMEM)
    return pl.pallas_call(
        functools.partial(mid_kernel, experts, team),
        name="between",
        in_specs=[pl.BlockSpec(memory_space=pltpu.SMEM)] + [inside] * 7,
        out_specs=tuple(inside for _ in shapes),
        out_shape=tuple(jax.ShapeDtypeStruct(s, d) for s, d in shapes),
        scratch_shapes=[pltpu.VMEM((group_rows, width), BF)],
        compiler_params=pltpu.CompilerParams(vmem_limit_bytes=48 * 2**20),
    )(member, att, wo, x, vec, rw, route, cot)


def turn_kernel(
    experts, layer_sum, second_sum, sums, middle, prob, hot, second, att, cot, rw, wo, vec,
    layer, middle_grad, flow_t, out_term, small_t,
):
    rows = middle.shape[0]
    lane = lax.broadcasted_iota(jnp.int32, (rows, 128), 1)
    layer[...] = (middle[...] + layer_sum[...]).astype(BF)
    chances, chosen = prob[...], hot[...]
    s0, s1 = sums[:, 0:1], sums[:, 1:2]
    mix1 = jnp.sum(jnp.where(lane == experts + 1, chances, 0.0), axis=1, keepdims=True)
    gate = jnp.sum(chances * chosen, axis=1, keepdims=True)
    pull_gate = s1 * mix1
    pulls = jnp.where(lane == experts, s0, jnp.where(lane == experts + 1, s1 * gate, 0.0))
    mean_pull = jnp.sum(chances * pulls, axis=1, keepdims=True)
    logit_grad = chances * jnp.where(
        lane < experts, pull_gate * (chosen - gate), pulls - mean_pull
    )
    logit_grad = jnp.where(lane < experts + 2, logit_grad, 0.0).astype(BF)
    second_grad = second_sum[...] + contract_cols(logit_grad, rw[...])
    hat, scale = normalize(middle[...])
    pull = second_grad * vec[1:2, :]
    part = scale * (
        pull
        - jnp.mean(pull, axis=-1, keepdims=True)
        - hat * jnp.mean(pull * hat, axis=-1, keepdims=True)
    )
    grad = cot[...].astype(F32) + part
    middle_grad[...] = grad
    branch = grad.astype(BF)
    width = wo.shape[0]

    def tile(n, carry):
        at = span(n, TILE)
        flow_t[at, :] = contract_cols(wo[at, :], branch).astype(BF)
        out_term[at, :] = dot_f32(att[at, :], branch).astype(BF)
        return carry

    lax.fori_loop(0, width // TILE, tile, 0)
    used = small_t.shape[0]
    routed = contract_rows(logit_grad, second[...])[:used, :]
    which = lax.broadcasted_iota(jnp.int32, routed.shape, 0)
    gain = jnp.sum(second_grad * hat, axis=0, keepdims=True)
    bias = jnp.sum(second_grad, axis=0, keepdims=True)
    small_t[...] = jnp.where(
        which == experts + 3, gain, jnp.where(which == experts + 5, bias, routed)
    )


def turn(experts, layer_sum, second_sum, sums, middle, prob, hot, second, att, cot, rw, wo, vec):
    rows, width = middle.shape
    used = -(-(experts + 6) // 8) * 8
    shapes = (
        ((rows, width), BF),
        ((rows, width), F32),
        ((width, rows), BF),
        ((width, width), BF),
        ((used, width), F32),
    )
    inside = pl.BlockSpec(memory_space=pltpu.VMEM)
    return pl.pallas_call(
        functools.partial(turn_kernel, experts),
        name="turn",
        in_specs=[inside] * 12,
        out_specs=tuple(inside for _ in shapes),
        out_shape=tuple(jax.ShapeDtypeStruct(s, d) for s, d in shapes),
        compiler_params=pltpu.CompilerParams(vmem_limit_bytes=40 * 2**20),
    )(layer_sum, second_sum, sums, middle, prob, hot, second, att, cot, rw, wo, vec)


def row_sum_kernel(left, right, out):
    out[0] = contract_rows(left[...], right[...])


def row_sum(left, right, tile):
    many, high = left.shape
    wide = right.shape[1]
    return pl.pallas_call(
        row_sum_kernel,
        name="row_sum",
        grid=(high // tile,),
        in_specs=[pl.BlockSpec((many, tile), lambda i: (0, i)), fixed(right.shape)],
        out_specs=pl.BlockSpec((1, tile, wide), lambda i: (0, i, 0)),
        out_shape=jax.ShapeDtypeStruct((1, high, wide), F32),
        compiler_params=pltpu.CompilerParams(vmem_limit_bytes=40 * 2**20),
        cost_estimate=pl.CostEstimate(
            flops=2 * many * high * wide, bytes_accessed=4 * high * wide, transcendentals=0
        ),
    )(left, right)


def gelu_and_slope(x):
    k = math.sqrt(2.0 / math.pi)
    square = x * x
    bent = jnp.tanh(k * (x + 0.044715 * (square * x)))
    half = 0.5 * (1.0 + bent)
    slope = half + (0.5 * k) * x * (1.0 - bent * bent) * (1.0 + (3 * 0.044715) * square)
    return x * half, slope


def feed_kernel(sizes, copies_count, *refs):
    two, groups, team = sizes
    (send_s, send_g, eup_h, edown_h, second_h, dgrad_h, ff_h, sel_h, cot_h, mix_h) = refs[:10]
    (layer_o, grad_o, sums_o, active_o, hgrad_o, arr_s_o, arr_g_o, ffg_o) = refs[10:18]
    (
        arr_s, arr_g, eup, edown, second, dgrad, upw, downw, sel, cot, mix,
        slope, active, hgrad, acc, give, got_s, got_g, ret_s, ret_g, back_s, back_g,
        low, ugrad, dense, spart, lay, spa, sums, lay_r, spa_r, sums_r,
        term_give, term_got, send_sem, recv_sem, load_sem, out_sem,
    ) = refs[18:]
    c = lax.axis_index("dp")
    i = lax.axis_index("ctx")
    g, t = lax.div(i, team), lax.rem(i, team)
    width = second.shape[1]
    rows = lay.shape[1]
    hid, ehid = upw.shape[1], eup.shape[1]
    core = lax.rem(c + 1, two)

    def device(step):
        dc, dg, dt = step
        return (
            lax.rem(c + dc, two),
            lax.rem(g + dg, groups) * team + lax.rem(t + dt, team),
        )

    index = [0]

    def remote(src, dst, step):
        k = index[0]
        index[0] += 1
        assert k < copies_count
        return pltpu.make_async_remote_copy(
            src_ref=src,
            dst_ref=dst,
            send_sem=send_sem.at[k],
            recv_sem=recv_sem.at[k],
            device_id=device(step),
            device_id_type=MESH,
        )

    group_steps = [(0, k, 0) for k in range(1, groups)]
    team_steps = [(0, 0, k) for k in range(1, team)]
    swap = (1, 0, 0)
    deep = ff_h.shape[2]

    def block_of(core, k):
        return pl.ds(pl.multiple_of((core * groups + k) * deep, deep), deep)

    loads = []
    for k, (src, dst) in enumerate(
        [
            (second_h, second), (dgrad_h, dgrad), (eup_h, eup), (edown_h, edown), (sel_h, sel), (cot_h, cot), (mix_h, mix),
            (send_s.at[g], arr_s.at[c, g]), (send_g.at[g], arr_g.at[c, g]),
        ]
        + [
            (ff_h.at[k, n], weight.at[block_of(c, k), :])
            for k in range(groups)
            for n, weight in enumerate((upw, downw))
        ]
    ):
        load = pltpu.make_async_copy(src, dst, load_sem.at[k])
        load.start()
        loads.append(load)

    barrier = pltpu.get_barrier_semaphore()
    greet = group_steps + team_steps + [swap]
    for step in greet:
        pl.semaphore_signal(barrier, inc=1, device_id=device(step), device_id_type=MESH)
    pl.semaphore_wait(barrier, len(greet))

    every = []

    def launch(copy):
        copy.start()
        every.append(copy)
        return copy

    def to_groups(src, dst):
        return [
            launch(remote(src.at[lax.rem(g + s[1], groups)], dst.at[g], s)) for s in group_steps
        ]

    def source(s):
        return lax.rem(g + groups - s[1], groups)

    swap_w = [
        launch(remote(ff_h.at[k, n], weight.at[block_of(c, k), :], swap))
        for k in range(groups)
        for n, weight in enumerate((upw, downw))
    ]
    out_s = [
        launch(remote(send_s.at[lax.rem(g + s[1], groups)], arr_s.at[c, g], s))
        for s in group_steps
    ]
    swap_s = [launch(remote(send_s.at[g], arr_s.at[c, g], swap))]
    out_g = [
        launch(remote(send_g.at[lax.rem(g + s[1], groups)], arr_g.at[c, g], s))
        for s in group_steps
    ]
    swap_g = [launch(remote(send_g.at[g], arr_g.at[c, g], swap))]

    for load in loads[:2] + loads[9:]:
        load.wait()
    for copy in swap_w:
        copy.wait_recv()

    def dense_in(h, carry):
        at = span(h, TILE)
        value, bend = gelu_and_slope(dot_f32(second[...], upw[:, at]))
        low[:, at] = value.astype(BF)
        ugrad[:, at] = (bend * contract_cols(dgrad[...], downw[at, :])).astype(BF)
        return carry

    lax.fori_loop(0, hid // TILE, dense_in, 0)

    def dense_out(n, carry):
        at = span(n, TILE)
        dense[:, at] = dot_f32(low[...], downw[:, at])
        spart[:, at] = contract_cols(ugrad[...], upw[at, :])
        return carry

    lax.fori_loop(0, width // TILE, dense_out, 0)

    for load in loads[2:9]:
        load.wait()
    for copy, s in zip(out_s, group_steps):
        copy.wait_recv()
        swap_s.append(launch(remote(arr_s.at[c, source(s)], arr_s.at[c, source(s)], swap)))
    for copy in swap_s:
        copy.wait_recv()
    entries = 2 * groups * arr_s.shape[2]

    def expert_in(h, carry):
        at = span(h, TILE)
        value, bend = gelu_and_slope(dot_f32(arr_s[...].reshape(entries, width), eup[:, at]))
        active[:, at] = value.astype(BF)
        slope[:, at] = bend
        return carry

    lax.fori_loop(0, ehid // TILE, expert_in, 0)
    keeps = [
        pltpu.make_async_copy(active, active_o, out_sem.at[0]),
        pltpu.make_async_copy(arr_s, arr_s_o, out_sem.at[1]),
    ]
    for copy in keeps:
        copy.start()

    def expert_out(n, carry):
        at = span(n, TILE)
        acc[:, :, at] = dot_f32(active[...], edown[:, at]).reshape(2, entries // 2, TILE)
        return carry

    lax.fori_loop(0, width // TILE, expert_out, 0)
    give[0] = acc[core].astype(BF)
    other_s = launch(remote(give.at[0], got_s, swap))

    for copy, s in zip(out_g, group_steps):
        copy.wait_recv()
        swap_g.append(launch(remote(arr_g.at[c, source(s)], arr_g.at[c, source(s)], swap)))
    other_s.wait_recv()
    ret_s[...] = (acc[c] + got_s[...].astype(F32)).astype(BF).reshape(ret_s.shape)
    home_s = to_groups(ret_s, back_s)
    back_s[g] = ret_s[g]
    for copy in swap_g:
        copy.wait_recv()

    def expert_back(h, carry):
        at = span(h, TILE)
        pull = contract_cols(arr_g[...].reshape(entries, width), edown[at, :])
        hgrad[:, at] = (slope[:, at] * pull).astype(BF)
        return carry

    lax.fori_loop(0, ehid // TILE, expert_back, 0)
    keeps += [
        pltpu.make_async_copy(hgrad, hgrad_o, out_sem.at[2]),
        pltpu.make_async_copy(arr_g, arr_g_o, out_sem.at[3]),
    ]
    for copy in keeps[2:]:
        copy.start()

    def expert_back_out(n, carry):
        at = span(n, TILE)
        acc[:, :, at] = contract_cols(hgrad[...], eup[at, :]).reshape(2, entries // 2, TILE)
        return carry

    lax.fori_loop(0, width // TILE, expert_back_out, 0)
    give[1] = acc[core].astype(BF)
    other_g = launch(remote(give.at[1], got_g, swap))
    other_g.wait_recv()
    ret_g[...] = (acc[c] + got_g[...].astype(F32)).astype(BF).reshape(ret_g.shape)
    home_g = to_groups(ret_g, back_g)
    back_g[g] = ret_g[g]

    for copy in home_s:
        copy.wait_recv()
    slots = groups * back_s.shape[1]
    lane = lax.broadcasted_iota(jnp.int32, (rows, 128), 1)

    def join_layer(r, carry):
        at = span(r, rows)
        found = dot_f32(sel[at, :], back_s[...].reshape(slots, width))
        own = dense[at, :]
        flow = cot[at, :].astype(F32)
        mixes = mix[at, :]
        lay[r] = (mixes[:, 0:1] * own + mixes[:, 1:2] * found).astype(BF)
        plain = jnp.sum(flow * own, axis=1, keepdims=True)
        routed = jnp.sum(flow * found, axis=1, keepdims=True)
        sums[r] = jnp.where(lane == 0, plain, jnp.where(lane == 1, routed, 0.0))
        return carry

    lax.fori_loop(0, team, join_layer, 0)

    def to_team(src, dst):
        made = [launch(remote(src.at[lax.rem(t + s[2], team)], dst.at[t], s)) for s in team_steps]
        dst[t] = src[t]
        return made

    team_copies = to_team(lay, lay_r) + to_team(sums, sums_r)

    for copy in home_g:
        copy.wait_recv()

    def join_grad(r, carry):
        at = span(r, rows)
        found = dot_f32(sel[at, :], back_g[...].reshape(slots, width))
        spa[r] = (spart[at, :] + found).astype(BF)
        return carry

    lax.fori_loop(0, team, join_grad, 0)
    team_copies += to_team(spa, spa_r)

    half = hid // 2
    term_tile = 128

    def down_term(base, n):
        at = pl.ds(pl.multiple_of(base + n * term_tile, term_tile), term_tile)
        return contract_rows(low[:, at], dgrad[...])

    def up_term(base, n):
        at = pl.ds(pl.multiple_of(base + n * term_tile, term_tile), term_tile)
        return contract_rows(second[:, at], ugrad[...])

    terms = []
    for k, (term, size) in enumerate(((down_term, half), (up_term, width // 2))):

        def giving(n, carry, k=k, term=term, size=size):
            term_give[k, span(n, term_tile), :] = term(core * size, n).astype(BF)
            return carry

        lax.fori_loop(0, size // term_tile, giving, 0)
        terms.append(launch(remote(term_give.at[k], term_got.at[k], swap)))
    for k, (term, size) in enumerate(((down_term, half), (up_term, width // 2))):
        terms[k].wait_recv()

        def keeping(n, carry, k=k, term=term, size=size):
            at = span(n, term_tile)
            total = term(c * size, n) + term_got[k, at, :].astype(F32)
            ffg_o[at, k * width : (k + 1) * width] = total.astype(BF)
            return carry

        lax.fori_loop(0, size // term_tile, keeping, 0)

    for copy in team_copies:
        copy.wait_recv()
    layer_o[...] = jnp.sum(lay_r[...].astype(F32), axis=0)
    grad_o[...] = jnp.sum(spa_r[...].astype(F32), axis=0)
    sums_o[...] = jnp.sum(sums_r[...], axis=0)
    for copy in keeps:
        copy.wait()
    for copy in every:
        copy.wait_send()


def feed_forward(sizes, rows, send_s, send_g, eup, edown, second, dgrad, ff, sel, cot, mix):
    two, groups, team = sizes
    slots = send_s.shape[1]
    width = second.shape[1]
    hid, ehid = second.shape[1] * ff.shape[3] // width, eup.shape[1]
    entries = 2 * groups * slots
    count = 2 * (groups - 1) * 2 + 2 * groups + 2 + 3 * (team - 1) + 2 + 2 * groups
    arrived = (two, groups, slots, width)
    anywhere = pl.BlockSpec(memory_space=pl.ANY)
    inside = pl.BlockSpec(memory_space=pltpu.VMEM)
    team_rows = team * rows
    return pl.pallas_call(
        functools.partial(feed_kernel, sizes, count),
        name="feed_forward",
        out_shape=(
            jax.ShapeDtypeStruct((rows, width), F32),
            jax.ShapeDtypeStruct((rows, width), F32),
            jax.ShapeDtypeStruct((rows, 128), F32),
            jax.ShapeDtypeStruct((entries, ehid), BF),
            jax.ShapeDtypeStruct((entries, ehid), BF),
            jax.ShapeDtypeStruct(arrived, BF),
            jax.ShapeDtypeStruct(arrived, BF),
            jax.ShapeDtypeStruct((hid // 2, 2 * width), BF),
        ),
        in_specs=[anywhere] * 10,
        out_specs=(inside, inside, inside, anywhere, anywhere, anywhere, anywhere, inside),
        scratch_shapes=[
            pltpu.VMEM((two, groups, slots, width), BF),
            pltpu.VMEM((two, groups, slots, width), BF),
            pltpu.VMEM(eup.shape, BF),
            pltpu.VMEM(edown.shape, BF),
            pltpu.VMEM(second.shape, BF),
            pltpu.VMEM(dgrad.shape, BF),
            pltpu.VMEM((width, hid), BF),
            pltpu.VMEM((hid, width), BF),
            pltpu.VMEM(sel.shape, BF),
            pltpu.VMEM(cot.shape, BF),
            pltpu.VMEM(mix.shape, F32),
            pltpu.VMEM((entries, ehid), F32),
            pltpu.VMEM((entries, ehid), BF),
            pltpu.VMEM((entries, ehid), BF),
            pltpu.VMEM((2, entries // 2, width), F32),
            pltpu.VMEM((2, entries // 2, width), BF),
            pltpu.VMEM((entries // 2, width), BF),
            pltpu.VMEM((entries // 2, width), BF),
            pltpu.VMEM((groups, slots, width), BF),
            pltpu.VMEM((groups, slots, width), BF),
            pltpu.VMEM((groups, slots, width), BF),
            pltpu.VMEM((groups, slots, width), BF),
            pltpu.VMEM((team_rows, hid), BF),
            pltpu.VMEM((team_rows, hid), BF),
            pltpu.VMEM((team_rows, width), F32),
            pltpu.VMEM((team_rows, width), F32),
            pltpu.VMEM((team, rows, width), BF),
            pltpu.VMEM((team, rows, width), BF),
            pltpu.VMEM((team, rows, 128), F32),
            pltpu.VMEM((team, rows, width), BF),
            pltpu.VMEM((team, rows, width), BF),
            pltpu.VMEM((team, rows, 128), F32),
            pltpu.VMEM((2, hid // 2, width), BF),
            pltpu.VMEM((2, hid // 2, width), BF),
            pltpu.SemaphoreType.DMA((count,)),
            pltpu.SemaphoreType.DMA((count,)),
            pltpu.SemaphoreType.DMA((9 + 2 * groups,)),
            pltpu.SemaphoreType.DMA((4,)),
        ],
        compiler_params=pltpu.CompilerParams(
            collective_id=5, has_side_effects=True, vmem_limit_bytes=60 * 2**20
        ),
        cost_estimate=pl.CostEstimate(
            flops=0, bytes_accessed=240_000_000, transcendentals=0
        ),
    )(send_s, send_g, eup, edown, second, dgrad, ff, sel, cot, mix)


def tall(chunk):
    rows, cols = chunk.shape[-2:]
    factor = 1
    while (rows * factor) % 16:
        factor *= 2
    return chunk.reshape(chunk.shape[:-2] + (rows * factor, cols // factor))


def per_device(
    tokens,
    cotangent,
    block_order,
    doc_lengths,
    routes,
    w_qkv,
    w_out,
    w_up,
    w_down,
    router,
    norm_gains,
    norm_biases,
    expert_up,
    expert_down,
):
    rows, width = tokens.shape[1], tokens.shape[2]
    ctx_count = lax.axis_size("ctx")
    two = lax.axis_size("dp")
    team = math.gcd(4, ctx_count)
    groups = ctx_count // team
    sizes = (two, groups, team)
    team_heads = HEADS // team
    reps = groups // team_heads
    length = rows * ctx_count
    group_rows = rows * team
    experts = ctx_count * expert_up.shape[0]
    capacity = max(2, 2 * rows // experts)
    block_rows = length // block_order.shape[0]
    hidden = w_up.shape[1]
    hidden_dev = w_down.shape[0]
    wr = w_qkv.shape[0]
    qkv_cols = 3 * width // team
    up_cols = hidden // team
    core = lax.axis_index("dp")
    ctx = lax.axis_index("ctx")
    group, member = lax.div(ctx, team), lax.rem(ctx, team)
    team_steps = [(0, 0, k) for k in range(1, team)]
    group_steps = [(0, k, 0) for k in range(1, groups)]
    by_group = [[g * team + t for g in range(groups)] for t in range(team)]
    by_team = [[g * team + t for t in range(team)] for g in range(groups)]
    swap = [(d, (d + 1) % two) for d in range(two)]

    small_flat = jnp.concatenate(
        [router.reshape(-1), norm_gains.reshape(-1), norm_biases.reshape(-1)]
    )
    small_size = -(-small_flat.shape[0] // 2048) * 2048
    small = jnp.pad(small_flat, (0, small_size - small_flat.shape[0])).astype(BF)
    small = small.reshape(-1, 128)

    qkv_first = tall(
        w_qkv.astype(BF).reshape(wr, 3, team, width // team).transpose(2, 0, 1, 3).reshape(
            team, wr, qkv_cols
        )
    )
    up_first = tall(
        w_up.reshape(wr, two * groups, team, hidden_dev)
        .transpose(2, 0, 1, 3)
        .reshape(team, wr, up_cols)
        .astype(BF)
    )
    down_first = tall(w_down.astype(BF).reshape(team, wr, width))
    out_first = tall(w_out.astype(BF))
    route_row = jnp.broadcast_to(routes[0, :, 0][None, :], (8, rows))

    def first(coords, ins, outs):
        c, g, t = coords
        moves, local = [], []
        for s in team_steps:
            to = lax.rem(t + s[2], team)
            moves.append(Move(s, ins[0], outs[0].at[t]))
            moves.append(Move(s, ins[1].at[to], outs[1].at[t]))
            moves.append(Move(s, ins[3], outs[3].at[t]))
            moves.append(Move(s, ins[4], outs[4].at[t]))
            moves.append(Move(s, ins[2].at[to], outs[2].at[0, t]))
        for s in group_steps:
            moves.append(Move(s, ins[5], outs[5].at[g]))
        local.append((ins[0], outs[0].at[t]))
        local.append((ins[1].at[t], outs[1].at[t]))
        local.append((ins[2].at[t], outs[2].at[0, t]))
        local.append((ins[3], outs[3].at[t]))
        local.append((ins[4], outs[4].at[t]))
        local.append((ins[5], outs[5].at[g]))
        local.append((ins[6], outs[2].at[1]))
        return local, moves

    token_rows, qkv_part, ff_part, small_part, route_all, out_part = exchange(
        "first",
        1,
        sizes,
        (tokens[0], qkv_first, up_first, small, route_row, out_first, down_first),
        [
            ((team, rows, width), BF),
            (qkv_first.shape, BF),
            ((2,) + up_first.shape, BF),
            ((team,) + small.shape, BF),
            ((team, 8, rows), jnp.int32),
            ((groups,) + out_first.shape, BF),
        ],
        first,
    )

    def second_build(coords, ins, outs):
        c, g, t = coords
        moves, local = [], []
        for k, s in enumerate(group_steps):
            moves.append(Move(s, ins[0], outs[0].at[c, g]))
            moves.append(Move(s, ins[1], outs[1].at[c, g]))
        for s in team_steps:
            moves.append(Move(s, ins[2], outs[2].at[t]))
        local.append((ins[0], outs[0].at[c, g]))
        local.append((ins[1], outs[1].at[c, g]))
        local.append((ins[2], outs[2].at[t]))
        other = (1, 0, 0)
        for n in range(2):
            moves.append(Move(other, ins[n], outs[n].at[c, g]))
        for k, s in enumerate(group_steps):
            source = lax.rem(g + groups - s[1], groups)
            for n in range(2):
                moves.append(
                    Move(other, outs[n].at[c, source], outs[n].at[c, source], after=2 * k + n)
                )
        return local, moves

    qkv_all, small_all, cot_rows = exchange(
        "second",
        2,
        sizes,
        (qkv_part, small_part, cotangent[0]),
        [
            ((two, groups) + qkv_part.shape, BF),
            ((two, groups) + small_part.shape, BF),
            ((team, rows, width), BF),
        ],
        second_build,
    )
    qkv_weight = qkv_all.reshape(width, qkv_cols)
    small_rows = small_all.reshape(two * ctx_count, -1)
    router_cols = router.shape[1]
    router_weight = jnp.pad(
        small_rows[:, : wr * router_cols].reshape(width, router_cols),
        ((0, 0), (0, 128 - router_cols)),
    )
    vectors = small_rows[:, wr * router_cols : small_flat.shape[0]].reshape(
        two * ctx_count, 4, wr
    )
    vectors = vectors.transpose(1, 0, 2).reshape(4, width).astype(F32)
    vectors = jnp.pad(vectors, ((0, 4), (0, 0)))

    ff_half = lax.all_gather(
        ff_part.reshape(2, team * wr, width),
        "ctx",
        axis=0,
        tiled=False,
        axis_index_groups=by_group,
    )

    def core_half(term):
        halves = term.reshape((two, term.shape[0] // two) + term.shape[1:])
        keep = lax.dynamic_index_in_dim(halves, core, 0, keepdims=False)
        give = lax.dynamic_index_in_dim(halves, 1 - core, 0, keepdims=False)
        return keep + lax.ppermute(give.astype(BF), "dp", swap).astype(F32)

    def over_groups(term):
        return lax.psum_scatter(
            term, "ctx", scatter_dimension=0, tiled=True, axis_index_groups=by_group
        )

    doc_id = jnp.arange(doc_lengths.shape[1], dtype=jnp.int32)
    doc_ends = jnp.sum(
        jnp.where(doc_id[:, None] <= doc_id[None, :], doc_lengths[0][:, None], 0), axis=0
    )
    all_rows = jnp.arange(length, dtype=jnp.int32)
    marks = (all_rows // block_rows)[:, None] == jnp.arange(
        block_order.shape[0], dtype=jnp.int32
    )[None, :]
    anchor = jnp.sum(jnp.where(marks, block_order[None, :], 0), axis=1)
    all_place = anchor * block_rows + all_rows % block_rows

    def low_of(place):
        return jnp.max(
            jnp.where(doc_ends[None, :] <= place[:, None], doc_ends[None, :], 0), axis=1
        )

    sorted_rows = reps == 1 and block_rows == BLOCK
    query_length = length // reps
    tiles = query_length // TILE
    part = lax.rem(group, reps)
    if sorted_rows:
        query_place = all_rows
        lows = low_of(all_rows)
        bounds = jnp.stack(
            [lows[::TILE] // TILE, jnp.arange(1, tiles + 1, dtype=jnp.int32)], axis=1
        )
        number = jnp.arange(block_order.shape[0], dtype=jnp.int32)
        inverse = jnp.sum(
            jnp.where(block_order[None, :] == number[:, None], number[None, :], 0), axis=1
        )
    else:
        query_place = lax.dynamic_slice(all_place, (part * query_length,), (query_length,))
        lows = low_of(query_place)
        bounds = jnp.broadcast_to(
            jnp.array([[0, length // TILE]], dtype=jnp.int32), (tiles, 2)
        )
    meta = jnp.concatenate(
        [query_place[None], lows[None], jnp.zeros((6, query_length), jnp.int32)], axis=0
    )

    token_rows = token_rows.reshape(group_rows, width)
    inputs = token_rows.astype(F32)
    normed_low = layer_norm(inputs, vectors[0], vectors[2]).astype(BF)
    mixed_t = lax.dot_general(
        qkv_weight, normed_low, (((0,), (1,)), ((), ())), preferred_element_type=F32
    ).astype(BF)
    mixed_t = mixed_t.reshape(3, team_heads, HEAD_DIM, group_rows)

    def spread_heads(coords, ins, outs):
        c, g, t = coords
        moves = [
            Move(s, ins[0].at[:, lax.div(lax.rem(g + s[1], groups), reps)], outs[0].at[g])
            for s in group_steps
        ]
        local = [(ins[0].at[:, lax.div(g, reps)], outs[0].at[g])]
        other = (1, 0, 0)
        moves.append(Move(other, ins[1], outs[1].at[c, :, t]))
        local.append((ins[1], outs[1].at[c, :, t]))
        first_team = len(moves)
        for s in team_steps:
            moves.append(Move(s, ins[1], outs[1].at[c, :, t]))
        for k, s in enumerate(team_steps):
            source = lax.rem(t + team - s[2], team)
            view = outs[1].at[c, :, source]
            moves.append(Move(other, view, view, after=first_team + k))
        return local, moves

    head_parts, out_weight = exchange(
        "heads",
        3,
        sizes,
        (mixed_t, out_part),
        [
            ((groups, 3, HEAD_DIM, group_rows), BF),
            ((two, groups, team) + out_first.shape, BF),
        ],
        spread_heads,
    )
    out_weight = out_weight.reshape(width, width)
    head_parts = head_parts.reshape(groups, 3 * HEAD_DIM, group_rows)
    if sorted_rows:
        low_t, attention_t, log_total, q_pad, kv_t, kv_rows = sorted_attend(
            bounds, inverse, block_order, meta, head_parts
        )
    else:
        place_col = all_place[:, None]
        head_t = head_parts.transpose(1, 0, 2).reshape(3 * HEAD_DIM, length)
        zeros = jnp.zeros((HEAD_DIM, query_length), BF)
        kv_t = head_t[HEAD_DIM:]
        kv_rows = kv_t.T
        q_t = lax.dynamic_slice(
            head_t[:HEAD_DIM], (0, part * query_length), (HEAD_DIM, query_length)
        )
        q_pad = jnp.concatenate([q_t * jnp.asarray(SCALE, BF), zeros], axis=0)
        attention_t, log_total = attend(False, bounds, meta, place_col, q_pad, kv_rows, kv_t)
        low_t = lax.dynamic_update_slice(
            jnp.zeros((HEAD_DIM, length), BF),
            attention_t.astype(BF),
            (0, part * query_length),
        )
        low_t = low_t.reshape(HEAD_DIM, groups, group_rows).transpose(1, 0, 2)

    def gather_heads(coords, ins, outs):
        c, g, t = coords
        moves = [
            Move(s, ins[0].at[lax.rem(g + s[1], groups)], outs[0].at[t, g]) for s in group_steps
        ]
        local = [(ins[0].at[g], outs[0].at[t, g])]
        for s in team_steps:
            moves.append(Move(s, ins[0].at[g], outs[0].at[t, g]))
        for k, s in enumerate(group_steps):
            source = lax.rem(g + groups - s[1], groups)
            for e in team_steps:
                moves.append(Move(e, outs[0].at[t, source], outs[0].at[t, source], after=k))
        return local, moves

    [attended] = exchange(
        "attended",
        4,
        sizes,
        (low_t,),
        [((team, groups, HEAD_DIM, group_rows), BF)],
        gather_heads,
    )
    if reps > 1:
        attended = lax.dynamic_index_in_dim(
            attended.reshape(team, team_heads, reps, HEAD_DIM, group_rows),
            lax.div(group, groups // reps),
            2,
            keepdims=False,
        )
    attended_t = attended.reshape(width, group_rows)

    slots = team * capacity
    (
        second_low,
        dense_grad,
        send_s,
        send_g,
        select,
        mixes,
        middle_own,
        prob_own,
        hot_own,
        second_own,
        attended_own,
    ) = between(
        experts,
        sizes,
        slots,
        member[None],
        attended_t,
        out_weight,
        token_rows,
        vectors,
        router_weight,
        route_all,
        cot_rows.reshape(group_rows, width),
    )
    (
        layer_sum,
        second_sum,
        sums_own,
        expert_active,
        hidden_grad,
        arrived_in,
        arrived_grad,
        ff_terms,
    ) = feed_forward(
        sizes,
        rows,
        send_s,
        send_g,
        expert_up[0],
        expert_down[0],
        second_low,
        dense_grad,
        ff_half,
        select,
        cot_rows.reshape(group_rows, width),
        mixes,
    )
    ff_sum = over_groups(ff_terms)
    down_sum = ff_sum[:, :width].astype(F32)
    up_sum = ff_sum[:, width:].reshape(team, wr, up_cols)
    entries = two * groups * slots
    expert_down_grad = row_sum(expert_active, arrived_grad.reshape(entries, width), TILE)
    expert_up_grad = row_sum(arrived_in.reshape(entries, width), hidden_grad, 128)

    layer_out, middle_grad, flow_t, out_term, small_t = turn(
        experts,
        layer_sum,
        second_sum,
        sums_own,
        middle_own,
        prob_own,
        hot_own,
        second_own,
        attended_own,
        cotangent[0],
        router_weight,
        out_weight,
        vectors,
    )
    flow_t = flow_t.reshape(team, team_heads, HEAD_DIM, rows)
    out_halves = out_term.reshape(two, groups, team, wr, width)

    def spread_flow(coords, ins, outs):
        c, g, t = coords
        moves = []
        for dg in range(groups):
            for dt in range(team):
                if dg or dt:
                    to_g, to_t = lax.rem(g + dg, groups), lax.rem(t + dt, team)
                    moves.append(
                        Move((0, dg, dt), ins[0].at[to_t, lax.div(to_g, reps)], outs[0].at[g, t])
                    )
        moves.append(Move((1, 0, 0), ins[1].at[lax.rem(c + 1, two)], outs[1]))
        return [(ins[0].at[t, lax.div(g, reps)], outs[0].at[g, t])], moves

    flow_parts, out_got = exchange(
        "flow",
        8,
        sizes,
        (flow_t, out_halves),
        [((groups, team, HEAD_DIM, rows), BF), (out_halves.shape[1:], BF)],
        spread_flow,
    )
    if sorted_rows:
        grad_parts = sorted_back(
            bounds,
            inverse,
            block_order,
            meta,
            flow_parts.reshape(ctx_count, HEAD_DIM, rows),
            attention_t,
            log_total,
            q_pad,
            kv_t,
            kv_rows,
            groups,
        )
    else:
        flow_all = flow_parts.transpose(2, 0, 1, 3).reshape(HEAD_DIM, length)
        flow_all = lax.dynamic_slice(
            flow_all, (0, part * query_length), (HEAD_DIM, query_length)
        )
        do_pad = jnp.concatenate([zeros, flow_all], axis=0)
        query_grad, pair_grad = attend_back(
            False,
            bounds,
            meta,
            place_col,
            q_pad,
            do_pad,
            attention_t,
            log_total,
            kv_rows,
            kv_t,
        )
        query_grad = lax.dynamic_update_slice(
            jnp.zeros((HEAD_DIM, length), BF), query_grad, (0, part * query_length)
        )
        grad_parts = jnp.concatenate([query_grad, pair_grad], axis=0)
        grad_parts = grad_parts.reshape(3, HEAD_DIM, groups, group_rows).transpose(2, 0, 1, 3)
    out_keep = lax.dynamic_index_in_dim(out_halves, core, 0, keepdims=False)
    out_parts = tall(
        (out_keep.astype(F32) + out_got.astype(F32))
        .astype(BF)
        .transpose(1, 0, 2, 3)
        .reshape(team, groups * wr, width)
    )

    def mixed_build(coords, ins, outs):
        c, g, t = coords
        moves = [
            Move(s, ins[0].at[lax.rem(g + s[1], groups)], outs[0].at[:, g])
            for s in group_steps
        ]
        moves += [
            Move(s, ins[1].at[lax.rem(t + s[2], team)], outs[1].at[t]) for s in team_steps
        ]
        return [(ins[0].at[g], outs[0].at[:, g]), (ins[1].at[t], outs[1].at[t])], moves

    grad_parts, out_parts = exchange(
        "mixed",
        9,
        sizes,
        (grad_parts, out_parts),
        [((3, groups, HEAD_DIM, group_rows), BF), (out_parts.shape, BF)],
        mixed_build,
    )
    out_parts = tall(
        jnp.sum(out_parts.astype(F32), axis=0).astype(BF).reshape(groups, wr, width)
    )
    if reps > 1:
        grad_parts = jnp.sum(
            grad_parts.reshape(3, team_heads, reps, HEAD_DIM, group_rows).astype(F32), axis=2
        ).astype(BF)
    mixed_grad_t = grad_parts.reshape(qkv_cols, group_rows)
    normed_part = (
        lax.dot_general(
            mixed_grad_t, qkv_weight, (((0,), (1,)), ((), ())), preferred_element_type=F32
        )
        .astype(BF)
        .reshape(team, rows, width)
    )
    qkv_term = lax.dot_general(
        normed_low, mixed_grad_t, (((0,), (1,)), ((), ())), preferred_element_type=F32
    )
    qkv_parts = core_half(qkv_term).astype(BF).reshape(groups, team * wr, qkv_cols)

    def normed_build(coords, ins, outs):
        c, g, t = coords
        moves, local = [], [(ins[2].at[t], outs[2].at[t])]
        for n in range(2):
            for s in group_steps:
                moves.append(Move(s, ins[n].at[lax.rem(g + s[1], groups)], outs[n].at[g]))
            local.append((ins[n].at[g], outs[n].at[g]))
        for s in team_steps:
            moves.append(Move(s, ins[2].at[lax.rem(t + s[2], team)], outs[2].at[t]))
        return local, moves

    qkv_parts, out_parts, normed_own = exchange(
        "normed",
        10,
        sizes,
        (qkv_parts, out_parts, normed_part),
        [(qkv_parts.shape, BF), (out_parts.shape, BF), (normed_part.shape, BF)],
        normed_build,
    )
    qkv_sum = (
        jnp.sum(qkv_parts.astype(F32), axis=0).astype(BF).reshape(team, wr, qkv_cols)
    )
    out_sum = jnp.sum(out_parts.astype(F32), axis=0).reshape(wr, width)
    normed_grad = jnp.sum(normed_own.astype(F32), axis=0)
    input_part_grad, gain_first, bias_first = jax.vjp(
        layer_norm, tokens[0].astype(F32), vectors[0], vectors[2]
    )[1](normed_grad)
    input_grad = middle_grad + input_part_grad

    small_used = small_t.shape[0]
    small_row = jnp.arange(small_used, dtype=jnp.int32)[:, None]
    small_t = jnp.where(
        small_row == experts + 2,
        gain_first[None],
        jnp.where(small_row == experts + 4, bias_first[None], small_t),
    )
    small_cols = small_used * wr
    small_pad = -(-small_cols // 1024) * 1024
    small_parts = jnp.pad(
        small_t.reshape(small_used, two * ctx_count, wr)
        .transpose(1, 0, 2)
        .reshape(two * ctx_count, small_cols),
        ((0, 0), (0, small_pad - small_cols)),
    ).reshape(two * ctx_count, small_pad // 128, 128)

    def owners_build(coords, ins, outs):
        c, g, t = coords
        moves, local = [], []
        for n in range(2):
            for s in team_steps:
                moves.append(Move(s, ins[n].at[lax.rem(t + s[2], team)], outs[n].at[t]))
            local.append((ins[n].at[t], outs[n].at[t]))
        me = c * ctx_count + g * team + t
        for dc in range(two):
            for dg in range(groups):
                for dt in range(team):
                    if dc or dg or dt:
                        to = (
                            lax.rem(c + dc, two) * ctx_count
                            + lax.rem(g + dg, groups) * team
                            + lax.rem(t + dt, team)
                        )
                        moves.append(Move((dc, dg, dt), ins[2].at[to], outs[2].at[me]))
        local.append((ins[2].at[me], outs[2].at[me]))
        return local, moves

    up_own, qkv_own, small_own = exchange(
        "owners",
        11,
        sizes,
        (tall(up_sum), tall(qkv_sum), small_parts),
        [
            (tall(up_sum).shape, BF),
            (tall(qkv_sum).shape, BF),
            (small_parts.shape, F32),
        ],
        owners_build,
    )
    small_sum = jnp.sum(small_own, axis=0).reshape(-1)[:small_cols].reshape(small_used, wr)
    up_own = (
        up_own.reshape(team, wr, two * groups, hidden_dev)
        .transpose(1, 2, 0, 3)
        .reshape(wr, hidden)
        .astype(F32)
    )
    qkv_own = (
        qkv_own.reshape(team, wr, 3, width // team)
        .transpose(1, 2, 0, 3)
        .reshape(wr, 3 * width)
        .astype(F32)
    )
    return (
        layer_out[None],
        input_grad[None].astype(BF),
        qkv_own,
        out_sum,
        up_own,
        down_sum,
        small_sum[:router_cols].T,
        small_sum[router_cols : router_cols + 2],
        small_sum[router_cols + 2 : router_cols + 4],
        expert_up_grad,
        expert_down_grad,
    )


def solution(mesh):
    in_specs = (
        P("dp", "ctx", None),
        P("dp", "ctx", None),
        P(),
        P("dp", None),
        P("dp", "ctx", None),
        P(("dp", "ctx"), None),
        P(("dp", "ctx"), None),
        P(("dp", "ctx"), None),
        P(("dp", "ctx"), None),
        P(("dp", "ctx"), None),
        P(None, ("dp", "ctx")),
        P(None, ("dp", "ctx")),
        P("ctx", None, "dp"),
        P("ctx", "dp", None),
    )
    out_specs = (
        P("dp", "ctx", None),
        P("dp", "ctx", None),
        P(("dp", "ctx"), None),
        P(("dp", "ctx"), None),
        P(("dp", "ctx"), None),
        P(("dp", "ctx"), None),
        P(("dp", "ctx"), None),
        P(None, ("dp", "ctx")),
        P(None, ("dp", "ctx")),
        P("ctx", None, "dp"),
        P("ctx", "dp", None),
    )
    return jax.shard_map(
        per_device, mesh=mesh, in_specs=in_specs, out_specs=out_specs, check_vma=False
    )
```

profile of v0, /device:TPU:0, one launch (start us, length us, event | category | flops | bytes accessed | tf_op | source)
XLA Modules:
  0.0 408.3 jit_solution(11013362147573683180)
XLA Ops:
  16.6 28.2 %first.1 = (bf16[4,128,1024]{2,1,0:T(8,128)(2,1)}, bf16[4,32,768]{2,1,0:T(8,128)(2,1)}, bf16[2,4,32,1024]{3,2,1,0:T(8,128)(2,1)}, bf16[4,16,128]{2,1,0:T(8,128)(...) custom-call(bf16[128,1024]{1,0:T(8,128)(2,1)} %bitcast.117, bf16[4,32,768]{2,1,0:T(8,128)(2,1)} %reshape.263.refs_1_, ...), custom_call_target="tpu_custom_call" | custom-call | bytes 60000000 | tf_op jit(solution)/shard_map/first/pallas_call | solution.py:138
  45.4 30.1 %second.1 = (bf16[2,4,4,32,768]{4,3,2,1,0:T(8,128)(2,1)}, bf16[2,4,4,16,128]{4,3,2,1,0:T(8,128)(2,1)}, bf16[4,128,1024]{2,1,0:T(8,128)(2,1)}) custom-call(bf16[4,32,768]{2,1,0:T(8,128)(2,1)} %get-tuple-element.62.refs_0_, bf16[4,16,128]{2,1,0:T(8,128)(2,1)} %get-tuple-element.63.refs_1_, bf16[128,1024]{1,0:T(8,128)(2,1)} %bitcast.109), custom_call_target="tpu_custom_call" | custom-call | bytes 60000000 | tf_op jit(solution)/shard_map/second/pallas_call | solution.py:138
  79.1 1.9 convolution_convert_fusion.1
  81.0 33.0 %heads.1 = (bf16[4,3,64,512]{3,2,1,0:T(8,128)(2,1)}, bf16[2,4,4,32,1024]{4,3,2,1,0:T(8,128)(2,1)}) custom-call(bf16[3,4,64,512]{3,2,1,0:T(8,128)(2,1)} %bitcast.138, bf16[4,32,1024]{2,1,0:T(8,128)(2,1)} %get-tuple-element.67.refs_1_), custom_call_target="tpu_custom_call" | custom-call | bytes 60000000 | tf_op jit(solution)/shard_map/heads/pallas_call | solution.py:138
  115.4 13.7 %attend.1 = (bf16[4,64,512]{2,1,0:T(8,128)(2,1)S(1)}, f32[64,2048]{1,0:T(8,128)S(1)}, f32[1,2048]{1,0:T(1,128)S(1)}, bf16[128,2048]{1,0:T(8,128)(2,1)S(1)}, bf16...) custom-call(s32[8,2]{1,0:T(8,128)S(1)} %copy.66.bounds, s32[32]{0:T(128)S(1)} %select_reduce_fusion.1.inverse, ...), custom_call_target="tpu_custom_call" | custom-call | tf_op jit(solution)/shard_map/attend/pallas_call | solution.py:456
  132.9 20.1 %attended.1 = bf16[4,4,64,512]{3,2,1,0:T(8,128)(2,1)} custom-call(bf16[4,64,512]{2,1,0:T(8,128)(2,1)} %copy-done.31), custom_call_target="tpu_custom_call" | custom-call | bytes 60000000 | tf_op jit(solution)/shard_map/attended/pallas_call | solution.py:138
  154.3 7.7 %between.1 = (bf16[512,1024]{1,0:T(8,128)(2,1)S(1)}, bf16[512,1024]{1,0:T(8,128)(2,1)S(1)}, bf16[4,64,1024]{2,1,0:T(8,128)(2,1)S(1)}, bf16[4,64,1024]{2,1,0:T(8,...) custom-call(s32[1]{0:T(128)} %bitcast.member, ...), custom_call_target="tpu_custom_call" | custom-call | tf_op jit(solution)/shard_map/between/pallas_call | solution.py:578
  168.2 67.4 %feed_forward.1 = (f32[128,1024]{1,0:T(8,128)}, f32[128,1024]{1,0:T(8,128)}, f32[128,128]{1,0:T(8,128)}, bf16[512,2048]{1,0:T(8,128)(2,1)}, bf16[512,2048]{1,0:T...) custom-call(bf16[4,64,1024]{2,1,0:T(8,128)(2,1)} %copy-done.25, ...), custom_call_target="tpu_custom_call" | custom-call | bytes 240000000 | tf_op jit(solution)/shard_map/feed_forward/pallas_call | solution.py:972
  235.7 2.8 fusion.8
  238.5 2.3 copy.74
  247.5 3.3 turn.1
  254.2 26.2 %flow.1 = (bf16[4,4,64,128]{3,2,1,0:T(8,128)(2,1)}, bf16[4,4,32,1024]{3,2,1,0:T(8,128)(2,1)}) custom-call(bf16[4,4,64,128]{3,2,1,0:T(8,128)(2,1)} %bitcast.114, bf16[2,4,4,32,1024]{4,3,2,1,0:T(8,128)(2,1)} %bitcast.106), custom_call_target="tpu_custom_call" | custom-call | bytes 60000000 | tf_op jit(solution)/shard_map/flow/pallas_call | solution.py:138
  283.4 14.1 %attend_back.1.refs_0_ = bf16[4,3,64,512]{3,2,1,0:T(8,128)(2,1)S(1)} custom-call(s32[8,2]{1,0:T(8,128)S(1)} %copy.66.bounds, s32[32]{0:T(128)S(1)} %select_reduce_fusion.1.inverse, s32[32]{0:T(128)S(1)} %copy-done.42, s32[8,2048]{1,0:T(8,128)S(1)} %add_add_fusion.1.meta_ref, bf16[16,64,128]{2,1,0:T(8,128)(2,1)S(1)} %bitcast.115, f32[64,2048]{1,0:T(8,128)S(1)} %copy-done.18, ...), custom_call_target="tpu_custom_call" | custom-call | tf_op jit(solution)/shard_map/attend_back/pallas_call | solution.py:471
  298.4 21.2 %mixed.1 = (bf16[3,4,64,512]{3,2,1,0:T(8,128)(2,1)}, bf16[4,128,1024]{2,1,0:T(8,128)(2,1)}) custom-call(bf16[4,3,64,512]{3,2,1,0:T(8,128)(2,1)} %copy-done.4, bf16[4,128,1024]{2,1,0:T(8,128)(2,1)} %bitcast.119), custom_call_target="tpu_custom_call" | custom-call | bytes 60000000 | tf_op jit(solution)/shard_map/mixed/pallas_call | solution.py:138
  319.7 2.2 fusion.32
  324.5 2.2 reduce_sum.161
  326.7 6.4 %row_sum.2 = f32[1,1024,2048]{2,1,0:T(8,128)} custom-call(bf16[512,1024]{1,0:T(8,128)(2,1)S(1)} %bitcast.112, bf16[512,2048]{1,0:T(8,128)(2,1)S(1)} %copy-done.6), custom_call_target="tpu_custom_call" | custom-call | flops 2147483648 | bytes 8388608 | tf_op jit(solution)/shard_map/row_sum/pallas_call | solution.py:665
  333.2 6.4 %row_sum.3 = f32[1,2048,1024]{2,1,0:T(8,128)} custom-call(bf16[512,2048]{1,0:T(8,128)(2,1)S(1)} %copy-done.5, bf16[512,1024]{1,0:T(8,128)(2,1)S(1)} %bitcast.111), custom_call_target="tpu_custom_call" | custom-call | flops 2147483648 | bytes 8388608 | tf_op jit(solution)/shard_map/row_sum/pallas_call | solution.py:665
  339.6 2.0 convolution_convert_fusion
  341.6 2.2 fusion.7
  343.8 28.2 %normed.1 = (bf16[4,128,768]{2,1,0:T(8,128)(2,1)}, bf16[4,32,1024]{2,1,0:T(8,128)(2,1)}, bf16[4,128,1024]{2,1,0:T(8,128)(2,1)}) custom-call(bf16[4,128,768]{2,1,0:T(8,128)(2,1)} %bitcast.124, bf16[4,32,1024]{2,1,0:T(8,128)(2,1)} %bitcast.134, bf16[4,128,1024]{2,1,0:T(8,128)(2,1)} %bitcast.130), custom_call_target="tpu_custom_call" | custom-call | bytes 60000000 | tf_op jit(solution)/shard_map/normed/pallas_call | solution.py:138
  372.1 2.0 reduce_sum.167
  379.4 2.0 slice_convert_fusion
  381.4 14.0 %owners.1 = (bf16[4,32,1024]{2,1,0:T(8,128)(2,1)}, bf16[4,32,768]{2,1,0:T(8,128)(2,1)}, f32[32,8,128]{2,1,0:T(8,128)}) custom-call(bf16[4,32,1024]{2,1,0:T(8,128)(2,1)} %bitcast.128, bf16[4,32,768]{2,1,0:T(8,128)(2,1)} %bitcast.137, f32[32,8,128]{2,1,0:T(8,128)} %bitcast.140), custom_call_target="tpu_custom_call" | custom-call | bytes 60000000 | tf_op jit(solution)/shard_map/owners/pallas_call | solution.py:138
  (200 shorter events, 53.9 us)
Async XLA Ops:
  7.2 6.4 %copy-start.49 = (f32[32,4096]{1,0:T(8,128)S(1)}, f32[32,4096]{1,0:T(8,128)}, u32[]{:S(2)}) copy-start(f32[32,4096]{1,0:T(8,128)} %param.21) | copy-start | bytes 1572868
  7.2 161.1 %all-gather.2.cloned.1.call-start = ((), (), s32[]{:S(2)}) async-start(), calls=%async_computation.1 | async-start | bytes 2621440 | tf_op jit(solution)/shard_map/all_gather | solution.py:1193
  11.3 3.3 copy-start.50
  12.5 3.5 copy-start.53
  13.6 31.4 %copy-start.56 = (s32[1,8]{1,0:T(1,128)S(1)}, s32[1,8]{1,0:T(1,128)}, u32[]{:S(2)}) copy-start(s32[1,8]{1,0:T(1,128)} %param.17) | copy-start | bytes 100
  44.8 32.8 %copy-start.43 = (bf16[4,128,1024]{2,1,0:T(8,128)(2,1)S(1)}, bf16[4,128,1024]{2,1,0:T(8,128)(2,1)}, u32[]{:S(2)}) copy-start(bf16[4,128,1024]{2,1,0:T(8,128)(2,1)} %get-tuple-element.65) | copy-start | bytes 3145732
  44.8 334.6 %reduce-scatter.2.cloned.1.call-start = ((), (), s32[]{:S(2)}) async-start(), calls=%async_computation.2 | async-start | bytes 2621440 | tf_op jit(solution)/shard_map/reduce_scatter | solution.py:1208
  79.1 34.9 %copy-start.42 = (s32[32]{0:T(128)S(1)}, s32[32]{0:T(128)}, u32[]{:S(2)}) copy-start(s32[32]{0:T(128)} %order.3) | copy-start | bytes 388
  81.0 72.1 %copy-start.41 = (s32[4,8,128]{2,1,0:T(8,128)S(1)}, s32[4,8,128]{2,1,0:T(8,128)}, u32[]{:S(2)}) copy-start(s32[4,8,128]{2,1,0:T(8,128)} %get-tuple-element.71.route) | copy-start | bytes 49156
  168.2 67.4 %copy-start.27 = (bf16[1024,128]{1,0:T(8,128)(2,1)}, bf16[1024,128]{1,0:T(8,128)(2,1)S(1)}, u32[]{:S(2)}) copy-start(bf16[1024,128]{1,0:T(8,128)(2,1)S(1)} %get-tuple-element.87.att) | copy-start | bytes 786436
  235.7 6.2 %copy-start = (bf16[2,4,4,32,1024]{4,3,2,1,0:T(8,128)(2,1)S(1)}, bf16[2,4,4,32,1024]{4,3,2,1,0:T(8,128)(2,1)}, u32[]{:S(2)}) copy-start(bf16[2,4,4,32,1024]{4,3,2,1,0:T(8,128)(2,1)} %get-tuple-element.70) | copy-start | bytes 6291460
  235.7 6.2 %copy-start.7 = (bf16[1,128,1024]{2,1,0:T(8,128)(2,1)S(1)}, bf16[1,128,1024]{2,1,0:T(8,128)(2,1)}, u32[]{:S(2)}) copy-start(bf16[1,128,1024]{2,1,0:T(8,128)(2,1)} %param.15) | copy-start | bytes 786436
  254.2 26.2 %copy-start.2 = (bf16[1024,1024]{1,0:T(8,128)(2,1)S(1)}, bf16[1024,1024]{1,0:T(8,128)(2,1)}, u32[]{:S(2)}) copy-start(bf16[1024,1024]{1,0:T(8,128)(2,1)} %copy-done.1) | copy-start | bytes 6291460
  283.4 36.3 %copy-start.47 = (bf16[1024,512]{1,0:T(8,128)(2,1)S(1)}, bf16[1024,512]{1,0:T(8,128)(2,1)}, u32[]{:S(2)}) copy-start(bf16[1024,512]{1,0:T(8,128)(2,1)} %copy.74) | copy-start | bytes 3145732
  319.7 7.1 %copy-start.9 = (bf16[2,4,64,1024]{3,2,1,0:T(8,128)(2,1)S(1)}, bf16[2,4,64,1024]{3,2,1,0:T(8,128)(2,1)}, u32[]{:S(2)}) copy-start(bf16[2,4,64,1024]{3,2,1,0:T(8,128)(2,1)} %get-tuple-element.109) | copy-start | bytes 3145732
  323.5 3.2 copy-start.6
  324.5 17.1 %collective-permute-start = (bf16[512,768]{1,0:T(8,128)(2,1)}, bf16[512,768]{1,0:T(8,128)(2,1)}, u32[]{:S(2)}, u32[]{:S(2)}) collective-permute-start(bf16[512,768]{1,0:T(8,128)(2,1)} %fusion.10), channel_id=1, source_target_pairs={{0,16},{16,0},{1,17},{17,1},{2,18},{18,2},{3,19},{19,3},{4,20},{20... | collective-permute-start | bytes 2359304 | tf_op jit(solution)/shard_map/ppermute | solution.py:1205
  326.7 6.5 %copy-start.5 = (bf16[512,2048]{1,0:T(8,128)(2,1)S(1)}, bf16[512,2048]{1,0:T(8,128)(2,1)}, u32[]{:S(2)}) copy-start(bf16[512,2048]{1,0:T(8,128)(2,1)} %get-tuple-element.111.left) | copy-start | bytes 6291460
  326.7 6.5 %copy-start.8 = (bf16[2,4,64,1024]{3,2,1,0:T(8,128)(2,1)S(1)}, bf16[2,4,64,1024]{3,2,1,0:T(8,128)(2,1)}, u32[]{:S(2)}) copy-start(bf16[2,4,64,1024]{3,2,1,0:T(8,128)(2,1)} %get-tuple-element.112) | copy-start | bytes 3145732
  333.2 6.4 %copy-start.48 = (bf16[3,4,64,512]{3,2,1,0:T(8,128)(2,1)S(1)}, bf16[3,4,64,512]{3,2,1,0:T(8,128)(2,1)}, u32[]{:S(2)}) copy-start(bf16[3,4,64,512]{3,2,1,0:T(8,128)(2,1)} %get-tuple-element.99) | copy-start | bytes 2359300
  333.2 6.4 %copy-start.55 = (bf16[2,4,4,32,768]{4,3,2,1,0:T(8,128)(2,1)S(1)}, bf16[2,4,4,32,768]{4,3,2,1,0:T(8,128)(2,1)}, u32[]{:S(2)}) copy-start(bf16[2,4,4,32,768]{4,3,2,1,0:T(8,128)(2,1)} %get-tuple-element.64) | copy-start | bytes 4718596
  343.8 32.0 %copy-start.46 = (bf16[1,128,1024]{2,1,0:T(8,128)(2,1)S(1)}, bf16[1,128,1024]{2,1,0:T(8,128)(2,1)}, u32[]{:S(2)}) copy-start(bf16[1,128,1024]{2,1,0:T(8,128)(2,1)} %param.14) | copy-start | bytes 786436
  372.1 4.4 %copy-start.35 = (f32[24,1024]{1,0:T(8,128)S(1)}, f32[24,1024]{1,0:T(8,128)}, u32[]{:S(2)}) copy-start(f32[24,1024]{1,0:T(8,128)} %copy-done.34) | copy-start | bytes 294916
  395.4 4.6 %copy-start.52 = (bf16[4,32,768]{2,1,0:T(8,128)(2,1)S(1)}, bf16[4,32,768]{2,1,0:T(8,128)(2,1)}, u32[]{:S(2)}) copy-start(bf16[4,32,768]{2,1,0:T(8,128)(2,1)} %get-tuple-element.105) | copy-start | bytes 589828
  (36 other events, 46.5 us)
Sparse Core Ops, SparseCore 0:
  45.0 67.0 all-gather.1
  235.8 58.5 reduce-scatter.1
where the time goes:
time: 407 us; the launch traced here: 408 us
  Pallas kernels  320 us (79%)
  local copies, waits for them, and re-layouts  40.4 us (10%)
  other arithmetic  26.8 us (7%)
  between operations  14.7 us (4%)
  matrix products  6.16 us (2%)
    pallas_call x8, Pallas kernels, exchange(): pl.pallas_call(kernel, name=name, out_shape=tuple((jax.ShapeDtypeStruct(s...  201 us
    pallas_call x1, Pallas kernels, feed_forward(): pl.pallas_call(functools.partial(feed_kernel, sizes, count), name='feed_f...  67.4 us
    unnamed x118, local copies, waits for them, and re-layouts  27 us
    pallas_call x1, Pallas kernels, sorted_back(): pl.pallas_call(sorted_back_kernel, name='attend_back', grid=(length // TI...  14.1 us
    pallas_call x1, Pallas kernels, sorted_attend(): pl.pallas_call(sorted_attend_kernel, name='attend', grid=(length // TILE,...  13.7 us
    pallas_call x2, Pallas kernels, row_sum(): pl.pallas_call(row_sum_kernel, name='row_sum', grid=(high // tile,), in_s...  12.8 us
  transfers between devices with their start and end apart: 3, of which 0 were waited for; matrix products, arithmetic and copies ran while one was open for 8% of the time, Pallas kernels for 52%

commit v1 on v0

--- a/solution.py
+++ b/solution.py
@@ -512,7 +512,7 @@
         part = att[:, at]
         middle = x[at, :].astype(F32) + contract_rows(part, wo[...])
         hat, _ = normalize(middle)
-        low = (hat * vec[1:2, :] + vec[3:4, :]).astype(BF)
+        low = (hat * vec[5:6, :] + vec[7:8, :]).astype(BF)
         second[at, :] = low
         logits = dot_f32(low, rw[...])
         is_expert = lane < experts
@@ -606,7 +606,7 @@
     logit_grad = jnp.where(lane < experts + 2, logit_grad, 0.0).astype(BF)
     second_grad = second_sum[...] + contract_cols(logit_grad, rw[...])
     hat, scale = normalize(middle[...])
-    pull = second_grad * vec[1:2, :]
+    pull = second_grad * vec[5:6, :]
     part = scale * (
         pull
         - jnp.mean(pull, axis=-1, keepdims=True)
@@ -674,6 +674,371 @@
             flops=2 * many * high * wide, bytes_accessed=4 * high * wide, transcendentals=0
         ),
     )(left, right)
+
+
+class Net:
+    def __init__(self, sizes, send_sem, recv_sem):
+        self.two, self.groups, self.team = sizes
+        self.send_sem, self.recv_sem = send_sem, recv_sem
+        self.c = lax.axis_index("dp")
+        i = lax.axis_index("ctx")
+        self.g, self.t = lax.div(i, self.team), lax.rem(i, self.team)
+        self.group_steps = [(0, k, 0) for k in range(1, self.groups)]
+        self.team_steps = [(0, 0, k) for k in range(1, self.team)]
+        self.swap = (1, 0, 0)
+        self.started = []
+
+    def device(self, step):
+        dc, dg, dt = step
+        return (
+            lax.rem(self.c + dc, self.two),
+            lax.rem(self.g + dg, self.groups) * self.team + lax.rem(self.t + dt, self.team),
+        )
+
+    def greet(self):
+        barrier = pltpu.get_barrier_semaphore()
+        steps = self.group_steps + self.team_steps + [self.swap]
+        for step in steps:
+            pl.semaphore_signal(barrier, inc=1, device_id=self.device(step), device_id_type=MESH)
+        pl.semaphore_wait(barrier, len(steps))
+
+    def send(self, src, dst, step):
+        k = len(self.started)
+        copy = pltpu.make_async_remote_copy(
+            src_ref=src,
+            dst_ref=dst,
+            send_sem=self.send_sem.at[k],
+            recv_sem=self.recv_sem.at[k],
+            device_id=self.device(step),
+            device_id_type=MESH,
+        )
+        copy.start()
+        self.started.append(copy)
+        return copy
+
+    def group_to(self, step):
+        return lax.rem(self.g + step[1], self.groups)
+
+    def group_from(self, step):
+        return lax.rem(self.g + self.groups - step[1], self.groups)
+
+    def team_to(self, step):
+        return lax.rem(self.t + step[2], self.team)
+
+    def team_from(self, step):
+        return lax.rem(self.t + self.team - step[2], self.team)
+
+    def close(self):
+        for copy in self.started:
+            copy.wait_send()
+
+
+def arrive(copies):
+    for copy in copies:
+        copy.wait_recv()
+
+
+class Local:
+    def __init__(self, sem):
+        self.sem, self.count, self.open = sem, 0, []
+
+    def copy(self, src, dst):
+        made = pltpu.make_async_copy(src, dst, self.sem.at[self.count])
+        made.start()
+        self.count += 1
+        self.open.append(made)
+        return made
+
+    def wait(self, *copies):
+        for made in copies or tuple(self.open):
+            made.wait()
+            self.open = [other for other in self.open if other is not made]
+
+
+def start_kernel(sizes, *refs):
+    tokens, cot, own, up, down, out, route = refs[:7]
+    token_o, cot_o, heads_o, normed_o, weight_o, vec_o, out_o, ff_o, route_o = refs[7:16]
+    stage, weights, tokens_v, normed, mixed, heads, out_v, send_sem, recv_sem, local_sem = refs[16:]
+    net, local = Net(sizes, send_sem, recv_sem), Local(local_sem)
+    c, g, t = net.c, net.g, net.t
+    two, groups, team = sizes
+    rows, width = tokens.shape
+    used = own.shape[2] - 128
+    own_stage = local.copy(own.at[t], stage.at[t])
+    own_tokens = local.copy(tokens, tokens_v.at[t])
+    own_out = local.copy(out, out_v.at[g])
+    local.copy(cot, cot_o.at[t])
+    local.copy(up.at[t], ff_o.at[0, t])
+    local.copy(down, ff_o.at[1])
+    local.copy(route, route_o.at[t])
+    net.greet()
+    staged = [net.send(own.at[net.team_to(s)], stage.at[t], s) for s in net.team_steps]
+    told = [net.send(tokens, tokens_v.at[t], s) for s in net.team_steps]
+    later = [net.send(route, route_o.at[t], s) for s in net.team_steps]
+    later += [net.send(up.at[net.team_to(s)], ff_o.at[0, t], s) for s in net.team_steps]
+    local.wait(own_stage)
+    arrive(staged)
+    spread = [net.send(stage, weights.at[c, g], s) for s in net.group_steps]
+    swapped = [net.send(stage, weights.at[c, g], net.swap)]
+    mine = local.copy(stage, weights.at[c, g])
+    spread_out = [net.send(out, out_v.at[g], s) for s in net.group_steps]
+    later += [net.send(cot, cot_o.at[t], s) for s in net.team_steps]
+    local.wait(own_tokens)
+    arrive(told)
+    local.copy(tokens_v, token_o)
+    local.wait(mine)
+    for copy, s in zip(spread, net.group_steps):
+        copy.wait_recv()
+        view = weights.at[c, net.group_from(s)]
+        swapped.append(net.send(view, view, net.swap))
+    arrive(swapped)
+    local.copy(weights, weight_o)
+
+    small = weights[:, :, :, :, used:].reshape(width, 128).astype(F32).T
+    vec_o[...] = small[120:, :]
+
+    def norm(b, carry):
+        hat, _ = normalize(tokens_v[b].astype(F32))
+        normed[b] = (hat * vec_o[4:5, :] + vec_o[6:7, :]).astype(BF)
+        return carry
+
+    lax.fori_loop(0, team, norm, 0)
+    local.copy(normed, normed_o)
+    group_rows = rows * team
+    per = used // 3 // 128
+    pair = 128 // HEAD_DIM
+    for n in range(used // 128):
+        columns = weights[:, :, :, :, n * 128 : (n + 1) * 128].reshape(width, 128)
+        made = dot_f32(normed[...].reshape(group_rows, width), columns).T.astype(BF)
+        at = (n % per) * pair
+        mixed[n // per, at : at + pair] = made.reshape(pair, HEAD_DIM, group_rows)
+    given = [net.send(mixed.at[:, net.group_to(s)], heads.at[g], s) for s in net.group_steps]
+    local.wait(local.copy(mixed.at[:, g], heads.at[g]))
+
+    local.wait(own_out)
+    arrive(spread_out)
+    local.copy(out_v, out_o.at[c, :, t])
+    swapped = [net.send(out_v, out_o.at[c, :, t], net.swap)]
+    outed = [net.send(out_v, out_o.at[c, :, t], s) for s in net.team_steps]
+    for copy, s in zip(outed, net.team_steps):
+        copy.wait_recv()
+        view = out_o.at[c, :, net.team_from(s)]
+        swapped.append(net.send(view, view, net.swap))
+    arrive(given)
+    local.copy(heads, heads_o)
+    arrive(swapped + later)
+    local.wait()
+    net.close()
+
+
+def start(sizes, tokens, cot, own, up, down, out, route):
+    two, groups, team = sizes
+    rows, width = tokens.shape
+    wr, cols = own.shape[1], own.shape[2]
+    used = cols - 128
+    head = (3, groups, HEAD_DIM, team * rows)
+    shapes = (
+        ((team, rows, width), BF),
+        ((team, rows, width), BF),
+        ((groups, 3, HEAD_DIM, team * rows), BF),
+        ((team, rows, width), BF),
+        ((two, groups, team, wr, cols), BF),
+        ((8, width), F32),
+        ((two, groups, team, wr, width), BF),
+        ((2,) + up.shape, BF),
+        ((team,) + route.shape, jnp.int32),
+    )
+    anywhere = pl.BlockSpec(memory_space=pl.ANY)
+    inside = pl.BlockSpec(memory_space=pltpu.VMEM)
+    count = 6 * (team - 1) + 4 * (groups - 1) + 2 + (team - 1)
+    return pl.pallas_call(
+        functools.partial(start_kernel, sizes),
+        name="start",
+        out_shape=tuple(jax.ShapeDtypeStruct(s, d) for s, d in shapes),
+        in_specs=[anywhere] * 7,
+        out_specs=tuple(inside if n == 5 else anywhere for n in range(9)),
+        scratch_shapes=[
+            pltpu.VMEM((team, wr, cols), BF),
+            pltpu.VMEM((two, groups, team, wr, cols), BF),
+            pltpu.VMEM((team, rows, width), BF),
+            pltpu.VMEM((team, rows, width), BF),
+            pltpu.VMEM(head, BF),
+            pltpu.VMEM((groups, 3, HEAD_DIM, team * rows), BF),
+            pltpu.VMEM((groups, wr, width), BF),
+            pltpu.SemaphoreType.DMA((count,)),
+            pltpu.SemaphoreType.DMA((count,)),
+            pltpu.SemaphoreType.DMA((14,)),
+        ],
+        compiler_params=pltpu.CompilerParams(
+            collective_id=12, has_side_effects=True, vmem_limit_bytes=32 * 2**20
+        ),
+        cost_estimate=pl.CostEstimate(flops=0, bytes_accessed=150_000_000, transcendentals=0),
+    )(tokens, cot, own, up, down, out, route)
+
+
+def end_kernel(sizes, experts, *refs):
+    groups = sizes[1]
+    parts, refs = refs[:groups], refs[groups:]
+    weight, normed, tokens, vec, middle_grad, small, up, out = refs[:8]
+    grad_o, qkv_o, up_o, out_o, small_o = refs[8:13]
+    (
+        mixed, turned, weights, normed_v, give, got, zsend, zrecv, npart, nrecv, qsend, qrecv,
+        out_r, small_a, small_b, small_c, send_sem, recv_sem, local_sem,
+    ) = refs[13:]
+    net, local = Net(sizes, send_sem, recv_sem), Local(local_sem)
+    c, g, t = net.c, net.g, net.t
+    team = sizes[2]
+    rows, width = tokens.shape
+    group_rows, used = turned.shape
+    for k, part in enumerate(parts):
+        local.copy(part, mixed.at[:, net.group_from((0, k, 0))])
+    local.copy(normed, normed_v)
+    local.copy(weight, weights)
+    local.copy(up.at[t], up_o.at[t])
+    local.copy(out.at[g], out_r.at[g])
+    net.greet()
+    later = [net.send(up.at[net.team_to(s)], up_o.at[t], s) for s in net.team_steps]
+    local.wait()
+    per = used // 3 // 128
+    pair = 128 // HEAD_DIM
+    for n in range(used // 128):
+        at = (n % per) * pair
+        block = mixed[n // per, at : at + pair].reshape(128, group_rows)
+        turned[:, n * 128 : (n + 1) * 128] = block.astype(F32).T.astype(BF)
+
+    half = width // 2
+    tile = 128
+
+    def term(core, n):
+        at = pl.ds(pl.multiple_of(core * half + n * tile, tile), tile)
+        left = normed_v[:, :, at].reshape(group_rows, tile)
+        return contract_rows(left, turned[...])
+
+    def giving(n, carry):
+        give[span(n, tile), :] = term(lax.rem(c + 1, 2), n).astype(BF)
+        return carry
+
+    lax.fori_loop(0, half // tile, giving, 0)
+    crossed = net.send(give, got, net.swap)
+
+    def part_of(r, carry):
+        columns = weights[:, :, :, :, :used].reshape(width, used)
+        npart[r] = contract_cols(turned[span(r, rows), :], columns).astype(BF)
+        return carry
+
+    lax.fori_loop(0, team, part_of, 0)
+    owned = [net.send(npart.at[net.team_to(s)], nrecv.at[t], s) for s in net.team_steps]
+    nrecv[t] = npart[t]
+    crossed.wait_recv()
+
+    def keeping(n, carry):
+        at = span(n, tile)
+        zsend[at, :] = (term(c, n) + got[at, :].astype(F32)).astype(BF)
+        return carry
+
+    lax.fori_loop(0, half // tile, keeping, 0)
+    deep = half // groups
+    summed = [
+        net.send(zsend.at[span(net.group_to(s), deep), :], zrecv.at[g], s)
+        for s in net.group_steps
+    ]
+    outed = [net.send(out.at[net.group_to(s)], out_r.at[g], s) for s in net.group_steps]
+    zrecv[g] = zsend[span(g, deep), :]
+
+    arrive(owned)
+    flow = jnp.sum(nrecv[...].astype(F32), axis=0)
+    hat, scale = normalize(tokens[...].astype(F32))
+    pull = flow * vec[4:5, :]
+    pulled = scale * (
+        pull
+        - jnp.mean(pull, axis=-1, keepdims=True)
+        - hat * jnp.mean(pull * hat, axis=-1, keepdims=True)
+    )
+    grad_o[...] = (middle_grad[...] + pulled).astype(BF)
+
+    gain = jnp.sum(flow * hat, axis=0, keepdims=True)
+    bias = jnp.sum(flow, axis=0, keepdims=True)
+    which = lax.broadcasted_iota(jnp.int32, small.shape, 0)
+    mine = jnp.where(
+        which == experts + 2, gain, jnp.where(which == experts + 4, bias, small[...])
+    )
+    small_a[c] = mine
+    crossing = net.send(small_a.at[c], small_a.at[c], net.swap)
+    crossing.wait_recv()
+    small_c[...] = small_a[0] + small_a[1]
+
+    def columns_of(k):
+        return span(c * groups + k, 128)
+
+    moved = [
+        net.send(small_c.at[:, columns_of(net.group_to(s))], small_b.at[g], s)
+        for s in net.group_steps
+    ]
+    small_b[g] = small_c[:, columns_of(g)]
+    arrive(moved)
+    small_o[t] = jnp.sum(small_b[...], axis=0)
+    later += [net.send(small_o.at[t], small_o.at[t], s) for s in net.team_steps]
+
+    arrive(summed)
+    qsend[...] = jnp.sum(zrecv[...].astype(F32), axis=0).astype(BF).reshape(qsend.shape)
+    later += [net.send(qsend.at[net.team_to(s)], qrecv.at[t], s) for s in net.team_steps]
+    qrecv[t] = qsend[t]
+    arrive(outed)
+    out_o[...] = jnp.sum(out_r[...].astype(F32), axis=0)
+    arrive(later)
+    qkv_o[...] = qrecv[...]
+    net.close()
+
+
+def end(sizes, experts, parts, weight, normed, tokens, vec, middle_grad, small, up, out):
+    two, groups, team = sizes
+    rows, width = tokens.shape
+    wr = out.shape[1]
+    used = 3 * groups * HEAD_DIM
+    group_rows = parts[0].shape[2]
+    half = width // 2
+    shapes = (
+        ((rows, width), BF),
+        ((team, wr, used), BF),
+        ((team, wr, width), BF),
+        ((wr, width), F32),
+        ((team, small.shape[0], 128), F32),
+    )
+    anywhere = pl.BlockSpec(memory_space=pl.ANY)
+    inside = pl.BlockSpec(memory_space=pltpu.VMEM)
+    count = 5 * (team - 1) + 3 * (groups - 1) + 2
+    return pl.pallas_call(
+        functools.partial(end_kernel, sizes, experts),
+        name="end",
+        out_shape=tuple(jax.ShapeDtypeStruct(s, d) for s, d in shapes),
+        in_specs=[anywhere] * (groups + 2) + [inside] * 4 + [anywhere] * 2,
+        out_specs=tuple(inside for _ in shapes),
+        scratch_shapes=[
+            pltpu.VMEM((3, groups, HEAD_DIM, group_rows), BF),
+            pltpu.VMEM((group_rows, used), BF),
+            pltpu.VMEM(weight.shape, BF),
+            pltpu.VMEM(normed.shape, BF),
+            pltpu.VMEM((half, used), BF),
+            pltpu.VMEM((half, used), BF),
+            pltpu.VMEM((half, used), BF),
+            pltpu.VMEM((groups, half // groups, used), BF),
+            pltpu.VMEM((team, rows, width), BF),
+            pltpu.VMEM((team, rows, width), BF),
+            pltpu.VMEM((team, wr, used), BF),
+            pltpu.VMEM((team, wr, used), BF),
+            pltpu.VMEM((groups, wr, width), BF),
+            pltpu.VMEM((2,) + small.shape, F32),
+            pltpu.VMEM((groups, small.shape[0], 128), F32),
+            pltpu.VMEM(small.shape, F32),
+            pltpu.SemaphoreType.DMA((count,)),
+            pltpu.SemaphoreType.DMA((count,)),
+            pltpu.SemaphoreType.DMA((groups + 4,)),
+        ],
+        compiler_params=pltpu.CompilerParams(
+            collective_id=13, has_side_effects=True, vmem_limit_bytes=32 * 2**20
+        ),
+        cost_estimate=pl.CostEstimate(flops=0, bytes_accessed=120_000_000, transcendentals=0),
+    )(*parts, weight, normed, tokens, vec, middle_grad, small, up, out)
 
 
 def gelu_and_slope(x):
@@ -1041,7 +1406,7 @@
     return chunk.reshape(chunk.shape[:-2] + (rows * factor, cols // factor))
 
 
-def per_device(
+def per_device_general(
     tokens,
     cotangent,
     block_order,
@@ -1188,7 +1553,7 @@
         two * ctx_count, 4, wr
     )
     vectors = vectors.transpose(1, 0, 2).reshape(4, width).astype(F32)
-    vectors = jnp.pad(vectors, ((0, 4), (0, 0)))
+    vectors = jnp.pad(vectors, ((4, 0), (0, 0)))
 
     ff_half = lax.all_gather(
         ff_part.reshape(2, team * wr, width),
@@ -1251,7 +1616,7 @@
 
     token_rows = token_rows.reshape(group_rows, width)
     inputs = token_rows.astype(F32)
-    normed_low = layer_norm(inputs, vectors[0], vectors[2]).astype(BF)
+    normed_low = layer_norm(inputs, vectors[4], vectors[6]).astype(BF)
     mixed_t = lax.dot_general(
         qkv_weight, normed_low, (((0,), (1,)), ((), ())), preferred_element_type=F32
     ).astype(BF)
@@ -1546,7 +1911,7 @@
     out_sum = jnp.sum(out_parts.astype(F32), axis=0).reshape(wr, width)
     normed_grad = jnp.sum(normed_own.astype(F32), axis=0)
     input_part_grad, gain_first, bias_first = jax.vjp(
-        layer_norm, tokens[0].astype(F32), vectors[0], vectors[2]
+        layer_norm, tokens[0].astype(F32), vectors[4], vectors[6]
     )[1](normed_grad)
     input_grad = middle_grad + input_part_grad
 
@@ -1627,6 +1992,317 @@
     )
 
 
+def where_rows(block_order, doc_lengths, rows, block_rows):
+    doc_id = jnp.arange(doc_lengths.shape[1], dtype=jnp.int32)
+    doc_ends = jnp.sum(
+        jnp.where(doc_id[:, None] <= doc_id[None, :], doc_lengths[0][:, None], 0), axis=0
+    )
+    lows = jnp.max(jnp.where(doc_ends[None, :] <= rows[:, None], doc_ends[None, :], 0), axis=1)
+    tiles = rows.shape[0] // TILE
+    bounds = jnp.stack([lows[::TILE] // TILE, jnp.arange(1, tiles + 1, dtype=jnp.int32)], axis=1)
+    number = jnp.arange(block_order.shape[0], dtype=jnp.int32)
+    inverse = jnp.sum(
+        jnp.where(block_order[None, :] == number[:, None], number[None, :], 0), axis=1
+    )
+    meta = jnp.concatenate(
+        [rows[None], lows[None], jnp.zeros((6, rows.shape[0]), jnp.int32)], axis=0
+    )
+    return bounds, inverse, meta
+
+
+def per_device(
+    tokens,
+    cotangent,
+    block_order,
+    doc_lengths,
+    routes,
+    w_qkv,
+    w_out,
+    w_up,
+    w_down,
+    router,
+    norm_gains,
+    norm_biases,
+    expert_up,
+    expert_down,
+):
+    rows, width = tokens.shape[1], tokens.shape[2]
+    ctx_count = lax.axis_size("ctx")
+    two = lax.axis_size("dp")
+    team = math.gcd(4, ctx_count)
+    groups = ctx_count // team
+    sizes = (two, groups, team)
+    length = rows * ctx_count
+    wr = w_qkv.shape[0]
+    experts = ctx_count * expert_up.shape[0]
+    if groups * team != HEADS or length // block_order.shape[0] != BLOCK or team * wr != 128:
+        return per_device_general(
+            tokens, cotangent, block_order, doc_lengths, routes, w_qkv, w_out, w_up, w_down,
+            router, norm_gains, norm_biases, expert_up, expert_down,
+        )
+    group_rows = rows * team
+    capacity = max(2, 2 * rows // experts)
+    slots = team * capacity
+    hidden = w_up.shape[1]
+    hidden_dev = w_down.shape[0]
+    qkv_cols = 3 * width // team
+    up_cols = hidden // team
+    ctx = lax.axis_index("ctx")
+    core = lax.axis_index("dp")
+    group, member = lax.div(ctx, team), lax.rem(ctx, team)
+    by_group = [[g * team + t for g in range(groups)] for t in range(team)]
+    team_steps = [(0, 0, k) for k in range(1, team)]
+
+    router_cols = router.shape[1]
+    small = jnp.concatenate(
+        [router, jnp.zeros((wr, 124 - router_cols), F32), norm_gains.T, norm_biases.T], axis=1
+    )
+    own = jnp.concatenate(
+        [
+            w_qkv.reshape(wr, 3, team, width // team)
+            .transpose(2, 0, 1, 3)
+            .reshape(team, wr, qkv_cols),
+            jnp.broadcast_to(small[None], (team, wr, 128)),
+        ],
+        axis=2,
+    ).astype(BF)
+    up_first = (
+        w_up.reshape(wr, two * groups, team, hidden_dev)
+        .transpose(2, 0, 1, 3)
+        .reshape(team, wr, up_cols)
+        .astype(BF)
+    )
+    route_row = jnp.broadcast_to(routes[0, :, 0][None, :], (8, rows))
+    (
+        token_rows,
+        cot_rows,
+        head_parts,
+        normed,
+        weights,
+        vectors,
+        out_weight,
+        ff_part,
+        route_all,
+    ) = start(
+        sizes,
+        tokens[0],
+        cotangent[0],
+        own,
+        up_first,
+        w_down.astype(BF).reshape(team, wr, width),
+        w_out.astype(BF),
+        route_row,
+    )
+    router_weight = weights[:, :, :, :, qkv_cols:].reshape(width, 128)
+    out_weight = out_weight.reshape(width, width)
+    token_rows = token_rows.reshape(group_rows, width)
+    cot_rows = cot_rows.reshape(group_rows, width)
+
+    ff_half = lax.all_gather(
+        ff_part.reshape(2, team * wr, width),
+        "ctx",
+        axis=0,
+        tiled=False,
+        axis_index_groups=by_group,
+    )
+    bounds, inverse, meta = where_rows(
+        block_order, doc_lengths, jnp.arange(length, dtype=jnp.int32), BLOCK
+    )
+    low_t, attention_t, log_total, q_pad, kv_t, kv_rows = sorted_attend(
+        bounds, inverse, block_order, meta, head_parts.reshape(groups, 3 * HEAD_DIM, group_rows)
+    )
+
+    def gather_heads(coords, ins, outs):
+        c, g, t = coords
+        steps = [(0, k, 0) for k in range(1, groups)]
+        moves = [Move(s, ins[0].at[lax.rem(g + s[1], groups)], outs[0].at[t, g]) for s in steps]
+        local = [(ins[0].at[g], outs[0].at[t, g])]
+        for s in team_steps:
+            moves.append(Move(s, ins[0].at[g], outs[0].at[t, g]))
+        for k, s in enumerate(steps):
+            source = lax.rem(g + groups - s[1], groups)
+            for e in team_steps:
+                moves.append(Move(e, outs[0].at[t, source], outs[0].at[t, source], after=k))
+        return local, moves
+
+    [attended] = exchange(
+        "attended",
+        4,
+        sizes,
+        (low_t,),
+        [((team, groups, HEAD_DIM, group_rows), BF)],
+        gather_heads,
+    )
+    (
+        second_low,
+        dense_grad,
+        send_s,
+        send_g,
+        select,
+        mixes,
+        middle_own,
+        prob_own,
+        hot_own,
+        second_own,
+        attended_own,
+    ) = between(
+        experts,
+        sizes,
+        slots,
+        member[None],
+        attended.reshape(width, group_rows),
+        out_weight,
+        token_rows,
+        vectors,
+        router_weight,
+        route_all,
+        cot_rows,
+    )
+    (
+        layer_sum,
+        second_sum,
+        sums_own,
+        expert_active,
+        hidden_grad,
+        arrived_in,
+        arrived_grad,
+        ff_terms,
+    ) = feed_forward(
+        sizes,
+        rows,
+        send_s,
+        send_g,
+        expert_up[0],
+        expert_down[0],
+        second_low,
+        dense_grad,
+        ff_half,
+        select,
+        cot_rows,
+        mixes,
+    )
+    ff_sum = lax.psum_scatter(
+        ff_terms, "ctx", scatter_dimension=0, tiled=True, axis_index_groups=by_group
+    )
+    down_sum = ff_sum[:, :width].astype(F32)
+    up_sum = ff_sum[:, width:].reshape(team, wr, up_cols)
+
+    layer_out, middle_grad, flow_t, out_term, small_t = turn(
+        experts,
+        layer_sum,
+        second_sum,
+        sums_own,
+        middle_own,
+        prob_own,
+        hot_own,
+        second_own,
+        attended_own,
+        cotangent[0],
+        router_weight,
+        out_weight,
+        vectors,
+    )
+    flow_t = flow_t.reshape(team, groups, HEAD_DIM, rows)
+    out_halves = out_term.reshape(two, groups, team, wr, width)
+
+    def spread_flow(coords, ins, outs):
+        c, g, t = coords
+        moves = []
+        for dg in range(groups):
+            for dt in range(team):
+                if dg or dt:
+                    to_g, to_t = lax.rem(g + dg, groups), lax.rem(t + dt, team)
+                    moves.append(Move((0, dg, dt), ins[0].at[to_t, to_g], outs[0].at[g, t]))
+        moves.append(Move((1, 0, 0), ins[1].at[lax.rem(c + 1, two)], outs[1]))
+        return [(ins[0].at[t, g], outs[0].at[g, t])], moves
+
+    flow_parts, out_got = exchange(
+        "flow",
+        8,
+        sizes,
+        (flow_t, out_halves),
+        [((groups, team, HEAD_DIM, rows), BF), (out_halves.shape[1:], BF)],
+        spread_flow,
+    )
+    out_keep = lax.dynamic_index_in_dim(out_halves, core, 0, keepdims=False)
+    out_parts = (out_keep.astype(F32) + out_got.astype(F32)).astype(BF).transpose(1, 0, 2, 3)
+    grad_parts = sorted_back(
+        bounds,
+        inverse,
+        block_order,
+        meta,
+        flow_parts.reshape(ctx_count, HEAD_DIM, rows),
+        attention_t,
+        log_total,
+        q_pad,
+        kv_t,
+        kv_rows,
+        groups,
+    )
+
+    def moved(array, axis, step, base, count, pairs):
+        chunk = lax.dynamic_index_in_dim(
+            array, lax.rem(base + step, count), axis, keepdims=False
+        )
+        return lax.ppermute(chunk, "ctx", pairs)
+
+    group_pairs = [
+        [(g * team + t, (g + k) % groups * team + t) for g in range(groups) for t in range(team)]
+        for k in range(groups)
+    ]
+    team_pairs = [
+        [(g * team + t, g * team + (t + k) % team) for g in range(groups) for t in range(team)]
+        for k in range(team)
+    ]
+    pieces = [lax.dynamic_index_in_dim(grad_parts, group, 0, keepdims=False)]
+    pieces += [moved(grad_parts, 0, k, group, groups, group_pairs[k]) for k in range(1, groups)]
+    out_sum = lax.dynamic_index_in_dim(out_parts, member, 0, keepdims=False).astype(F32)
+    for k in range(1, team):
+        out_sum = out_sum + moved(out_parts, 0, k, member, team, team_pairs[k]).astype(F32)
+    entries = two * groups * slots
+    expert_down_grad = row_sum(expert_active, arrived_grad.reshape(entries, width), TILE)
+    expert_up_grad = row_sum(arrived_in.reshape(entries, width), hidden_grad, 128)
+    input_grad, qkv_own, up_own, out_own, small_own = end(
+        sizes,
+        experts,
+        pieces,
+        weights,
+        normed,
+        tokens[0],
+        vectors,
+        middle_grad,
+        small_t,
+        up_sum,
+        out_sum.astype(BF),
+    )
+    up_own = (
+        up_own.reshape(team, wr, two * groups, hidden_dev)
+        .transpose(1, 2, 0, 3)
+        .reshape(wr, hidden)
+        .astype(F32)
+    )
+    qkv_own = (
+        qkv_own.reshape(team, wr, 3, width // team)
+        .transpose(1, 2, 0, 3)
+        .reshape(wr, 3 * width)
+        .astype(F32)
+    )
+    small_sum = lax.dynamic_slice_in_dim(jnp.sum(small_own, axis=0), member * wr, wr, axis=1)
+    return (
+        layer_out[None],
+        input_grad[None],
+        qkv_own,
+        out_own,
+        up_own,
+        down_sum,
+        small_sum[:router_cols].T,
+        small_sum[router_cols : router_cols + 2],
+        small_sum[router_cols + 2 : router_cols + 4],
+        expert_up_grad,
+        expert_down_grad,
+    )
+
+
 def solution(mesh):
     in_specs = (
         P("dp", "ctx", None),

time: 407 us -> 351 us (0.86)
  Pallas kernels: 320 us -> 264 us
  other arithmetic: 26.8 us -> 4.24 us
  local copies, waits for them, and re-layouts: 40.4 us -> 52.4 us
  starting transfers between devices: 0.08 us -> 11.9 us
  matrix products: 6.16 us -> 0 us
    pallas_call x8 -> x2, Pallas kernels: 201 us -> 50.5 us  [exchange(): pl.pallas_call(kernel, name=name, out_shape=tuple((jax.ShapeDtypeStruct(s...]
    pallas_call x0 -> x2, Pallas kernels: none -> 88.9 us  [the longest x1 50.2 us: start(): pl.pallas_call(functools.partial(start_kernel, sizes), name='start', out_...]
    unnamed x118 -> x144, local copies, waits for them, and re-layouts: 27 us -> 42.9 us
    ppermute x1 -> x6, starting transfers between devices: 0.01 us -> 11.6 us  [moved(): return lax.ppermute(chunk, 'ctx', pairs)]
    reduce_sum x12 -> x3, other arithmetic: 10 us -> 0.2 us  [the longest x1 0.11 us: where_rows(): jnp.sum(jnp.where(block_order[None, :] == number[:, None], number[None, :...]
    convert_element_type x8 -> x5, other arithmetic: 7.11 us -> 0.65 us  [the longest x1 0.4 us: per_device(): (out_keep.astype(F32) + out_got.astype(F32)).astype(BF)]
    pallas_call x1, Pallas kernels: 67.4 us -> 73.6 us  [feed_forward(): pl.pallas_call(functools.partial(feed_kernel, sizes, count), name='feed_f...]
    dot_general x3 -> x0, matrix products: 6.16 us -> none  [the longest x1 2.23 us: per_device(): lax.dot_general(normed_low, mixed_grad_t, (((0,), (1,)), ((), ())), prefe...]
  transfers between devices with their start and end apart: 3 -> 8, of which waited for: 0 -> 1; matrix products, arithmetic and copies ran while one was open for 8% -> 1% of each run, Pallas kernels for 52% -> 29%
where the time goes in v1:
time: 351 us
  Pallas kernels  264 us (75%)
  local copies, waits for them, and re-layouts  52.4 us (15%)
  between operations  14.7 us (4%)
  starting transfers between devices  11.9 us (3%)
  other arithmetic  4.24 us (1%)
  waiting for transfers between devices  3.8 us (1%)
    pallas_call x1, Pallas kernels, feed_forward(): pl.pallas_call(functools.partial(feed_kernel, sizes, count), name='feed_f...  73.6 us
    pallas_call x2, Pallas kernels, exchange(): pl.pallas_call(kernel, name=name, out_shape=tuple((jax.ShapeDtypeStruct(s...  50.5 us
    pallas_call x1, Pallas kernels, start(): pl.pallas_call(functools.partial(start_kernel, sizes), name='start', out_...  50.2 us
    unnamed x144, local copies, waits for them, and re-layouts  42.9 us
    pallas_call x1, Pallas kernels, end(): pl.pallas_call(functools.partial(end_kernel, sizes, experts), name='end',...  38.7 us
    pallas_call x1, Pallas kernels, sorted_back(): pl.pallas_call(sorted_back_kernel, name='attend_back', grid=(length // TI...  13.9 us
    pallas_call x1, Pallas kernels, sorted_attend(): pl.pallas_call(sorted_attend_kernel, name='attend', grid=(length // TILE,...  13.7 us
    pallas_call x2, Pallas kernels, row_sum(): pl.pallas_call(row_sum_kernel, name='row_sum', grid=(high // tile,), in_s...  12.8 us
  transfers between devices with their start and end apart: 8, of which 1 were waited for; matrix products, arithmetic and copies ran while one was open for 1% of the time, Pallas kernels for 29%

profile of v1, /device:TPU:0, one launch (start us, length us, event | category | flops | bytes accessed | tf_op | source)
XLA Modules:
  0.0 351.4 jit_solution(339052610245321731)
XLA Ops:
  9.6 1.1 convert.18
  13.6 50.2 %start.1 = (bf16[4,128,1024]{2,1,0:T(8,128)(2,1)S(1)}, bf16[4,128,1024]{2,1,0:T(8,128)(2,1)S(1)}, bf16[4,3,64,512]{3,2,1,0:T(8,128)(2,1)S(1)}, bf16[4,128,1024]{...) custom-call(bf16[128,1024]{1,0:T(8,128)(2,1)S(1)} %bitcast.82, ...), custom_call_target="tpu_custom_call" | custom-call | bytes 150000000 | tf_op jit(solution)/shard_map/start/pallas_call | solution.py:854
  63.8 1.3 copy-done
  69.7 1.1 copy-done.22
  70.8 13.7 %attend.1 = (bf16[4,64,512]{2,1,0:T(8,128)(2,1)S(1)}, f32[64,2048]{1,0:T(8,128)S(1)}, f32[1,2048]{1,0:T(1,128)S(1)}, bf16[128,2048]{1,0:T(8,128)(2,1)S(1)}, bf16...) custom-call(s32[8,2]{1,0:T(8,128)S(1)} %copy.70.bounds, s32[32]{0:T(128)S(1)} %select_reduce_fusion.1.inverse, ...), custom_call_target="tpu_custom_call" | custom-call | tf_op jit(solution)/shard_map/attend/pallas_call | solution.py:456
  87.6 26.3 %attended.1 = bf16[4,4,64,512]{3,2,1,0:T(8,128)(2,1)} custom-call(bf16[4,64,512]{2,1,0:T(8,128)(2,1)} %copy-done.48), custom_call_target="tpu_custom_call" | custom-call | bytes 60000000 | tf_op jit(solution)/shard_map/attended/pallas_call | solution.py:138
  114.0 1.2 copy-done.4
  115.2 7.7 %between.1 = (bf16[512,1024]{1,0:T(8,128)(2,1)S(1)}, bf16[512,1024]{1,0:T(8,128)(2,1)S(1)}, bf16[4,64,1024]{2,1,0:T(8,128)(2,1)S(1)}, bf16[4,64,1024]{2,1,0:T(8,...) custom-call(s32[1]{0:T(128)} %bitcast.member, ...), custom_call_target="tpu_custom_call" | custom-call | tf_op jit(solution)/shard_map/between/pallas_call | solution.py:578
  131.4 73.6 %feed_forward.1 = (f32[128,1024]{1,0:T(8,128)}, f32[128,1024]{1,0:T(8,128)}, f32[128,128]{1,0:T(8,128)}, bf16[512,2048]{1,0:T(8,128)(2,1)}, bf16[512,2048]{1,0:T...) custom-call(bf16[4,64,1024]{2,1,0:T(8,128)(2,1)} %copy-done.38, ...), custom_call_target="tpu_custom_call" | custom-call | bytes 240000000 | tf_op jit(solution)/shard_map/feed_forward/pallas_call | solution.py:1337
  205.1 1.5 copy-done.1
  215.1 3.2 turn.1
  218.3 1.3 copy-done.2
  221.8 24.2 %flow.1 = (bf16[4,4,64,128]{3,2,1,0:T(8,128)(2,1)}, bf16[4,4,32,1024]{3,2,1,0:T(8,128)(2,1)}) custom-call(bf16[4,4,64,128]{3,2,1,0:T(8,128)(2,1)} %bitcast.91, bf16[2,4,4,32,1024]{4,3,2,1,0:T(8,128)(2,1)} %bitcast.72), custom_call_target="tpu_custom_call" | custom-call | bytes 60000000 | tf_op jit(solution)/shard_map/flow/pallas_call | solution.py:138
  246.9 13.9 %attend_back.1 = bf16[4,3,64,512]{3,2,1,0:T(8,128)(2,1)S(1)} custom-call(s32[8,2]{1,0:T(8,128)S(1)} %copy.70.bounds, s32[32]{0:T(128)S(1)} %select_reduce_fusion.1.inverse, s32[32]{0:T(128)S(1)} %copy-done.63, s32[8,2048]{1,0:T(8,128)S(1)} %add_add_fusion.meta_ref, bf16[16,64,128]{2,1,0:T(8,128)(2,1)S(1)} %bitcast.92, f32[64,2048]{1,0:T(8,128)S(1)} %copy-done.31, ...), custom_call_target="tpu_custom_call" | custom-call | tf_op jit(solution)/shard_map/attend_back/pallas_call | solution.py:471
  261.7 4.2 %collective-permute-start = (bf16[3,64,512]{2,1,0:T(8,128)(2,1)}, bf16[3,64,512]{2,1,0:T(8,128)(2,1)}, u32[]{:S(2)}, u32[]{:S(2)}) collective-permute-start(bf16[3,64,512]{2,1,0:T(8,128)(2,1)} %get-tuple-element.108), channel_id=1, source_target_pairs={{0,4},{1,5},{2,6},{3,7},{4,8},{5,9},{6,10},{7,11},{8,12},{9,13},{1... | collective-permute-start | bytes 589832 | tf_op jit(solution)/shard_map/ppermute | solution.py:2247
  266.0 3.9 %collective-permute-start.1 = (bf16[3,64,512]{2,1,0:T(8,128)(2,1)}, bf16[3,64,512]{2,1,0:T(8,128)(2,1)}, u32[]{:S(2)}, u32[]{:S(2)}) collective-permute-start(bf16[3,64,512]{2,1,0:T(8,128)(2,1)} %get-tuple-element.107), channel_id=1, source_target_pairs={{0,8},{1,9},{2,10},{3,11},{4,12},{5,13},{6,14},{7,15},{8,0},{9,1},... | collective-permute-start | bytes 589832 | tf_op jit(solution)/shard_map/ppermute | solution.py:2247
  270.4 2.0 collective-permute-start.5
  272.4 1.5 collective-permute-start.4
  273.9 6.4 %row_sum.2 = f32[1,1024,2048]{2,1,0:T(8,128)} custom-call(bf16[512,1024]{1,0:T(8,128)(2,1)S(1)} %bitcast.87, bf16[512,2048]{1,0:T(8,128)(2,1)S(1)} %copy-done.9), custom_call_target="tpu_custom_call" | custom-call | flops 2147483648 | bytes 8388608 | tf_op jit(solution)/shard_map/row_sum/pallas_call | solution.py:665
  280.4 6.4 %row_sum.3 = f32[1,2048,1024]{2,1,0:T(8,128)} custom-call(bf16[512,2048]{1,0:T(8,128)(2,1)S(1)} %copy-done.8, bf16[512,1024]{1,0:T(8,128)(2,1)S(1)} %bitcast.86), custom_call_target="tpu_custom_call" | custom-call | flops 2147483648 | bytes 8388608 | tf_op jit(solution)/shard_map/row_sum/pallas_call | solution.py:665
  287.0 2.0 slice_convert_fusion
  289.0 3.7 %collective-permute-done.2.refs_3_ = bf16[3,64,512]{2,1,0:T(8,128)(2,1)} collective-permute-done((bf16[3,64,512]{2,1,0:T(8,128)(2,1)}, bf16[3,64,512]{2,1,0:T(8,128)(2,1)}, u32[]{:S(2)}, u32[]{:S(2)}) %collective-permute-start.2) | collective-permute-done | bytes 196640 | tf_op jit(solution)/shard_map/ppermute | solution.py:2247
  296.6 38.7 %end.1 = (bf16[128,1024]{1,0:T(8,128)(2,1)S(1)}, bf16[4,32,768]{2,1,0:T(8,128)(2,1)S(1)}, bf16[4,32,1024]{2,1,0:T(8,128)(2,1)S(1)}, f32[32,1024]{1,0:T(8,128)S(1)}, f32[4,24,128]{2,1,0:T(8,128)S(1)}) custom-call(bf16[3,64,512]{2,1,0:T(8,128)(2,1)S(1)} %copy-done.20, bf16[3,64,512]{2,1,0:T(8,128)(2,1)} %collective-permute-done.refs_1_, ...), custom_call_target="tpu_custom_call" | custom-call | bytes 120000000 | tf_op jit(solution)/shard_map/end/pallas_call | solution.py:1010
  338.1 1.2 reshape.128
  (194 shorter events, 46.3 us)
Async XLA Ops:
  7.2 4.0 %copy-start.65 = (f32[32,4096]{1,0:T(8,128)S(1)}, f32[32,4096]{1,0:T(8,128)}, u32[]{:S(2)}) copy-start(f32[32,4096]{1,0:T(8,128)} %param.21) | copy-start | bytes 1572868
  7.2 124.2 %all-gather.2.cloned.1.call-start = ((), (), s32[]{:S(2)}) async-start(), calls=%async_computation.1 | async-start | bytes 2621440 | tf_op jit(solution)/shard_map/all_gather | solution.py:2101
  11.5 57.5 %copy-start.69 = (s32[1,8]{1,0:T(1,128)S(1)}, s32[1,8]{1,0:T(1,128)}, u32[]{:S(2)}) copy-start(s32[1,8]{1,0:T(1,128)} %param.17) | copy-start | bytes 100
  11.5 58.0 %copy-start.63 = (s32[32]{0:T(128)S(1)}, s32[32]{0:T(128)}, u32[]{:S(2)}) copy-start(s32[32]{0:T(128)} %order.3) | copy-start | bytes 388
  68.7 54.2 %copy-start.6 = (bf16[2,4,4,32,896]{4,3,2,1,0:T(8,128)(2,1)}, bf16[2,4,4,32,896]{4,3,2,1,0:T(8,128)(2,1)S(1)}, u32[]{:S(2)}) copy-start(bf16[2,4,4,32,896]{4,3,2,1,0:T(8,128)(2,1)S(1)} %get-tuple-element.62.refs_4_) | copy-start | bytes 5505028
  68.7 218.2 %reduce-scatter.2.cloned.1.call-start = ((), (), s32[]{:S(2)}) async-start(), calls=%async_computation.2 | async-start | bytes 2621440 | tf_op jit(solution)/shard_map/reduce_scatter | solution.py:2184
  87.6 26.3 %copy-start.36 = (bf16[2048,128]{1,0:T(8,128)(2,1)}, bf16[2048,128]{1,0:T(8,128)(2,1)S(1)}, u32[]{:S(2)}) copy-start(bf16[2048,128]{1,0:T(8,128)(2,1)S(1)} %get-tuple-element.88.rows_ref) | copy-start | bytes 1572868
  221.8 24.2 %copy-start.31 = (f32[64,2048]{1,0:T(8,128)S(1)}, f32[64,2048]{1,0:T(8,128)}, u32[]{:S(2)}) copy-start(f32[64,2048]{1,0:T(8,128)} %copy-done.30) | copy-start | bytes 1572868
  221.8 24.2 %copy-start.33 = (bf16[128,2048]{1,0:T(8,128)(2,1)S(1)}, bf16[128,2048]{1,0:T(8,128)(2,1)}, u32[]{:S(2)}) copy-start(bf16[128,2048]{1,0:T(8,128)(2,1)} %copy-done.32) | copy-start | bytes 1572868
  221.8 24.2 %copy-start.35 = (bf16[128,2048]{1,0:T(8,128)(2,1)S(1)}, bf16[128,2048]{1,0:T(8,128)(2,1)}, u32[]{:S(2)}) copy-start(bf16[128,2048]{1,0:T(8,128)(2,1)} %copy-done.34) | copy-start | bytes 1572868
  221.8 24.2 %copy-start.37 = (bf16[2048,128]{1,0:T(8,128)(2,1)S(1)}, bf16[2048,128]{1,0:T(8,128)(2,1)}, u32[]{:S(2)}) copy-start(bf16[2048,128]{1,0:T(8,128)(2,1)} %copy-done.36) | copy-start | bytes 1572868
  246.9 23.0 %copy-start.3 = (bf16[1024,1024]{1,0:T(8,128)(2,1)S(1)}, bf16[1024,1024]{1,0:T(8,128)(2,1)}, u32[]{:S(2)}) copy-start(bf16[1024,1024]{1,0:T(8,128)(2,1)} %copy-done.2) | copy-start | bytes 6291460
  246.9 23.0 %copy-start.64 = (bf16[4,4,32,1024]{3,2,1,0:T(8,128)(2,1)S(1)}, bf16[4,4,32,1024]{3,2,1,0:T(8,128)(2,1)}, u32[]{:S(2)}) copy-start(bf16[4,4,32,1024]{3,2,1,0:T(8,128)(2,1)} %get-tuple-element.93) | copy-start | bytes 3145732
  261.7 27.3 %collective-permute-start = (bf16[3,64,512]{2,1,0:T(8,128)(2,1)}, bf16[3,64,512]{2,1,0:T(8,128)(2,1)}, u32[]{:S(2)}, u32[]{:S(2)}) collective-permute-start(bf16[3,64,512]{2,1,0:T(8,128)(2,1)} %get-tuple-element.108), channel_id=1, source_target_pairs={{0,4},{1,5},{2,6},{3,7},{4,8},{5,9},{6,10},{7,11},{8,12},{9,13},{1... | collective-permute-start | bytes 589832 | tf_op jit(solution)/shard_map/ppermute | solution.py:2247
  266.0 23.0 %collective-permute-start.1 = (bf16[3,64,512]{2,1,0:T(8,128)(2,1)}, bf16[3,64,512]{2,1,0:T(8,128)(2,1)}, u32[]{:S(2)}, u32[]{:S(2)}) collective-permute-start(bf16[3,64,512]{2,1,0:T(8,128)(2,1)} %get-tuple-element.107), channel_id=1, source_target_pairs={{0,8},{1,9},{2,10},{3,11},{4,12},{5,13},{6,14},{7,15},{8,0},{9,1},... | collective-permute-start | bytes 589832 | tf_op jit(solution)/shard_map/ppermute | solution.py:2247
  269.9 4.0 %copy-start.9 = (bf16[512,2048]{1,0:T(8,128)(2,1)S(1)}, bf16[512,2048]{1,0:T(8,128)(2,1)}, u32[]{:S(2)}) copy-start(bf16[512,2048]{1,0:T(8,128)(2,1)} %get-tuple-element.100.right) | copy-start | bytes 6291460
  269.9 4.0 %copy-start.17 = (bf16[2,4,64,1024]{3,2,1,0:T(8,128)(2,1)S(1)}, bf16[2,4,64,1024]{3,2,1,0:T(8,128)(2,1)}, u32[]{:S(2)}) copy-start(bf16[2,4,64,1024]{3,2,1,0:T(8,128)(2,1)} %get-tuple-element.99) | copy-start | bytes 3145732
  270.4 16.4 %collective-permute-start.5 = (bf16[4,32,1024]{2,1,0:T(8,128)(2,1)S(1)}, bf16[4,32,1024]{2,1,0:T(8,128)(2,1)S(1)}, u32[]{:S(2)}, u32[]{:S(2)}) collective-permute-start(bf16[4,32,1024]{2,1,0:T(8,128)(2,1)S(1)} %get-tuple-element.104), channel_id=1, source_target_pairs={{0,3},{1,0},{2,1},{3,2},{4,7},{5,4},{6,5},{7,6},{8,11},{9,8},{10,9... | collective-permute-start | bytes 786440 | tf_op jit(solution)/shard_map/ppermute | solution.py:2247
  272.4 14.3 %collective-permute-start.4 = (bf16[4,32,1024]{2,1,0:T(8,128)(2,1)S(1)}, bf16[4,32,1024]{2,1,0:T(8,128)(2,1)S(1)}, u32[]{:S(2)}, u32[]{:S(2)}) collective-permute-start(bf16[4,32,1024]{2,1,0:T(8,128)(2,1)S(1)} %get-tuple-element.105), channel_id=1, source_target_pairs={{0,2},{1,3},{2,0},{3,1},{4,6},{5,7},{6,4},{7,5},{8,10},{9,11},{10,... | collective-permute-start | bytes 786440 | tf_op jit(solution)/shard_map/ppermute | solution.py:2247
  273.9 12.9 %collective-permute-start.3 = (bf16[4,32,1024]{2,1,0:T(8,128)(2,1)S(1)}, bf16[4,32,1024]{2,1,0:T(8,128)(2,1)S(1)}, u32[]{:S(2)}, u32[]{:S(2)}) collective-permute-start(bf16[4,32,1024]{2,1,0:T(8,128)(2,1)S(1)} %get-tuple-element.103), channel_id=1, source_target_pairs={{0,1},{1,2},{2,3},{3,0},{4,5},{5,6},{6,7},{7,4},{8,9},{9,10},{10,1... | collective-permute-start | bytes 786440 | tf_op jit(solution)/shard_map/ppermute | solution.py:2247
  273.9 6.5 %copy-start.8 = (bf16[512,2048]{1,0:T(8,128)(2,1)S(1)}, bf16[512,2048]{1,0:T(8,128)(2,1)}, u32[]{:S(2)}) copy-start(bf16[512,2048]{1,0:T(8,128)(2,1)} %get-tuple-element.101.left) | copy-start | bytes 6291460
  273.9 6.5 %copy-start.16 = (bf16[2,4,64,1024]{3,2,1,0:T(8,128)(2,1)S(1)}, bf16[2,4,64,1024]{3,2,1,0:T(8,128)(2,1)}, u32[]{:S(2)}) copy-start(bf16[2,4,64,1024]{3,2,1,0:T(8,128)(2,1)} %get-tuple-element.102) | copy-start | bytes 3145732
  286.8 6.0 %copy-start.7 = (bf16[2,4,4,32,896]{4,3,2,1,0:T(8,128)(2,1)S(1)}, bf16[2,4,4,32,896]{4,3,2,1,0:T(8,128)(2,1)}, u32[]{:S(2)}) copy-start(bf16[2,4,4,32,896]{4,3,2,1,0:T(8,128)(2,1)} %copy-done.6) | copy-start | bytes 5505028
  286.8 6.0 %collective-permute-start.2 = (bf16[3,64,512]{2,1,0:T(8,128)(2,1)}, bf16[3,64,512]{2,1,0:T(8,128)(2,1)}, u32[]{:S(2)}, u32[]{:S(2)}) collective-permute-start(bf16[3,64,512]{2,1,0:T(8,128)(2,1)} %get-tuple-element.106), channel_id=1, source_target_pairs={{0,12},{1,13},{2,14},{3,15},{4,0},{5,1},{6,2},{7,3},{8,4},{9,5},{1... | collective-permute-start | bytes 589832 | tf_op jit(solution)/shard_map/ppermute | solution.py:2247
  (54 other events, 58.7 us)
Sparse Core Ops, SparseCore 0:
  68.9 56.5 all-gather.1
  205.1 57.5 reduce-scatter.1

commit v2 on v1

--- a/solution.py
+++ b/solution.py
@@ -322,9 +322,27 @@
     return ref[lax.div(k, per), :, span(lax.rem(k, per), 128)].astype(F32)
 
 
+def fill_inverse(order, inverse, count):
+    def put(n, carry):
+        inverse[order[n]] = n
+        return carry
+
+    lax.fori_loop(0, count, put, 0)
+
+
+def query_lows(lengths, step):
+    place = lax.broadcasted_iota(jnp.int32, (1, TILE), 1) + step * TILE
+    low = jnp.zeros((1, TILE), jnp.int32)
+    first, end = 0, 0
+    for n in range(lengths.shape[0]):
+        end = end + lengths[n]
+        low = jnp.where(end <= place, end, low)
+        first = jnp.where(end <= step * TILE, end, first)
+    return place, low, lax.div(first, TILE)
+
+
 def sorted_attend_kernel(
-    bounds, inverse, order, meta_ref, parts_ref,
-    low_ref, out_ref, lse_ref, q_ref, kvt_ref, rows_ref,
+    lengths, order, parts_ref, low_ref, out_ref, lse_ref, q_ref, kvt_ref, rows_ref, inverse
 ):
     step = pl.program_id(0)
     length = q_ref.shape[1]
@@ -332,6 +350,8 @@
 
     @pl.when(step == 0)
     def _():
+        fill_inverse(order, inverse, length // BLOCK)
+
         def place(d, carry):
             tile = pick_pair(lambda k: column_block(parts_ref, k, per), inverse, d)
             at = span(d, 128)
@@ -345,7 +365,7 @@
 
     here = span(step, TILE)
     queries = q_ref[:, here]
-    place, low = meta_ref[0:1, :], meta_ref[1:2, :]
+    place, low, first = query_lows(lengths, step)
 
     def body(kt, carry):
         peak, total, acc = carry
@@ -365,7 +385,7 @@
         jnp.zeros((1, TILE), F32),
         jnp.zeros((HEAD_DIM, TILE), F32),
     )
-    peak, total, acc = lax.fori_loop(bounds[step, 0], bounds[step, 1], body, start)
+    peak, total, acc = lax.fori_loop(first, step + 1, body, start)
     out_ref[:, here] = acc / total
     lse_ref[:, here] = peak + jnp.log(total)
 
@@ -380,8 +400,8 @@
 
 
 def sorted_back_kernel(
-    bounds, inverse, order, meta_ref, flow_ref, out_ref, lse_ref, q_ref, kvt_ref, rows_ref,
-    grad_ref, do_ref, dq_ref, acc_ref,
+    lengths, order, flow_ref, out_ref, lse_ref, q_ref, kvt_ref, rows_ref,
+    grad_ref, do_ref, dq_ref, acc_ref, inverse,
 ):
     step = pl.program_id(0)
     length = q_ref.shape[1]
@@ -390,6 +410,7 @@
     @pl.when(step == 0)
     def _():
         acc_ref[...] = jnp.zeros_like(acc_ref)
+        fill_inverse(order, inverse, length // BLOCK)
 
         def place(d, carry):
             tile = pick_pair(lambda k: flow_ref[k].astype(F32), inverse, d)
@@ -402,7 +423,7 @@
 
     here = span(step, TILE)
     queries, flows = q_ref[:, here], do_ref[:, here]
-    place, low = meta_ref[0:1, :], meta_ref[1:2, :]
+    place, low, first = query_lows(lengths, step)
     log_total = lse_ref[:, here]
     delta = jnp.sum(flows[HEAD_DIM:, :].astype(F32) * out_ref[:, here], axis=0, keepdims=True)
 
@@ -420,7 +441,7 @@
         return dq
 
     dq = lax.fori_loop(
-        bounds[step, 0], bounds[step, 1], body, jnp.zeros((HEAD_DIM, TILE), F32)
+        first, step + 1, body, jnp.zeros((HEAD_DIM, TILE), F32)
     )
     dq_ref[:, here] = dq * SCALE
 
@@ -442,7 +463,7 @@
     return pl.BlockSpec(shape, lambda i: (0,) * len(shape))
 
 
-def sorted_attend(bounds, inverse, order, meta, parts):
+def sorted_attend(lengths, order, parts):
     groups, _, columns = parts.shape
     length = groups * columns
     shapes = (
@@ -457,23 +478,25 @@
         sorted_attend_kernel,
         name="attend",
         grid=(length // TILE,),
-        in_specs=[pl.BlockSpec(memory_space=pltpu.SMEM)] * 3
-        + [pl.BlockSpec((8, TILE), lambda i: (0, i)), fixed(parts.shape)],
+        in_specs=[pl.BlockSpec(memory_space=pltpu.SMEM)] * 2 + [fixed(parts.shape)],
         out_specs=tuple(fixed(s) for s, _ in shapes),
         out_shape=tuple(jax.ShapeDtypeStruct(s, d) for s, d in shapes),
-        compiler_params=pltpu.CompilerParams(vmem_limit_bytes=40 * 2**20),
-    )(bounds, inverse, order, meta, parts)
-
-
-def sorted_back(bounds, inverse, order, meta, flow, out, lse, q_pad, kv_t, kv_rows, groups):
+        scratch_shapes=[pltpu.SMEM((length // BLOCK,), jnp.int32)],
+        compiler_params=pltpu.CompilerParams(vmem_limit_bytes=60 * 2**20),
+        cost_estimate=pl.CostEstimate(
+            flops=0, bytes_accessed=42_000_000, transcendentals=0
+        ),
+    )(lengths, order, parts)
+
+
+def sorted_back(lengths, order, flow, out, lse, q_pad, kv_t, kv_rows, groups):
     length = out.shape[1]
     grad = (groups, 3, HEAD_DIM, length // groups)
     return pl.pallas_call(
         sorted_back_kernel,
         name="attend_back",
         grid=(length // TILE,),
-        in_specs=[pl.BlockSpec(memory_space=pltpu.SMEM)] * 3
-        + [pl.BlockSpec((8, TILE), lambda i: (0, i))]
+        in_specs=[pl.BlockSpec(memory_space=pltpu.SMEM)] * 2
         + [fixed(a.shape) for a in (flow, out, lse, q_pad, kv_t, kv_rows)],
         out_specs=fixed(grad),
         out_shape=jax.ShapeDtypeStruct(grad, BF),
@@ -481,9 +504,13 @@
             pltpu.VMEM((2 * HEAD_DIM, length), BF),
             pltpu.VMEM((HEAD_DIM, length), F32),
             pltpu.VMEM((2 * HEAD_DIM, length), F32),
+            pltpu.SMEM((length // BLOCK,), jnp.int32),
         ],
         compiler_params=pltpu.CompilerParams(vmem_limit_bytes=40 * 2**20),
-    )(bounds, inverse, order, meta, flow, out, lse, q_pad, kv_t, kv_rows)
+        cost_estimate=pl.CostEstimate(
+            flops=0, bytes_accessed=42_000_000, transcendentals=0
+        ),
+    )(lengths, order, flow, out, lse, q_pad, kv_t, kv_rows)
 
 
 def normalize(values):
@@ -582,7 +609,7 @@
         out_specs=tuple(inside for _ in shapes),
         out_shape=tuple(jax.ShapeDtypeStruct(s, d) for s, d in shapes),
         scratch_shapes=[pltpu.VMEM((group_rows, width), BF)],
-        compiler_params=pltpu.CompilerParams(vmem_limit_bytes=48 * 2**20),
+        compiler_params=pltpu.CompilerParams(vmem_limit_bytes=60 * 2**20),
     )(member, att, wo, x, vec, rw, route, cot)
 
 
@@ -756,32 +783,54 @@
 
 
 def start_kernel(sizes, *refs):
-    tokens, cot, own, up, down, out, route = refs[:7]
-    token_o, cot_o, heads_o, normed_o, weight_o, vec_o, out_o, ff_o, route_o = refs[7:16]
-    stage, weights, tokens_v, normed, mixed, heads, out_v, send_sem, recv_sem, local_sem = refs[16:]
+    tokens, cot, w_qkv, w_up, w_down, w_out, router, gains, biases, routes = refs[:10]
+    token_o, cot_o, heads_o, normed_o, weight_o, vec_o, out_o, ff_o, route_o = refs[10:19]
+    (
+        own, up, down, route, square, stage, weights, tokens_v, normed, mixed, heads, out_v,
+        send_sem, recv_sem, local_sem,
+    ) = refs[19:]
     net, local = Net(sizes, send_sem, recv_sem), Local(local_sem)
     c, g, t = net.c, net.g, net.t
     two, groups, team = sizes
     rows, width = tokens.shape
     used = own.shape[2] - 128
-    own_stage = local.copy(own.at[t], stage.at[t])
+    wr = own.shape[1]
     own_tokens = local.copy(tokens, tokens_v.at[t])
-    own_out = local.copy(out, out_v.at[g])
     local.copy(cot, cot_o.at[t])
+
+    square[...] = jnp.zeros_like(square)
+    square[: router.shape[0], :wr] = router[...]
+    square[124:126, :wr] = gains[...]
+    square[126:128, :wr] = biases[...]
+    small = square[...].T[:wr, :].astype(BF)
+    third = used // 3
+    for n in range(team):
+        for k in range(3):
+            at = k * width + n * third
+            own[n, :, k * third : (k + 1) * third] = w_qkv[:, at : at + third].astype(BF)
+        own[n, :, used:] = small
+    stage[t] = own[t]
+    net.greet()
+    staged = [net.send(own.at[net.team_to(s)], stage.at[t], s) for s in net.team_steps]
+    told = [net.send(tokens, tokens_v.at[t], s) for s in net.team_steps]
+    out_v[g] = w_out[...].astype(BF)
+    spread_out = [net.send(out_v.at[g], out_v.at[g], s) for s in net.group_steps]
+    deep = w_down.shape[0]
+    for n in range(team):
+        for k in range(two * groups):
+            at = (k * team + n) * deep
+            up[n, :, k * deep : (k + 1) * deep] = w_up[:, at : at + deep].astype(BF)
+    down[...] = w_down[...].astype(BF).reshape(down.shape)
+    route[...] = jnp.broadcast_to(routes[...], route.shape)
     local.copy(up.at[t], ff_o.at[0, t])
     local.copy(down, ff_o.at[1])
     local.copy(route, route_o.at[t])
-    net.greet()
-    staged = [net.send(own.at[net.team_to(s)], stage.at[t], s) for s in net.team_steps]
-    told = [net.send(tokens, tokens_v.at[t], s) for s in net.team_steps]
     later = [net.send(route, route_o.at[t], s) for s in net.team_steps]
     later += [net.send(up.at[net.team_to(s)], ff_o.at[0, t], s) for s in net.team_steps]
-    local.wait(own_stage)
     arrive(staged)
     spread = [net.send(stage, weights.at[c, g], s) for s in net.group_steps]
     swapped = [net.send(stage, weights.at[c, g], net.swap)]
     mine = local.copy(stage, weights.at[c, g])
-    spread_out = [net.send(out, out_v.at[g], s) for s in net.group_steps]
     later += [net.send(cot, cot_o.at[t], s) for s in net.team_steps]
     local.wait(own_tokens)
     arrive(told)
@@ -815,7 +864,6 @@
     given = [net.send(mixed.at[:, net.group_to(s)], heads.at[g], s) for s in net.group_steps]
     local.wait(local.copy(mixed.at[:, g], heads.at[g]))
 
-    local.wait(own_out)
     arrive(spread_out)
     local.copy(out_v, out_o.at[c, :, t])
     swapped = [net.send(out_v, out_o.at[c, :, t], net.swap)]
@@ -831,12 +879,14 @@
     net.close()
 
 
-def start(sizes, tokens, cot, own, up, down, out, route):
+def start(sizes, tokens, cot, w_qkv, w_up, w_down, w_out, router, gains, biases, routes):
     two, groups, team = sizes
     rows, width = tokens.shape
-    wr, cols = own.shape[1], own.shape[2]
-    used = cols - 128
+    wr = w_qkv.shape[0]
+    used = 3 * width // team
+    cols = used + 128
     head = (3, groups, HEAD_DIM, team * rows)
+    up = (team, wr, width)
     shapes = (
         ((team, rows, width), BF),
         ((team, rows, width), BF),
@@ -845,8 +895,8 @@
         ((two, groups, team, wr, cols), BF),
         ((8, width), F32),
         ((two, groups, team, wr, width), BF),
-        ((2,) + up.shape, BF),
-        ((team,) + route.shape, jnp.int32),
+        ((2,) + up, BF),
+        ((team, 8, rows), jnp.int32),
     )
     anywhere = pl.BlockSpec(memory_space=pl.ANY)
     inside = pl.BlockSpec(memory_space=pltpu.VMEM)
@@ -855,9 +905,14 @@
         functools.partial(start_kernel, sizes),
         name="start",
         out_shape=tuple(jax.ShapeDtypeStruct(s, d) for s, d in shapes),
-        in_specs=[anywhere] * 7,
+        in_specs=[anywhere] * 2 + [inside] * 8,
         out_specs=tuple(inside if n == 5 else anywhere for n in range(9)),
         scratch_shapes=[
+            pltpu.VMEM((team, wr, cols), BF),
+            pltpu.VMEM(up, BF),
+            pltpu.VMEM(up, BF),
+            pltpu.VMEM((8, rows), jnp.int32),
+            pltpu.VMEM((128, 128), F32),
             pltpu.VMEM((team, wr, cols), BF),
             pltpu.VMEM((two, groups, team, wr, cols), BF),
             pltpu.VMEM((team, rows, width), BF),
@@ -870,10 +925,10 @@
             pltpu.SemaphoreType.DMA((14,)),
         ],
         compiler_params=pltpu.CompilerParams(
-            collective_id=12, has_side_effects=True, vmem_limit_bytes=32 * 2**20
+            collective_id=12, has_side_effects=True, vmem_limit_bytes=60 * 2**20
         ),
         cost_estimate=pl.CostEstimate(flops=0, bytes_accessed=150_000_000, transcendentals=0),
-    )(tokens, cot, own, up, down, out, route)
+    )(tokens, cot, w_qkv, w_up, w_down, w_out, router, gains, biases, routes)
 
 
 def end_kernel(sizes, experts, *refs):
@@ -882,7 +937,7 @@
     weight, normed, tokens, vec, middle_grad, small, up, out = refs[:8]
     grad_o, qkv_o, up_o, out_o, small_o = refs[8:13]
     (
-        mixed, turned, weights, normed_v, give, got, zsend, zrecv, npart, nrecv, qsend, qrecv,
+        up_r, small_d, mixed, turned, weights, normed_v, give, got, zsend, zrecv, npart, nrecv, qsend, qrecv,
         out_r, small_a, small_b, small_c, send_sem, recv_sem, local_sem,
     ) = refs[13:]
     net, local = Net(sizes, send_sem, recv_sem), Local(local_sem)
@@ -894,10 +949,11 @@
         local.copy(part, mixed.at[:, net.group_from((0, k, 0))])
     local.copy(normed, normed_v)
     local.copy(weight, weights)
-    local.copy(up.at[t], up_o.at[t])
+    local.copy(up.at[t], up_r.at[t])
     local.copy(out.at[g], out_r.at[g])
     net.greet()
-    later = [net.send(up.at[net.team_to(s)], up_o.at[t], s) for s in net.team_steps]
+    outed = [net.send(out.at[net.group_to(s)], out_r.at[g], s) for s in net.group_steps]
+    later = [net.send(up.at[net.team_to(s)], up_r.at[t], s) for s in net.team_steps]
     local.wait()
     per = used // 3 // 128
     pair = 128 // HEAD_DIM
@@ -942,7 +998,6 @@
         net.send(zsend.at[span(net.group_to(s), deep), :], zrecv.at[g], s)
         for s in net.group_steps
     ]
-    outed = [net.send(out.at[net.group_to(s)], out_r.at[g], s) for s in net.group_steps]
     zrecv[g] = zsend[span(g, deep), :]
 
     arrive(owned)
@@ -976,8 +1031,8 @@
     ]
     small_b[g] = small_c[:, columns_of(g)]
     arrive(moved)
-    small_o[t] = jnp.sum(small_b[...], axis=0)
-    later += [net.send(small_o.at[t], small_o.at[t], s) for s in net.team_steps]
+    small_d[t] = jnp.sum(small_b[...], axis=0)
+    later += [net.send(small_d.at[t], small_d.at[t], s) for s in net.team_steps]
 
     arrive(summed)
     qsend[...] = jnp.sum(zrecv[...].astype(F32), axis=0).astype(BF).reshape(qsend.shape)
@@ -986,7 +1041,16 @@
     arrive(outed)
     out_o[...] = jnp.sum(out_r[...].astype(F32), axis=0)
     arrive(later)
-    qkv_o[...] = qrecv[...]
+    small_o[...] = jnp.sum(small_d[...], axis=0)
+    third = used // 3
+    deep = up_o.shape[1] // (2 * groups * team)
+    for n in range(team):
+        for k in range(3):
+            at = k * width + n * third
+            qkv_o[:, at : at + third] = qrecv[n, :, k * third : (k + 1) * third].astype(F32)
+        for k in range(2 * groups):
+            at = (k * team + n) * deep
+            up_o[:, at : at + deep] = up_r[n, :, k * deep : (k + 1) * deep].astype(F32)
     net.close()
 
 
@@ -999,10 +1063,10 @@
     half = width // 2
     shapes = (
         ((rows, width), BF),
-        ((team, wr, used), BF),
-        ((team, wr, width), BF),
+        ((wr, 3 * width), F32),
+        ((wr, team * width), F32),
         ((wr, width), F32),
-        ((team, small.shape[0], 128), F32),
+        ((small.shape[0], 128), F32),
     )
     anywhere = pl.BlockSpec(memory_space=pl.ANY)
     inside = pl.BlockSpec(memory_space=pltpu.VMEM)
@@ -1014,6 +1078,8 @@
         in_specs=[anywhere] * (groups + 2) + [inside] * 4 + [anywhere] * 2,
         out_specs=tuple(inside for _ in shapes),
         scratch_shapes=[
+            pltpu.VMEM((team, wr, width), BF),
+            pltpu.VMEM((team, small.shape[0], 128), F32),
             pltpu.VMEM((3, groups, HEAD_DIM, group_rows), BF),
             pltpu.VMEM((group_rows, used), BF),
             pltpu.VMEM(weight.shape, BF),
@@ -1035,7 +1101,7 @@
             pltpu.SemaphoreType.DMA((groups + 4,)),
         ],
         compiler_params=pltpu.CompilerParams(
-            collective_id=13, has_side_effects=True, vmem_limit_bytes=32 * 2**20
+            collective_id=13, has_side_effects=True, vmem_limit_bytes=60 * 2**20
         ),
         cost_estimate=pl.CostEstimate(flops=0, bytes_accessed=120_000_000, transcendentals=0),
     )(*parts, weight, normed, tokens, vec, middle_grad, small, up, out)
@@ -1590,26 +1656,12 @@
             jnp.where(doc_ends[None, :] <= place[:, None], doc_ends[None, :], 0), axis=1
         )
 
-    sorted_rows = reps == 1 and block_rows == BLOCK
     query_length = length // reps
     tiles = query_length // TILE
     part = lax.rem(group, reps)
-    if sorted_rows:
-        query_place = all_rows
-        lows = low_of(all_rows)
-        bounds = jnp.stack(
-            [lows[::TILE] // TILE, jnp.arange(1, tiles + 1, dtype=jnp.int32)], axis=1
-        )
-        number = jnp.arange(block_order.shape[0], dtype=jnp.int32)
-        inverse = jnp.sum(
-            jnp.where(block_order[None, :] == number[:, None], number[None, :], 0), axis=1
-        )
-    else:
-        query_place = lax.dynamic_slice(all_place, (part * query_length,), (query_length,))
-        lows = low_of(query_place)
-        bounds = jnp.broadcast_to(
-            jnp.array([[0, length // TILE]], dtype=jnp.int32), (tiles, 2)
-        )
+    query_place = lax.dynamic_slice(all_place, (part * query_length,), (query_length,))
+    lows = low_of(query_place)
+    bounds = jnp.broadcast_to(jnp.array([[0, length // TILE]], dtype=jnp.int32), (tiles, 2))
     meta = jnp.concatenate(
         [query_place[None], lows[None], jnp.zeros((6, query_length), jnp.int32)], axis=0
     )
@@ -1654,27 +1706,22 @@
     )
     out_weight = out_weight.reshape(width, width)
     head_parts = head_parts.reshape(groups, 3 * HEAD_DIM, group_rows)
-    if sorted_rows:
-        low_t, attention_t, log_total, q_pad, kv_t, kv_rows = sorted_attend(
-            bounds, inverse, block_order, meta, head_parts
-        )
-    else:
-        place_col = all_place[:, None]
-        head_t = head_parts.transpose(1, 0, 2).reshape(3 * HEAD_DIM, length)
-        zeros = jnp.zeros((HEAD_DIM, query_length), BF)
-        kv_t = head_t[HEAD_DIM:]
-        kv_rows = kv_t.T
-        q_t = lax.dynamic_slice(
-            head_t[:HEAD_DIM], (0, part * query_length), (HEAD_DIM, query_length)
-        )
-        q_pad = jnp.concatenate([q_t * jnp.asarray(SCALE, BF), zeros], axis=0)
-        attention_t, log_total = attend(False, bounds, meta, place_col, q_pad, kv_rows, kv_t)
-        low_t = lax.dynamic_update_slice(
-            jnp.zeros((HEAD_DIM, length), BF),
-            attention_t.astype(BF),
-            (0, part * query_length),
-        )
-        low_t = low_t.reshape(HEAD_DIM, groups, group_rows).transpose(1, 0, 2)
+    place_col = all_place[:, None]
+    head_t = head_parts.transpose(1, 0, 2).reshape(3 * HEAD_DIM, length)
+    zeros = jnp.zeros((HEAD_DIM, query_length), BF)
+    kv_t = head_t[HEAD_DIM:]
+    kv_rows = kv_t.T
+    q_t = lax.dynamic_slice(
+        head_t[:HEAD_DIM], (0, part * query_length), (HEAD_DIM, query_length)
+    )
+    q_pad = jnp.concatenate([q_t * jnp.asarray(SCALE, BF), zeros], axis=0)
+    attention_t, log_total = attend(False, bounds, meta, place_col, q_pad, kv_rows, kv_t)
+    low_t = lax.dynamic_update_slice(
+        jnp.zeros((HEAD_DIM, length), BF),
+        attention_t.astype(BF),
+        (0, part * query_length),
+    )
+    low_t = low_t.reshape(HEAD_DIM, groups, group_rows).transpose(1, 0, 2)
 
     def gather_heads(coords, ins, outs):
         c, g, t = coords
@@ -1802,43 +1849,28 @@
         [((groups, team, HEAD_DIM, rows), BF), (out_halves.shape[1:], BF)],
         spread_flow,
     )
-    if sorted_rows:
-        grad_parts = sorted_back(
-            bounds,
-            inverse,
-            block_order,
-            meta,
-            flow_parts.reshape(ctx_count, HEAD_DIM, rows),
-            attention_t,
-            log_total,
-            q_pad,
-            kv_t,
-            kv_rows,
-            groups,
-        )
-    else:
-        flow_all = flow_parts.transpose(2, 0, 1, 3).reshape(HEAD_DIM, length)
-        flow_all = lax.dynamic_slice(
-            flow_all, (0, part * query_length), (HEAD_DIM, query_length)
-        )
-        do_pad = jnp.concatenate([zeros, flow_all], axis=0)
-        query_grad, pair_grad = attend_back(
-            False,
-            bounds,
-            meta,
-            place_col,
-            q_pad,
-            do_pad,
-            attention_t,
-            log_total,
-            kv_rows,
-            kv_t,
-        )
-        query_grad = lax.dynamic_update_slice(
-            jnp.zeros((HEAD_DIM, length), BF), query_grad, (0, part * query_length)
-        )
-        grad_parts = jnp.concatenate([query_grad, pair_grad], axis=0)
-        grad_parts = grad_parts.reshape(3, HEAD_DIM, groups, group_rows).transpose(2, 0, 1, 3)
+    flow_all = flow_parts.transpose(2, 0, 1, 3).reshape(HEAD_DIM, length)
+    flow_all = lax.dynamic_slice(
+        flow_all, (0, part * query_length), (HEAD_DIM, query_length)
+    )
+    do_pad = jnp.concatenate([zeros, flow_all], axis=0)
+    query_grad, pair_grad = attend_back(
+        False,
+        bounds,
+        meta,
+        place_col,
+        q_pad,
+        do_pad,
+        attention_t,
+        log_total,
+        kv_rows,
+        kv_t,
+    )
+    query_grad = lax.dynamic_update_slice(
+        jnp.zeros((HEAD_DIM, length), BF), query_grad, (0, part * query_length)
+    )
+    grad_parts = jnp.concatenate([query_grad, pair_grad], axis=0)
+    grad_parts = grad_parts.reshape(3, HEAD_DIM, groups, group_rows).transpose(2, 0, 1, 3)
     out_keep = lax.dynamic_index_in_dim(out_halves, core, 0, keepdims=False)
     out_parts = tall(
         (out_keep.astype(F32) + out_got.astype(F32))
@@ -1992,22 +2024,472 @@
     )
 
 
-def where_rows(block_order, doc_lengths, rows, block_rows):
-    doc_id = jnp.arange(doc_lengths.shape[1], dtype=jnp.int32)
-    doc_ends = jnp.sum(
-        jnp.where(doc_id[:, None] <= doc_id[None, :], doc_lengths[0][:, None], 0), axis=0
-    )
-    lows = jnp.max(jnp.where(doc_ends[None, :] <= rows[:, None], doc_ends[None, :], 0), axis=1)
-    tiles = rows.shape[0] // TILE
-    bounds = jnp.stack([lows[::TILE] // TILE, jnp.arange(1, tiles + 1, dtype=jnp.int32)], axis=1)
-    number = jnp.arange(block_order.shape[0], dtype=jnp.int32)
-    inverse = jnp.sum(
-        jnp.where(block_order[None, :] == number[:, None], number[None, :], 0), axis=1
-    )
-    meta = jnp.concatenate(
-        [rows[None], lows[None], jnp.zeros((6, rows.shape[0]), jnp.int32)], axis=0
-    )
-    return bounds, inverse, meta
+def whole_kernel(sizes, experts, copies_count, *refs):
+    two, groups, team = sizes
+    (send_s, send_g, eup_h, edown_h, second_h, dgrad_h, ff_h, sel_h, cot_h, mix_h) = refs[:10]
+    (middle_h, prob_h, hot_h, own_h, att_h, rw_h, wo_h, vec_h) = refs[10:18]
+    (
+        layer_o, middle_o, small_o, flow_o, out_o, down_o, up_o,
+        active_o, hgrad_o, arr_s_o, arr_g_o,
+    ) = refs[18:29]
+    (
+        arr_s, arr_g, eup, edown, second, dgrad, upw, downw, sel, cot, mix,
+        slope, active, hgrad, acc, give, got_s, got_g, ret_s, ret_g, back_s, back_g,
+        low, ugrad, dense, spart, lay, spa, sums, lay_r, spa_r, sums_r,
+        term_give, term_got, ffg, ff_r,
+        middle, prob, hot, own, att, rw, wo, vec, flow_t, flow_1,
+        send_sem, recv_sem, load_sem, out_sem,
+    ) = refs[29:]
+    c = lax.axis_index("dp")
+    i = lax.axis_index("ctx")
+    g, t = lax.div(i, team), lax.rem(i, team)
+    width = second.shape[1]
+    rows = lay.shape[1]
+    hid, ehid = upw.shape[1], eup.shape[1]
+    core = lax.rem(c + 1, two)
+
+    def device(step):
+        dc, dg, dt = step
+        return (
+            lax.rem(c + dc, two),
+            lax.rem(g + dg, groups) * team + lax.rem(t + dt, team),
+        )
+
+    index = [0]
+
+    def remote(src, dst, step):
+        k = index[0]
+        index[0] += 1
+        assert k < copies_count
+        return pltpu.make_async_remote_copy(
+            src_ref=src,
+            dst_ref=dst,
+            send_sem=send_sem.at[k],
+            recv_sem=recv_sem.at[k],
+            device_id=device(step),
+            device_id_type=MESH,
+        )
+
+    group_steps = [(0, k, 0) for k in range(1, groups)]
+    team_steps = [(0, 0, k) for k in range(1, team)]
+    swap = (1, 0, 0)
+    deep = ff_h.shape[2]
+
+    def block_of(core, k):
+        return pl.ds(pl.multiple_of((core * groups + k) * deep, deep), deep)
+
+    loads = []
+    for k, (src, dst) in enumerate(
+        [
+            (second_h, second), (dgrad_h, dgrad), (eup_h, eup), (edown_h, edown), (sel_h, sel), (cot_h, cot), (mix_h, mix),
+            (send_s.at[g], arr_s.at[c, g]), (send_g.at[g], arr_g.at[c, g]),
+            (middle_h, middle), (prob_h, prob), (hot_h, hot), (own_h, own),
+            (att_h, att), (rw_h, rw), (wo_h, wo), (vec_h, vec),
+        ]
+        + [
+            (ff_h.at[k, n], weight.at[block_of(c, k), :])
+            for k in range(groups)
+            for n, weight in enumerate((upw, downw))
+        ]
+    ):
+        load = pltpu.make_async_copy(src, dst, load_sem.at[k])
+        load.start()
+        loads.append(load)
+
+    barrier = pltpu.get_barrier_semaphore()
+    greet = group_steps + team_steps + [swap]
+    for step in greet:
+        pl.semaphore_signal(barrier, inc=1, device_id=device(step), device_id_type=MESH)
+    pl.semaphore_wait(barrier, len(greet))
+
+    every = []
+
+    def launch(copy):
+        copy.start()
+        every.append(copy)
+        return copy
+
+    def to_groups(src, dst):
+        return [
+            launch(remote(src.at[lax.rem(g + s[1], groups)], dst.at[g], s)) for s in group_steps
+        ]
+
+    def source(s):
+        return lax.rem(g + groups - s[1], groups)
+
+    swap_w = [
+        launch(remote(ff_h.at[k, n], weight.at[block_of(c, k), :], swap))
+        for k in range(groups)
+        for n, weight in enumerate((upw, downw))
+    ]
+    out_s = [
+        launch(remote(send_s.at[lax.rem(g + s[1], groups)], arr_s.at[c, g], s))
+        for s in group_steps
+    ]
+    swap_s = [launch(remote(send_s.at[g], arr_s.at[c, g], swap))]
+    out_g = [
+        launch(remote(send_g.at[lax.rem(g + s[1], groups)], arr_g.at[c, g], s))
+        for s in group_steps
+    ]
+    swap_g = [launch(remote(send_g.at[g], arr_g.at[c, g], swap))]
+
+    for load in loads[:2] + loads[17:]:
+        load.wait()
+    for copy in swap_w:
+        copy.wait_recv()
+
+    def dense_in(h, carry):
+        at = span(h, TILE)
+        value, bend = gelu_and_slope(dot_f32(second[...], upw[:, at]))
+        low[:, at] = value.astype(BF)
+        ugrad[:, at] = (bend * contract_cols(dgrad[...], downw[at, :])).astype(BF)
+        return carry
+
+    lax.fori_loop(0, hid // TILE, dense_in, 0)
+
+    def dense_out(n, carry):
+        at = span(n, TILE)
+        dense[:, at] = dot_f32(low[...], downw[:, at])
+        spart[:, at] = contract_cols(ugrad[...], upw[at, :])
+        return carry
+
+    lax.fori_loop(0, width // TILE, dense_out, 0)
+
+    half = hid // 2
+    term_tile = 128
+
+    def down_term(base, n):
+        at = pl.ds(pl.multiple_of(base + n * term_tile, term_tile), term_tile)
+        return contract_rows(low[:, at], dgrad[...])
+
+    def up_term(base, n):
+        at = pl.ds(pl.multiple_of(base + n * term_tile, term_tile), term_tile)
+        return contract_rows(second[:, at], ugrad[...])
+
+    terms = []
+    for k, (term, size) in enumerate(((down_term, half), (up_term, width // 2))):
+
+        def giving(n, carry, k=k, term=term, size=size):
+            term_give[k, span(n, term_tile), :] = term(core * size, n).astype(BF)
+            return carry
+
+        lax.fori_loop(0, size // term_tile, giving, 0)
+        terms.append(launch(remote(term_give.at[k], term_got.at[k], swap)))
+    for k, (term, size) in enumerate(((down_term, half), (up_term, width // 2))):
+        terms[k].wait_recv()
+
+        def keeping(n, carry, k=k, term=term, size=size):
+            at = span(n, term_tile)
+            total = term(c * size, n) + term_got[k, at, :].astype(F32)
+            ffg[k, at, :] = total.astype(BF)
+            return carry
+
+        lax.fori_loop(0, size // term_tile, keeping, 0)
+    up_copy = pltpu.make_async_copy(ffg.at[1], up_o, out_sem.at[4])
+    up_copy.start()
+
+    for load in loads[2:17]:
+        load.wait()
+    for copy, s in zip(out_s, group_steps):
+        copy.wait_recv()
+        swap_s.append(launch(remote(arr_s.at[c, source(s)], arr_s.at[c, source(s)], swap)))
+    for copy in swap_s:
+        copy.wait_recv()
+    entries = 2 * groups * arr_s.shape[2]
+
+    def expert_in(h, carry):
+        at = span(h, TILE)
+        value, bend = gelu_and_slope(dot_f32(arr_s[...].reshape(entries, width), eup[:, at]))
+        active[:, at] = value.astype(BF)
+        slope[:, at] = bend
+        return carry
+
+    lax.fori_loop(0, ehid // TILE, expert_in, 0)
+    keeps = [
+        pltpu.make_async_copy(active, active_o, out_sem.at[0]),
+        pltpu.make_async_copy(arr_s, arr_s_o, out_sem.at[1]),
+    ]
+    for copy in keeps:
+        copy.start()
+
+    def expert_out(n, carry):
+        at = span(n, TILE)
+        acc[:, :, at] = dot_f32(active[...], edown[:, at]).reshape(2, entries // 2, TILE)
+        return carry
+
+    lax.fori_loop(0, width // TILE, expert_out, 0)
+    give[0] = acc[core].astype(BF)
+    other_s = launch(remote(give.at[0], got_s, swap))
+
+    for copy, s in zip(out_g, group_steps):
+        copy.wait_recv()
+        swap_g.append(launch(remote(arr_g.at[c, source(s)], arr_g.at[c, source(s)], swap)))
+    other_s.wait_recv()
+    ret_s[...] = (acc[c] + got_s[...].astype(F32)).astype(BF).reshape(ret_s.shape)
+    home_s = to_groups(ret_s, back_s)
+    back_s[g] = ret_s[g]
+    for copy in swap_g:
+        copy.wait_recv()
+
+    def expert_back(h, carry):
+        at = span(h, TILE)
+        pull = contract_cols(arr_g[...].reshape(entries, width), edown[at, :])
+        hgrad[:, at] = (slope[:, at] * pull).astype(BF)
+        return carry
+
+    lax.fori_loop(0, ehid // TILE, expert_back, 0)
+    keeps += [
+        pltpu.make_async_copy(hgrad, hgrad_o, out_sem.at[2]),
+        pltpu.make_async_copy(arr_g, arr_g_o, out_sem.at[3]),
+    ]
+    for copy in keeps[2:]:
+        copy.start()
+
+    def expert_back_out(n, carry):
+        at = span(n, TILE)
+        acc[:, :, at] = contract_cols(hgrad[...], eup[at, :]).reshape(2, entries // 2, TILE)
+        return carry
+
+    lax.fori_loop(0, width // TILE, expert_back_out, 0)
+    give[1] = acc[core].astype(BF)
+    other_g = launch(remote(give.at[1], got_g, swap))
+    other_g.wait_recv()
+    ret_g[...] = (acc[c] + got_g[...].astype(F32)).astype(BF).reshape(ret_g.shape)
+    home_g = to_groups(ret_g, back_g)
+    back_g[g] = ret_g[g]
+
+    for copy in home_s:
+        copy.wait_recv()
+    slots = groups * back_s.shape[1]
+    lane = lax.broadcasted_iota(jnp.int32, (rows, 128), 1)
+
+    def join_layer(r, carry):
+        at = span(r, rows)
+        found = dot_f32(sel[at, :], back_s[...].reshape(slots, width))
+        own = dense[at, :]
+        flow = cot[at, :].astype(F32)
+        mixes = mix[at, :]
+        lay[r] = (mixes[:, 0:1] * own + mixes[:, 1:2] * found).astype(BF)
+        plain = jnp.sum(flow * own, axis=1, keepdims=True)
+        routed = jnp.sum(flow * found, axis=1, keepdims=True)
+        sums[r] = jnp.where(lane == 0, plain, jnp.where(lane == 1, routed, 0.0))
+        return carry
+
+    lax.fori_loop(0, team, join_layer, 0)
+
+    def to_team(src, dst):
+        made = [launch(remote(src.at[lax.rem(t + s[2], team)], dst.at[t], s)) for s in team_steps]
+        dst[t] = src[t]
+        return made
+
+    team_copies = to_team(lay, lay_r) + to_team(sums, sums_r)
+
+    for copy in home_g:
+        copy.wait_recv()
+    piece = half // groups
+    downs = [
+        launch(remote(ffg.at[0, span(lax.rem(g + s[1], groups), piece), :], ff_r.at[g], s))
+        for s in group_steps
+    ]
+    ff_r[g] = ffg[0, span(g, piece), :]
+
+    def join_grad(r, carry):
+        at = span(r, rows)
+        found = dot_f32(sel[at, :], back_g[...].reshape(slots, width))
+        spa[r] = (spart[at, :] + found).astype(BF)
+        return carry
+
+    lax.fori_loop(0, team, join_grad, 0)
+    team_copies += to_team(spa, spa_r)
+
+    for copy in team_copies:
+        copy.wait_recv()
+
+    sum_own = jnp.sum(sums_r[...], axis=0)
+    layer_o[...] = (middle[...] + jnp.sum(lay_r[...].astype(F32), axis=0)).astype(BF)
+    chances, chosen = prob[...], hot[...]
+    s0, s1 = sum_own[:, 0:1], sum_own[:, 1:2]
+    mix1 = jnp.sum(jnp.where(lane == experts + 1, chances, 0.0), axis=1, keepdims=True)
+    gate = jnp.sum(chances * chosen, axis=1, keepdims=True)
+    pulls = jnp.where(lane == experts, s0, jnp.where(lane == experts + 1, s1 * gate, 0.0))
+    mean_pull = jnp.sum(chances * pulls, axis=1, keepdims=True)
+    logit_grad = chances * jnp.where(
+        lane < experts, (s1 * mix1) * (chosen - gate), pulls - mean_pull
+    )
+    logit_grad = jnp.where(lane < experts + 2, logit_grad, 0.0).astype(BF)
+    second_grad = jnp.sum(spa_r[...].astype(F32), axis=0) + contract_cols(logit_grad, rw[...])
+    hat, scale = normalize(middle[...])
+    pull = second_grad * vec[5:6, :]
+    moved = scale * (
+        pull
+        - jnp.mean(pull, axis=-1, keepdims=True)
+        - hat * jnp.mean(pull * hat, axis=-1, keepdims=True)
+    )
+    middle_grad = cot[span(t, rows), :].astype(F32) + moved
+    middle_o[...] = middle_grad
+    branch = middle_grad.astype(BF)
+
+    for n in range(team):
+        at = slice(n * (width // team), (n + 1) * (width // team))
+        flow_t[n] = contract_cols(wo[at, :], branch).astype(BF).reshape(flow_t.shape[1:])
+    flowed = [
+        launch(remote(flow_t.at[lax.rem(t + s[2], team)], flow_1.at[t], s)) for s in team_steps
+    ]
+    flow_1[t] = flow_t[t]
+
+    def out_term(base, n):
+        at = pl.ds(pl.multiple_of(base + n * term_tile, term_tile), term_tile)
+        return dot_f32(att[at, :], branch)
+
+    def out_giving(n, carry):
+        term_give[0, span(n, term_tile), :] = out_term(core * (width // 2), n).astype(BF)
+        return carry
+
+    terms[0].wait_send()
+    every[:] = [copy for copy in every if copy is not terms[0]]
+    lax.fori_loop(0, width // 2 // term_tile, out_giving, 0)
+    out_cross = launch(remote(term_give.at[0], term_got.at[0], swap))
+    for copy in flowed:
+        copy.wait_recv()
+    flowed = [
+        launch(remote(flow_1.at[:, lax.rem(g + s[1], groups)], flow_o.at[g], s))
+        for s in group_steps
+    ]
+    own_flow = pltpu.make_async_copy(flow_1.at[:, g], flow_o.at[g], out_sem.at[5])
+    own_flow.start()
+    out_cross.wait_recv()
+    wr = out_o.shape[2]
+
+    def out_keeping(n, carry):
+        at = span(n, term_tile)
+        total = out_term(c * (width // 2), n) + term_got[0, at, :].astype(F32)
+        out_o[:, n] = total.astype(BF).reshape(team, wr, width)
+        return carry
+
+    lax.fori_loop(0, groups, out_keeping, 0)
+
+    routed = contract_rows(logit_grad, own[...])[: small_o.shape[0], :]
+    which = lax.broadcasted_iota(jnp.int32, routed.shape, 0)
+    gain = jnp.sum(second_grad * hat, axis=0, keepdims=True)
+    bias = jnp.sum(second_grad, axis=0, keepdims=True)
+    small_o[...] = jnp.where(
+        which == experts + 3, gain, jnp.where(which == experts + 5, bias, routed)
+    )
+    for copy in downs:
+        copy.wait_recv()
+    down_o[...] = jnp.sum(ff_r[...].astype(F32), axis=0)
+    for copy in flowed:
+        copy.wait_recv()
+    for copy in keeps + [up_copy, own_flow]:
+        copy.wait()
+    for copy in every:
+        copy.wait_send()
+
+
+def whole(
+    sizes, rows, experts, wr, send_s, send_g, eup, edown, second, dgrad, ff, sel, cot, mix,
+    middle, prob, hot, own, att, rw, wo, vec,
+):
+    two, groups, team = sizes
+    slots = send_s.shape[1]
+    width = second.shape[1]
+    hid, ehid = ff.shape[3], eup.shape[1]
+    entries = 2 * groups * slots
+    used = -(-(experts + 6) // 8) * 8
+    count = 6 * (groups - 1) + 2 * groups + 5 + 5 * (team - 1) + 2 * groups
+    arrived = (two, groups, slots, width)
+    anywhere = pl.BlockSpec(memory_space=pl.ANY)
+    inside = pl.BlockSpec(memory_space=pltpu.VMEM)
+    team_rows = team * rows
+    heads = (groups, HEAD_DIM, rows)
+    shapes = (
+        ((rows, width), BF),
+        ((rows, width), F32),
+        ((used, width), F32),
+        ((groups, team, HEAD_DIM, rows), BF),
+        ((team, groups, wr, width), BF),
+        ((hid // 2 // groups, width), F32),
+        ((width // 2, hid), BF),
+        ((entries, ehid), BF),
+        ((entries, ehid), BF),
+        (arrived, BF),
+        (arrived, BF),
+    )
+    scratch = (
+        (arrived, BF), (arrived, BF), (eup.shape, BF), (edown.shape, BF), (second.shape, BF),
+        (dgrad.shape, BF), ((width, hid), BF), ((hid, width), BF), (sel.shape, BF),
+        (cot.shape, BF), (mix.shape, F32),
+        ((entries, ehid), F32), ((entries, ehid), BF), ((entries, ehid), BF),
+        ((2, entries // 2, width), F32), ((2, entries // 2, width), BF),
+        ((entries // 2, width), BF), ((entries // 2, width), BF),
+        ((groups, slots, width), BF), ((groups, slots, width), BF),
+        ((groups, slots, width), BF), ((groups, slots, width), BF),
+        ((team_rows, hid), BF), ((team_rows, hid), BF), ((team_rows, width), F32),
+        ((team_rows, width), F32), ((team, rows, width), BF), ((team, rows, width), BF),
+        ((team, rows, 128), F32), ((team, rows, width), BF), ((team, rows, width), BF),
+        ((team, rows, 128), F32),
+        ((2, hid // 2, width), BF), ((2, hid // 2, width), BF), ((2, hid // 2, width), BF),
+        ((groups, hid // 2 // groups, width), BF),
+        (middle.shape, F32), (prob.shape, F32), (hot.shape, F32), (own.shape, BF),
+        (att.shape, BF), (rw.shape, BF), (wo.shape, BF), (vec.shape, F32),
+        ((team,) + heads, BF), ((team,) + heads, BF),
+    )
+    return pl.pallas_call(
+        functools.partial(whole_kernel, sizes, experts, count),
+        name="feed_forward",
+        out_shape=tuple(jax.ShapeDtypeStruct(s, d) for s, d in shapes),
+        in_specs=[anywhere] * 18,
+        out_specs=tuple(inside if n in (0, 1, 2, 4, 5) else anywhere for n in range(11)),
+        scratch_shapes=[pltpu.VMEM(s, d) for s, d in scratch]
+        + [
+            pltpu.SemaphoreType.DMA((count,)),
+            pltpu.SemaphoreType.DMA((count,)),
+            pltpu.SemaphoreType.DMA((17 + 2 * groups,)),
+            pltpu.SemaphoreType.DMA((6,)),
+        ],
+        compiler_params=pltpu.CompilerParams(
+            collective_id=14, has_side_effects=True, vmem_limit_bytes=60 * 2**20
+        ),
+        cost_estimate=pl.CostEstimate(flops=0, bytes_accessed=300_000_000, transcendentals=0),
+    )(
+        send_s, send_g, eup, edown, second, dgrad, ff, sel, cot, mix,
+        middle, prob, hot, own, att, rw, wo, vec,
+    )
+
+
+def deliver_kernel(experts, count, shift, small, *refs):
+    ins, outs = refs[:count], refs[count : 2 * count]
+    router, vectors = refs[2 * count : 2 * count + 2]
+    sem = refs[2 * count + 2]
+    copies = [pltpu.make_async_copy(a, b, sem.at[n]) for n, (a, b) in enumerate(zip(ins, outs))]
+    for copy in copies:
+        copy.start()
+    wr = router.shape[1]
+    mine = pltpu.roll(small[...], lax.rem(128 - shift[0], 128), 1)[:, :wr]
+    router[...] = mine[: experts + 2, :]
+    vectors[...] = mine[experts + 2 : experts + 6, :]
+    for copy in copies:
+        copy.wait()
+
+
+def deliver(experts, shift, small, arrays):
+    wr = arrays[2].shape[0]
+    anywhere = pl.BlockSpec(memory_space=pl.ANY)
+    inside = pl.BlockSpec(memory_space=pltpu.VMEM)
+    count = len(arrays)
+    return pl.pallas_call(
+        functools.partial(deliver_kernel, experts, count),
+        name="deliver",
+        in_specs=[pl.BlockSpec(memory_space=pltpu.SMEM), inside] + [anywhere] * count,
+        out_specs=tuple([anywhere] * count + [inside] * 2),
+        out_shape=tuple(jax.ShapeDtypeStruct(a.shape, a.dtype) for a in arrays)
+        + (
+            jax.ShapeDtypeStruct((experts + 2, wr), F32),
+            jax.ShapeDtypeStruct((4, wr), F32),
+        ),
+        scratch_shapes=[pltpu.SemaphoreType.DMA((count,))],
+        compiler_params=pltpu.CompilerParams(vmem_limit_bytes=60 * 2**20),
+    )(shift, small, *arrays)
 
 
 def per_device(
@@ -2035,7 +2517,8 @@
     length = rows * ctx_count
     wr = w_qkv.shape[0]
     experts = ctx_count * expert_up.shape[0]
-    if groups * team != HEADS or length // block_order.shape[0] != BLOCK or team * wr != 128:
+    fits = groups * team == HEADS and team * wr == 128 and w_up.shape[1] == team * width
+    if not fits or length // block_order.shape[0] != BLOCK:
         return per_device_general(
             tokens, cotangent, block_order, doc_lengths, routes, w_qkv, w_out, w_up, w_down,
             router, norm_gains, norm_biases, expert_up, expert_down,
@@ -2054,25 +2537,6 @@
     team_steps = [(0, 0, k) for k in range(1, team)]
 
     router_cols = router.shape[1]
-    small = jnp.concatenate(
-        [router, jnp.zeros((wr, 124 - router_cols), F32), norm_gains.T, norm_biases.T], axis=1
-    )
-    own = jnp.concatenate(
-        [
-            w_qkv.reshape(wr, 3, team, width // team)
-            .transpose(2, 0, 1, 3)
-            .reshape(team, wr, qkv_cols),
-            jnp.broadcast_to(small[None], (team, wr, 128)),
-        ],
-        axis=2,
-    ).astype(BF)
-    up_first = (
-        w_up.reshape(wr, two * groups, team, hidden_dev)
-        .transpose(2, 0, 1, 3)
-        .reshape(team, wr, up_cols)
-        .astype(BF)
-    )
-    route_row = jnp.broadcast_to(routes[0, :, 0][None, :], (8, rows))
     (
         token_rows,
         cot_rows,
@@ -2087,11 +2551,14 @@
         sizes,
         tokens[0],
         cotangent[0],
-        own,
-        up_first,
-        w_down.astype(BF).reshape(team, wr, width),
-        w_out.astype(BF),
-        route_row,
+        w_qkv,
+        w_up,
+        w_down,
+        w_out,
+        router.T,
+        norm_gains,
+        norm_biases,
+        routes[0].reshape(1, rows),
     )
     router_weight = weights[:, :, :, :, qkv_cols:].reshape(width, 128)
     out_weight = out_weight.reshape(width, width)
@@ -2105,11 +2572,8 @@
         tiled=False,
         axis_index_groups=by_group,
     )
-    bounds, inverse, meta = where_rows(
-        block_order, doc_lengths, jnp.arange(length, dtype=jnp.int32), BLOCK
-    )
     low_t, attention_t, log_total, q_pad, kv_t, kv_rows = sorted_attend(
-        bounds, inverse, block_order, meta, head_parts.reshape(groups, 3 * HEAD_DIM, group_rows)
+        doc_lengths[0], block_order, head_parts.reshape(groups, 3 * HEAD_DIM, group_rows)
     )
 
     def gather_heads(coords, ins, outs):
@@ -2159,17 +2623,22 @@
         cot_rows,
     )
     (
-        layer_sum,
-        second_sum,
-        sums_own,
+        layer_out,
+        middle_grad,
+        small_t,
+        flow_parts,
+        out_half,
+        down_sum,
+        up_half,
         expert_active,
         hidden_grad,
         arrived_in,
         arrived_grad,
-        ff_terms,
-    ) = feed_forward(
+    ) = whole(
         sizes,
         rows,
+        experts,
+        wr,
         send_s,
         send_g,
         expert_up[0],
@@ -2180,57 +2649,44 @@
         select,
         cot_rows,
         mixes,
-    )
-    ff_sum = lax.psum_scatter(
-        ff_terms, "ctx", scatter_dimension=0, tiled=True, axis_index_groups=by_group
-    )
-    down_sum = ff_sum[:, :width].astype(F32)
-    up_sum = ff_sum[:, width:].reshape(team, wr, up_cols)
-
-    layer_out, middle_grad, flow_t, out_term, small_t = turn(
-        experts,
-        layer_sum,
-        second_sum,
-        sums_own,
         middle_own,
         prob_own,
         hot_own,
         second_own,
         attended_own,
-        cotangent[0],
         router_weight,
         out_weight,
         vectors,
     )
-    flow_t = flow_t.reshape(team, groups, HEAD_DIM, rows)
-    out_halves = out_term.reshape(two, groups, team, wr, width)
-
-    def spread_flow(coords, ins, outs):
-        c, g, t = coords
-        moves = []
-        for dg in range(groups):
-            for dt in range(team):
-                if dg or dt:
-                    to_g, to_t = lax.rem(g + dg, groups), lax.rem(t + dt, team)
-                    moves.append(Move((0, dg, dt), ins[0].at[to_t, to_g], outs[0].at[g, t]))
-        moves.append(Move((1, 0, 0), ins[1].at[lax.rem(c + 1, two)], outs[1]))
-        return [(ins[0].at[t, g], outs[0].at[g, t])], moves
-
-    flow_parts, out_got = exchange(
-        "flow",
-        8,
-        sizes,
-        (flow_t, out_halves),
-        [((groups, team, HEAD_DIM, rows), BF), (out_halves.shape[1:], BF)],
-        spread_flow,
-    )
-    out_keep = lax.dynamic_index_in_dim(out_halves, core, 0, keepdims=False)
-    out_parts = (out_keep.astype(F32) + out_got.astype(F32)).astype(BF).transpose(1, 0, 2, 3)
+
+    def pieces_of(array, along):
+        count = groups if along == "g" else team
+        me = group if along == "g" else member
+        found = [lax.dynamic_index_in_dim(array, me, 0, keepdims=False)]
+        for step in range(1, count):
+            if along == "g":
+                pairs = [
+                    (g * team + t, (g + step) % groups * team + t)
+                    for g in range(groups)
+                    for t in range(team)
+                ]
+            else:
+                pairs = [
+                    (g * team + t, g * team + (t + step) % team)
+                    for g in range(groups)
+                    for t in range(team)
+                ]
+            chunk = lax.dynamic_index_in_dim(array, lax.rem(me + step, count), 0, keepdims=False)
+            found.append(lax.ppermute(chunk, "ctx", pairs))
+        return found
+
+    up_sum = lax.psum_scatter(
+        up_half, "ctx", scatter_dimension=0, tiled=True, axis_index_groups=by_group
+    ).reshape(team, wr, up_cols)
+    out_pieces = pieces_of(out_half, "t")
     grad_parts = sorted_back(
-        bounds,
-        inverse,
+        doc_lengths[0],
         block_order,
-        meta,
         flow_parts.reshape(ctx_count, HEAD_DIM, rows),
         attention_t,
         log_total,
@@ -2240,25 +2696,12 @@
         groups,
     )
 
-    def moved(array, axis, step, base, count, pairs):
-        chunk = lax.dynamic_index_in_dim(
-            array, lax.rem(base + step, count), axis, keepdims=False
-        )
-        return lax.ppermute(chunk, "ctx", pairs)
-
-    group_pairs = [
-        [(g * team + t, (g + k) % groups * team + t) for g in range(groups) for t in range(team)]
-        for k in range(groups)
-    ]
-    team_pairs = [
-        [(g * team + t, g * team + (t + k) % team) for g in range(groups) for t in range(team)]
-        for k in range(team)
-    ]
-    pieces = [lax.dynamic_index_in_dim(grad_parts, group, 0, keepdims=False)]
-    pieces += [moved(grad_parts, 0, k, group, groups, group_pairs[k]) for k in range(1, groups)]
-    out_sum = lax.dynamic_index_in_dim(out_parts, member, 0, keepdims=False).astype(F32)
-    for k in range(1, team):
-        out_sum = out_sum + moved(out_parts, 0, k, member, team, team_pairs[k]).astype(F32)
+    grad_parts, expert_active, hidden_grad = lax.optimization_barrier(
+        (grad_parts, expert_active, hidden_grad)
+    )
+
+    pieces = pieces_of(grad_parts, "g")
+    out_sum = sum(piece.astype(F32) for piece in out_pieces).astype(BF)
     entries = two * groups * slots
     expert_down_grad = row_sum(expert_active, arrived_grad.reshape(entries, width), TILE)
     expert_up_grad = row_sum(arrived_in.reshape(entries, width), hidden_grad, 128)
@@ -2273,21 +2716,15 @@
         middle_grad,
         small_t,
         up_sum,
-        out_sum.astype(BF),
-    )
-    up_own = (
-        up_own.reshape(team, wr, two * groups, hidden_dev)
-        .transpose(1, 2, 0, 3)
-        .reshape(wr, hidden)
-        .astype(F32)
-    )
-    qkv_own = (
-        qkv_own.reshape(team, wr, 3, width // team)
-        .transpose(1, 2, 0, 3)
-        .reshape(wr, 3 * width)
-        .astype(F32)
-    )
-    small_sum = lax.dynamic_slice_in_dim(jnp.sum(small_own, axis=0), member * wr, wr, axis=1)
+        out_sum,
+    )
+    delivered = deliver(
+        experts,
+        member[None] * wr,
+        small_own,
+        (layer_out, input_grad, qkv_own, out_own, up_own, down_sum),
+    )
+    layer_out, input_grad, qkv_own, out_own, up_own, down_sum, router_own, vectors_own = delivered
     return (
         layer_out[None],
         input_grad[None],
@@ -2295,9 +2732,9 @@
         out_own,
         up_own,
         down_sum,
-        small_sum[:router_cols].T,
-        small_sum[router_cols : router_cols + 2],
-        small_sum[router_cols + 2 : router_cols + 4],
+        router_own.T,
+        vectors_own[:2],
+        vectors_own[2:],
         expert_up_grad,
         expert_down_grad,
     )

time: 351 us -> 356 us (1.014)
  Pallas kernels: 264 us -> 317 us
  local copies, waits for them, and re-layouts: 52.4 us -> 5.48 us
  waiting for transfers between devices: 3.8 us -> 8.75 us
    pallas_call x2, Pallas kernels: 76.8 us -> 151 us  [the longest x1 85.5 us: whole(): pl.pallas_call(functools.partial(whole_kernel, sizes, experts, count), na...]
    unnamed x144 -> x32, local copies, waits for them, and re-layouts: 42.9 us -> 1.67 us
    pallas_call x2 -> x1, Pallas kernels: 50.5 us -> 27.7 us  [exchange(): pl.pallas_call(kernel, name=name, out_shape=tuple((jax.ShapeDtypeStruct(s...]
    convert_element_type x9 -> x0, local copies, waits for them, and re-layouts: 4.79 us -> none  [the longest x3 2.38 us: per_device(): qkv_own = qkv_own.reshape(team, wr, 3, width // team).transpose(1, 2, 0,...]
    pallas_call x1, Pallas kernels: 38.7 us -> 34.4 us  [end(): pl.pallas_call(functools.partial(end_kernel, sizes, experts), name='end',...]
  transfers between devices with their start and end apart: 8 -> 8, of which waited for: 1 -> 3; matrix products, arithmetic and copies ran while one was open for 1% -> 1% of each run, Pallas kernels for 29% -> 23%
where the time goes in v2:
time: 356 us; the launch traced here: 355 us
  Pallas kernels  317 us (89%)
  between operations  14.3 us (4%)
  waiting for transfers between devices  8.75 us (2%)
  starting transfers between devices  8.64 us (2%)
  local copies, waits for them, and re-layouts  5.48 us (2%)
    pallas_call x1, Pallas kernels, whole(): pl.pallas_call(functools.partial(whole_kernel, sizes, experts, count), na...  85.5 us
    pallas_call x1, Pallas kernels, deliver(): pl.pallas_call(functools.partial(deliver_kernel, experts, count), name='d...  66 us
    pallas_call x1, Pallas kernels, start(): pl.pallas_call(functools.partial(start_kernel, sizes), name='start', out_...  51 us
    pallas_call x1, Pallas kernels, end(): pl.pallas_call(functools.partial(end_kernel, sizes, experts), name='end',...  34.4 us
    pallas_call x1, Pallas kernels, exchange(): pl.pallas_call(kernel, name=name, out_shape=tuple((jax.ShapeDtypeStruct(s...  27.7 us
    pallas_call x1, Pallas kernels, sorted_attend(): pl.pallas_call(sorted_attend_kernel, name='attend', grid=(length // TILE,...  16.1 us
    pallas_call x1, Pallas kernels, sorted_back(): pl.pallas_call(sorted_back_kernel, name='attend_back', grid=(length // TI...  14.1 us
    pallas_call x2, Pallas kernels, row_sum(): pl.pallas_call(row_sum_kernel, name='row_sum', grid=(high // tile,), in_s...  12.8 us
  transfers between devices with their start and end apart: 8, of which 3 were waited for; matrix products, arithmetic and copies ran while one was open for 1% of the time, Pallas kernels for 23%

profile of v2, /device:TPU:0, one launch (start us, length us, event | category | flops | bytes accessed | tf_op | source)
XLA Modules:
  0.0 355.3 jit_solution(11494042111440123398)
XLA Ops:
  7.2 51.0 %start.1 = (bf16[4,128,1024]{2,1,0:T(8,128)(2,1)}, bf16[4,128,1024]{2,1,0:T(8,128)(2,1)}, bf16[4,3,64,512]{3,2,1,0:T(8,128)(2,1)}, bf16[4,128,1024]{2,1,0:T(8,12...) custom-call(bf16[128,1024]{1,0:T(8,128)(2,1)} %bitcast.54, ...), custom_call_target="tpu_custom_call" | custom-call | bytes 150000000 | tf_op jit(solution)/shard_map/start/pallas_call | solution.py:904
  58.5 16.1 %attend.1 = (bf16[4,64,512]{2,1,0:T(8,128)(2,1)}, f32[64,2048]{1,0:T(8,128)}, f32[1,2048]{1,0:T(1,128)}, bf16[128,2048]{1,0:T(8,128)(2,1)}, bf16[128,2048]{1,0:T(8,128)(2,1)}, /*index=5*/bf16[2048,128]{1,0:T(8,128)(2,1)}) custom-call(s32[8]{0:T(128)} %bitcast.42, s32[32]{0:T(128)} %order.3, bf16[4,192,512]{2,1,0:T(8,128)(2,1)} %bitcast.56), custom_call_target="tpu_custom_call" | custom-call | bytes 42000000 | tf_op jit(solution)/shard_map/attend/pallas_call | solution.py:477
  74.6 27.7 %attended.1 = bf16[4,4,64,512]{3,2,1,0:T(8,128)(2,1)} custom-call(bf16[4,64,512]{2,1,0:T(8,128)(2,1)} %get-tuple-element.65.refs_0_), custom_call_target="tpu_custom_call" | custom-call | bytes 60000000 | tf_op jit(solution)/shard_map/attended/pallas_call | solution.py:138
  102.3 1.7 slice.9
  103.9 9.6 %between.1 = (bf16[512,1024]{1,0:T(8,128)(2,1)}, bf16[512,1024]{1,0:T(8,128)(2,1)}, bf16[4,64,1024]{2,1,0:T(8,128)(2,1)}, bf16[4,64,1024]{2,1,0:T(8,128)(2,1)}, ...) custom-call(s32[1]{0:T(128)} %bitcast.member, ...), custom_call_target="tpu_custom_call" | custom-call | tf_op jit(solution)/shard_map/between/pallas_call | solution.py:605
  113.5 3.2 all-gather.2.cloned.1.call-done.refs_6_
  116.8 85.5 %feed_forward.1 = (bf16[128,1024]{1,0:T(8,128)(2,1)}, f32[128,1024]{1,0:T(8,128)}, f32[24,1024]{1,0:T(8,128)}, bf16[4,4,64,128]{3,2,1,0:T(8,128)(2,1)}, bf16[4,4...) custom-call(bf16[4,64,1024]{2,1,0:T(8,128)(2,1)} %get-tuple-element., ...), custom_call_target="tpu_custom_call" | custom-call | bytes 300000000 | tf_op jit(solution)/shard_map/feed_forward/pallas_call | solution.py:2437
  202.5 0.9 copy-done.8
  203.4 14.1 %attend_back.1 = bf16[4,3,64,512]{3,2,1,0:T(8,128)(2,1)S(1)} custom-call(s32[8]{0:T(128)S(1)} %bitcast.43, s32[32]{0:T(128)S(1)} %copy-done.11, bf16[16,64,128]{2,1,0:T(8,128)(2,1)S(1)} %bitcast.41, f32[64,2048]{1,0:T(8,128)S(1)} %copy-done.4, f32[1,2048]{1,0:T(1,128)S(1)} %copy-done.9, bf16[128,2048]{1,0:T(8,128)(2,1)S(1)} %copy-done.5, ...), custom_call_target="tpu_custom_call" | custom-call | bytes 42000000 | tf_op jit(solution)/shard_map/attend_back/pallas_call | solution.py:495
  217.5 0.8 dynamic-slice_bitcast_fusion.3
  218.3 1.3 collective-permute-start
  219.6 3.3 collective-permute-start.1
  222.9 2.0 collective-permute-start.5
  224.9 0.9 collective-permute-start.4
  226.0 6.4 %row_sum.2 = f32[1,1024,2048]{2,1,0:T(8,128)} custom-call(bf16[512,1024]{1,0:T(8,128)(2,1)S(1)} %bitcast.40, bf16[512,2048]{1,0:T(8,128)(2,1)S(1)} %copy-done.1), custom_call_target="tpu_custom_call" | custom-call | flops 2147483648 | bytes 8388608 | tf_op jit(solution)/shard_map/row_sum/pallas_call | solution.py:692
  232.5 6.4 %row_sum.3 = f32[1,2048,1024]{2,1,0:T(8,128)} custom-call(bf16[512,2048]{1,0:T(8,128)(2,1)S(1)} %copy-done, bf16[512,1024]{1,0:T(8,128)(2,1)S(1)} %bitcast.39), custom_call_target="tpu_custom_call" | custom-call | flops 2147483648 | bytes 8388608 | tf_op jit(solution)/shard_map/row_sum/pallas_call | solution.py:692
  238.9 0.8 collective-permute-start.2
  239.6 0.9 fusion.2.refs_11_
  240.5 1.5 collective-permute-done.1.refs_2_
  242.0 4.0 %collective-permute-done.2.refs_3_ = bf16[3,64,512]{2,1,0:T(8,128)(2,1)S(1)} collective-permute-done((bf16[3,64,512]{2,1,0:T(8,128)(2,1)S(1)}, bf16[3,64,512]{2,1,0:T(8,128)(2,1)S(1)}, u32[]{:S(2)}, u32[]{:S(2)}) %collective-permute-start.2) | collective-permute-done | bytes 196640 | tf_op jit(solution)/shard_map/ppermute | solution.py:2680
  246.0 0.7 copy-done.15
  246.7 34.4 %end.1 = (bf16[128,1024]{1,0:T(8,128)(2,1)}, f32[32,3072]{1,0:T(8,128)}, f32[32,4096]{1,0:T(8,128)}, f32[32,1024]{1,0:T(8,128)}, f32[24,128]{1,0:T(8,128)}) custom-call(bf16[3,64,512]{2,1,0:T(8,128)(2,1)} %get-tuple-element.123.refs_0_, bf16[3,64,512]{2,1,0:T(8,128)(2,1)} %copy-done.13, bf16[3,64,512]{2,1,0:T(8,128)(2,1)} %copy-done.14, ...), custom_call_target="tpu_custom_call" | custom-call | bytes 120000000 | tf_op jit(solution)/shard_map/end/pallas_call | solution.py:1074
  281.1 66.0 %deliver.1 = (bf16[128,1024]{1,0:T(8,128)(2,1)}, bf16[128,1024]{1,0:T(8,128)(2,1)}, f32[32,3072]{1,0:T(8,128)}, f32[32,1024]{1,0:T(8,128)}, f32[32,4096]{1,0:T(8...) custom-call(s32[1]{0:T(128)S(6)} %mul.3.shift, f32[24,128]{1,0:T(8,128)} %get-tuple-element.98.small, ...), custom_call_target="tpu_custom_call" | custom-call | tf_op jit(solution)/shard_map/deliver/pallas_call | solution.py:2480
  347.1 1.3 fusion.3
  (41 shorter events, 0.6 us)
Async XLA Ops:
  7.2 109.6 %all-gather.2.cloned.1.call-start = ((), (), s32[]{:S(2)}) async-start(), calls=%async_computation.1 | async-start | bytes 2621440 | tf_op jit(solution)/shard_map/all_gather | solution.py:2568
  58.3 187.7 %reduce-scatter.2.cloned.1.call-start = ((), (), s32[]{:S(2)}) async-start(), calls=%async_computation.2 | async-start | bytes 1310720 | tf_op jit(solution)/shard_map/reduce_scatter | solution.py:2683
  116.8 85.6 %copy-start.4 = (f32[64,2048]{1,0:T(8,128)S(1)}, f32[64,2048]{1,0:T(8,128)}, u32[]{:S(2)}) copy-start(f32[64,2048]{1,0:T(8,128)} %get-tuple-element.85.out_ref) | copy-start | bytes 1572868
  116.8 85.6 %copy-start.5 = (bf16[128,2048]{1,0:T(8,128)(2,1)S(1)}, bf16[128,2048]{1,0:T(8,128)(2,1)}, u32[]{:S(2)}) copy-start(bf16[128,2048]{1,0:T(8,128)(2,1)} %get-tuple-element.87.q_ref) | copy-start | bytes 1572868
  116.8 85.6 %copy-start.6 = (bf16[128,2048]{1,0:T(8,128)(2,1)S(1)}, bf16[128,2048]{1,0:T(8,128)(2,1)}, u32[]{:S(2)}) copy-start(bf16[128,2048]{1,0:T(8,128)(2,1)} %get-tuple-element.88.kvt_ref) | copy-start | bytes 1572868
  116.8 85.6 %copy-start.7 = (bf16[2048,128]{1,0:T(8,128)(2,1)S(1)}, bf16[2048,128]{1,0:T(8,128)(2,1)}, u32[]{:S(2)}) copy-start(bf16[2048,128]{1,0:T(8,128)(2,1)} %get-tuple-element.89.rows_ref) | copy-start | bytes 1572868
  116.8 85.7 %copy-start.9 = (f32[1,2048]{1,0:T(1,128)S(1)}, f32[1,2048]{1,0:T(1,128)}, u32[]{:S(2)}) copy-start(f32[1,2048]{1,0:T(1,128)} %get-tuple-element.86.lse_ref) | copy-start | bytes 24580
  116.8 85.7 %copy-start.10 = (s32[1,8]{1,0:T(1,128)S(1)}, s32[1,8]{1,0:T(1,128)}, u32[]{:S(2)}) copy-start(s32[1,8]{1,0:T(1,128)} %param.17) | copy-start | bytes 100
  116.8 85.7 %copy-start.11 = (s32[32]{0:T(128)S(1)}, s32[32]{0:T(128)}, u32[]{:S(2)}) copy-start(s32[32]{0:T(128)} %order.3) | copy-start | bytes 388
  202.4 1.0 copy-start.8
  203.4 19.5 %copy-start.12 = (bf16[4,4,32,1024]{3,2,1,0:T(8,128)(2,1)S(1)}, bf16[4,4,32,1024]{3,2,1,0:T(8,128)(2,1)}, u32[]{:S(2)}) copy-start(bf16[4,4,32,1024]{3,2,1,0:T(8,128)(2,1)} %get-tuple-element.97) | copy-start | bytes 3145732
  217.5 8.5 %copy-start.1 = (bf16[512,2048]{1,0:T(8,128)(2,1)S(1)}, bf16[512,2048]{1,0:T(8,128)(2,1)}, u32[]{:S(2)}) copy-start(bf16[512,2048]{1,0:T(8,128)(2,1)} %get-tuple-element.114.right) | copy-start | bytes 6291460
  217.5 8.5 %copy-start.3 = (bf16[2,4,64,1024]{3,2,1,0:T(8,128)(2,1)S(1)}, bf16[2,4,64,1024]{3,2,1,0:T(8,128)(2,1)}, u32[]{:S(2)}) copy-start(bf16[2,4,64,1024]{3,2,1,0:T(8,128)(2,1)} %get-tuple-element.113) | copy-start | bytes 3145732
  218.3 22.2 %collective-permute-start = (bf16[3,64,512]{2,1,0:T(8,128)(2,1)S(1)}, bf16[3,64,512]{2,1,0:T(8,128)(2,1)S(1)}, u32[]{:S(2)}, u32[]{:S(2)}) collective-permute-start(bf16[3,64,512]{2,1,0:T(8,128)(2,1)S(1)} %get-tuple-element.122), channel_id=1, source_target_pairs={{0,4},{1,5},{2,6},{3,7},{4,8},{5,9},{6,10},{7,11},{8,12},{9,13},{1... | collective-permute-start | bytes 589832 | tf_op jit(solution)/shard_map/ppermute | solution.py:2680
  219.6 22.4 %collective-permute-start.1 = (bf16[3,64,512]{2,1,0:T(8,128)(2,1)S(1)}, bf16[3,64,512]{2,1,0:T(8,128)(2,1)S(1)}, u32[]{:S(2)}, u32[]{:S(2)}) collective-permute-start(bf16[3,64,512]{2,1,0:T(8,128)(2,1)S(1)} %get-tuple-element.121), channel_id=1, source_target_pairs={{0,8},{1,9},{2,10},{3,11},{4,12},{5,13},{6,14},{7,15},{8,0},{9,1},... | collective-permute-start | bytes 589832 | tf_op jit(solution)/shard_map/ppermute | solution.py:2680
  222.9 15.9 %collective-permute-start.5 = (bf16[4,32,1024]{2,1,0:T(8,128)(2,1)S(1)}, bf16[4,32,1024]{2,1,0:T(8,128)(2,1)S(1)}, u32[]{:S(2)}, u32[]{:S(2)}) collective-permute-start(bf16[4,32,1024]{2,1,0:T(8,128)(2,1)S(1)} %get-tuple-element.118), channel_id=1, source_target_pairs={{0,3},{1,0},{2,1},{3,2},{4,7},{5,4},{6,5},{7,6},{8,11},{9,8},{10,9... | collective-permute-start | bytes 786440 | tf_op jit(solution)/shard_map/ppermute | solution.py:2680
  224.9 14.7 %collective-permute-start.4 = (bf16[4,32,1024]{2,1,0:T(8,128)(2,1)S(1)}, bf16[4,32,1024]{2,1,0:T(8,128)(2,1)S(1)}, u32[]{:S(2)}, u32[]{:S(2)}) collective-permute-start(bf16[4,32,1024]{2,1,0:T(8,128)(2,1)S(1)} %get-tuple-element.119), channel_id=1, source_target_pairs={{0,2},{1,3},{2,0},{3,1},{4,6},{5,7},{6,4},{7,5},{8,10},{9,11},{10,... | collective-permute-start | bytes 786440 | tf_op jit(solution)/shard_map/ppermute | solution.py:2680
  225.8 13.8 %collective-permute-start.3 = (bf16[4,32,1024]{2,1,0:T(8,128)(2,1)S(1)}, bf16[4,32,1024]{2,1,0:T(8,128)(2,1)S(1)}, u32[]{:S(2)}, u32[]{:S(2)}) collective-permute-start(bf16[4,32,1024]{2,1,0:T(8,128)(2,1)S(1)} %get-tuple-element.117), channel_id=1, source_target_pairs={{0,1},{1,2},{2,3},{3,0},{4,5},{5,6},{6,7},{7,4},{8,9},{9,10},{10,1... | collective-permute-start | bytes 786440 | tf_op jit(solution)/shard_map/ppermute | solution.py:2680
  226.0 6.5 %copy-start = (bf16[512,2048]{1,0:T(8,128)(2,1)S(1)}, bf16[512,2048]{1,0:T(8,128)(2,1)}, u32[]{:S(2)}) copy-start(bf16[512,2048]{1,0:T(8,128)(2,1)} %get-tuple-element.115.left) | copy-start | bytes 6291460
  226.0 6.5 %copy-start.2 = (bf16[2,4,64,1024]{3,2,1,0:T(8,128)(2,1)S(1)}, bf16[2,4,64,1024]{3,2,1,0:T(8,128)(2,1)}, u32[]{:S(2)}) copy-start(bf16[2,4,64,1024]{3,2,1,0:T(8,128)(2,1)} %get-tuple-element.116) | copy-start | bytes 3145732
  238.9 7.1 %collective-permute-start.2 = (bf16[3,64,512]{2,1,0:T(8,128)(2,1)S(1)}, bf16[3,64,512]{2,1,0:T(8,128)(2,1)S(1)}, u32[]{:S(2)}, u32[]{:S(2)}) collective-permute-start(bf16[3,64,512]{2,1,0:T(8,128)(2,1)S(1)} %get-tuple-element.120), channel_id=1, source_target_pairs={{0,12},{1,13},{2,14},{3,15},{4,0},{5,1},{6,2},{7,3},{8,4},{9,5},{1... | collective-permute-start | bytes 589832 | tf_op jit(solution)/shard_map/ppermute | solution.py:2680
  240.5 5.5 %copy-start.13 = (bf16[3,64,512]{2,1,0:T(8,128)(2,1)}, bf16[3,64,512]{2,1,0:T(8,128)(2,1)S(1)}, u32[]{:S(2)}) copy-start(bf16[3,64,512]{2,1,0:T(8,128)(2,1)S(1)} %collective-permute-done.refs_1_) | copy-start | bytes 589828
  242.0 4.0 %copy-start.14 = (bf16[3,64,512]{2,1,0:T(8,128)(2,1)}, bf16[3,64,512]{2,1,0:T(8,128)(2,1)S(1)}, u32[]{:S(2)}) copy-start(bf16[3,64,512]{2,1,0:T(8,128)(2,1)S(1)} %collective-permute-done.1.refs_2_) | copy-start | bytes 589828
  246.0 0.7 copy-start.15
Sparse Core Ops, SparseCore 0:
  58.4 58.3 all-gather.1
  202.4 34.8 reduce-scatter.1

commit v3 on v2

--- a/solution.py
+++ b/solution.py
@@ -2480,7 +2480,7 @@
     return pl.pallas_call(
         functools.partial(deliver_kernel, experts, count),
         name="deliver",
-        in_specs=[pl.BlockSpec(memory_space=pltpu.SMEM), inside] + [anywhere] * count,
+        in_specs=[pl.BlockSpec(memory_space=pltpu.SMEM)] + [inside] * (count + 1),
         out_specs=tuple([anywhere] * count + [inside] * 2),
         out_shape=tuple(jax.ShapeDtypeStruct(a.shape, a.dtype) for a in arrays)
         + (

time: 356 us -> 294 us (0.83)
  Pallas kernels: 317 us -> 259 us
    pallas_call x1, Pallas kernels: 66 us -> 3.51 us  [deliver(): pl.pallas_call(functools.partial(deliver_kernel, experts, count), name='d...]
    pallas_call x1, Pallas kernels: 85.5 us -> 89.2 us  [whole(): pl.pallas_call(functools.partial(whole_kernel, sizes, experts, count), na...]
  transfers between devices with their start and end apart: 8 -> 8, of which waited for: 3 -> 2; matrix products, arithmetic and copies ran while one was open for 1% -> 1% of each run, Pallas kernels for 23% -> 27%
where the time goes in v3:
time: 294 us
  Pallas kernels  259 us (88%)
  between operations  14.3 us (5%)
  starting transfers between devices  7.99 us (3%)
  waiting for transfers between devices  6.75 us (2%)
  local copies, waits for them, and re-layouts  5.48 us (2%)
    pallas_call x1, Pallas kernels, whole(): pl.pallas_call(functools.partial(whole_kernel, sizes, experts, count), na...  89.2 us
    pallas_call x1, Pallas kernels, start(): pl.pallas_call(functools.partial(start_kernel, sizes), name='start', out_...  51 us
    pallas_call x1, Pallas kernels, end(): pl.pallas_call(functools.partial(end_kernel, sizes, experts), name='end',...  36 us
    pallas_call x1, Pallas kernels, exchange(): pl.pallas_call(kernel, name=name, out_shape=tuple((jax.ShapeDtypeStruct(s...  26.4 us
    pallas_call x1, Pallas kernels, sorted_attend(): pl.pallas_call(sorted_attend_kernel, name='attend', grid=(length // TILE,...  16.1 us
    pallas_call x1, Pallas kernels, sorted_back(): pl.pallas_call(sorted_back_kernel, name='attend_back', grid=(length // TI...  14.1 us
    pallas_call x2, Pallas kernels, row_sum(): pl.pallas_call(row_sum_kernel, name='row_sum', grid=(high // tile,), in_s...  12.8 us
    pallas_call x1, Pallas kernels, between(): pl.pallas_call(functools.partial(mid_kernel, experts, team), name='betwee...  9.56 us
  transfers between devices with their start and end apart: 8, of which 2 were waited for; matrix products, arithmetic and copies ran while one was open for 1% of the time, Pallas kernels for 27%

profile of v3, /device:TPU:0, one launch (start us, length us, event | category | flops | bytes accessed | tf_op | source)
XLA Modules:
  0.0 294.1 jit_solution(408784907996898985)
XLA Ops:
  7.2 51.0 %start.1 = (bf16[4,128,1024]{2,1,0:T(8,128)(2,1)}, bf16[4,128,1024]{2,1,0:T(8,128)(2,1)}, bf16[4,3,64,512]{3,2,1,0:T(8,128)(2,1)}, bf16[4,128,1024]{2,1,0:T(8,12...) custom-call(bf16[128,1024]{1,0:T(8,128)(2,1)} %bitcast.54, ...), custom_call_target="tpu_custom_call" | custom-call | bytes 150000000 | tf_op jit(solution)/shard_map/start/pallas_call | solution.py:904
  58.5 16.1 %attend.1 = (bf16[4,64,512]{2,1,0:T(8,128)(2,1)}, f32[64,2048]{1,0:T(8,128)}, f32[1,2048]{1,0:T(1,128)}, bf16[128,2048]{1,0:T(8,128)(2,1)}, bf16[128,2048]{1,0:T(8,128)(2,1)}, /*index=5*/bf16[2048,128]{1,0:T(8,128)(2,1)}) custom-call(s32[8]{0:T(128)} %bitcast.42, s32[32]{0:T(128)} %order.3, bf16[4,192,512]{2,1,0:T(8,128)(2,1)} %bitcast.56), custom_call_target="tpu_custom_call" | custom-call | bytes 42000000 | tf_op jit(solution)/shard_map/attend/pallas_call | solution.py:477
  74.6 26.4 %attended.1 = bf16[4,4,64,512]{3,2,1,0:T(8,128)(2,1)} custom-call(bf16[4,64,512]{2,1,0:T(8,128)(2,1)} %get-tuple-element.65.refs_0_), custom_call_target="tpu_custom_call" | custom-call | bytes 60000000 | tf_op jit(solution)/shard_map/attended/pallas_call | solution.py:138
  101.0 1.7 slice.9
  102.7 9.6 %between.1 = (bf16[512,1024]{1,0:T(8,128)(2,1)}, bf16[512,1024]{1,0:T(8,128)(2,1)}, bf16[4,64,1024]{2,1,0:T(8,128)(2,1)}, bf16[4,64,1024]{2,1,0:T(8,128)(2,1)}, ...) custom-call(s32[1]{0:T(128)} %bitcast.member, ...), custom_call_target="tpu_custom_call" | custom-call | tf_op jit(solution)/shard_map/between/pallas_call | solution.py:605
  112.2 4.4 %all-gather.2.cloned.1.call-done.refs_6_ = bf16[4,2,128,1024]{3,2,1,0:T(8,128)(2,1)} async-done(((bf16[1,2,128,1024]{3,2,1,0:T(8,128)(2,1)}), bf16[4,2,128,1024]{3,2,1,0:T(8,128)(2,1)}) %all-gather.2.cloned.1.call-update) | async-done | bytes 2097168 | tf_op jit(solution)/shard_map/all_gather | solution.py:2568
  116.7 89.2 %feed_forward.1 = (bf16[128,1024]{1,0:T(8,128)(2,1)}, f32[128,1024]{1,0:T(8,128)}, f32[24,1024]{1,0:T(8,128)}, bf16[4,4,64,128]{3,2,1,0:T(8,128)(2,1)}, bf16[4,4...) custom-call(bf16[4,64,1024]{2,1,0:T(8,128)(2,1)} %get-tuple-element., ...), custom_call_target="tpu_custom_call" | custom-call | bytes 300000000 | tf_op jit(solution)/shard_map/feed_forward/pallas_call | solution.py:2437
  206.1 0.9 copy-done.8
  207.0 14.1 %attend_back.1 = bf16[4,3,64,512]{3,2,1,0:T(8,128)(2,1)S(1)} custom-call(s32[8]{0:T(128)S(1)} %bitcast.43, s32[32]{0:T(128)S(1)} %copy-done.11, bf16[16,64,128]{2,1,0:T(8,128)(2,1)S(1)} %bitcast.41, f32[64,2048]{1,0:T(8,128)S(1)} %copy-done.4, f32[1,2048]{1,0:T(1,128)S(1)} %copy-done.9, bf16[128,2048]{1,0:T(8,128)(2,1)S(1)} %copy-done.5, ...), custom_call_target="tpu_custom_call" | custom-call | bytes 42000000 | tf_op jit(solution)/shard_map/attend_back/pallas_call | solution.py:495
  221.2 0.8 dynamic-slice_bitcast_fusion.3
  221.9 1.3 collective-permute-start
  223.2 0.7 collective-permute-start.1
  224.0 0.8 collective-permute-start.5
  224.8 1.1 collective-permute-start.4
  225.9 0.9 collective-permute-start.3
  226.8 6.4 %row_sum.2 = f32[1,1024,2048]{2,1,0:T(8,128)} custom-call(bf16[512,1024]{1,0:T(8,128)(2,1)S(1)} %bitcast.40, bf16[512,2048]{1,0:T(8,128)(2,1)S(1)} %copy-done.1), custom_call_target="tpu_custom_call" | custom-call | flops 2147483648 | bytes 8388608 | tf_op jit(solution)/shard_map/row_sum/pallas_call | solution.py:692
  233.3 6.4 %row_sum.3 = f32[1,2048,1024]{2,1,0:T(8,128)} custom-call(bf16[512,2048]{1,0:T(8,128)(2,1)S(1)} %copy-done, bf16[512,1024]{1,0:T(8,128)(2,1)S(1)} %bitcast.39), custom_call_target="tpu_custom_call" | custom-call | flops 2147483648 | bytes 8388608 | tf_op jit(solution)/shard_map/row_sum/pallas_call | solution.py:692
  239.7 2.9 collective-permute-start.2
  242.6 0.9 fusion.2.refs_11_
  243.5 2.3 collective-permute-done.2.refs_3_
  245.8 0.7 copy-done.15
  246.5 36.0 %end.1 = (bf16[128,1024]{1,0:T(8,128)(2,1)}, f32[32,3072]{1,0:T(8,128)}, f32[32,4096]{1,0:T(8,128)}, f32[32,1024]{1,0:T(8,128)}, f32[24,128]{1,0:T(8,128)}) custom-call(bf16[3,64,512]{2,1,0:T(8,128)(2,1)} %get-tuple-element.123.refs_0_, bf16[3,64,512]{2,1,0:T(8,128)(2,1)} %copy-done.13, bf16[3,64,512]{2,1,0:T(8,128)(2,1)} %copy-done.14, ...), custom_call_target="tpu_custom_call" | custom-call | bytes 120000000 | tf_op jit(solution)/shard_map/end/pallas_call | solution.py:1074
  282.4 3.5 %deliver.1 = (bf16[128,1024]{1,0:T(8,128)(2,1)}, bf16[128,1024]{1,0:T(8,128)(2,1)}, f32[32,3072]{1,0:T(8,128)}, f32[32,1024]{1,0:T(8,128)}, f32[32,4096]{1,0:T(8...) custom-call(s32[1]{0:T(128)S(6)} %mul.3.shift, f32[24,128]{1,0:T(8,128)} %get-tuple-element.98.small, ...), custom_call_target="tpu_custom_call" | custom-call | tf_op jit(solution)/shard_map/deliver/pallas_call | solution.py:2480
  286.0 1.3 fusion.3
  (41 shorter events, 0.4 us)
Async XLA Ops:
  7.2 109.5 %all-gather.2.cloned.1.call-start = ((), (), s32[]{:S(2)}) async-start(), calls=%async_computation.1 | async-start | bytes 2621440 | tf_op jit(solution)/shard_map/all_gather | solution.py:2568
  58.3 187.5 %reduce-scatter.2.cloned.1.call-start = ((), (), s32[]{:S(2)}) async-start(), calls=%async_computation.2 | async-start | bytes 1310720 | tf_op jit(solution)/shard_map/reduce_scatter | solution.py:2683
  116.7 89.4 %copy-start.4 = (f32[64,2048]{1,0:T(8,128)S(1)}, f32[64,2048]{1,0:T(8,128)}, u32[]{:S(2)}) copy-start(f32[64,2048]{1,0:T(8,128)} %get-tuple-element.85.out_ref) | copy-start | bytes 1572868
  116.7 89.4 %copy-start.5 = (bf16[128,2048]{1,0:T(8,128)(2,1)S(1)}, bf16[128,2048]{1,0:T(8,128)(2,1)}, u32[]{:S(2)}) copy-start(bf16[128,2048]{1,0:T(8,128)(2,1)} %get-tuple-element.87.q_ref) | copy-start | bytes 1572868
  116.7 89.4 %copy-start.6 = (bf16[128,2048]{1,0:T(8,128)(2,1)S(1)}, bf16[128,2048]{1,0:T(8,128)(2,1)}, u32[]{:S(2)}) copy-start(bf16[128,2048]{1,0:T(8,128)(2,1)} %get-tuple-element.88.kvt_ref) | copy-start | bytes 1572868
  116.7 89.4 %copy-start.7 = (bf16[2048,128]{1,0:T(8,128)(2,1)S(1)}, bf16[2048,128]{1,0:T(8,128)(2,1)}, u32[]{:S(2)}) copy-start(bf16[2048,128]{1,0:T(8,128)(2,1)} %get-tuple-element.89.rows_ref) | copy-start | bytes 1572868
  116.7 89.4 %copy-start.9 = (f32[1,2048]{1,0:T(1,128)S(1)}, f32[1,2048]{1,0:T(1,128)}, u32[]{:S(2)}) copy-start(f32[1,2048]{1,0:T(1,128)} %get-tuple-element.86.lse_ref) | copy-start | bytes 24580
  116.7 89.4 %copy-start.10 = (s32[1,8]{1,0:T(1,128)S(1)}, s32[1,8]{1,0:T(1,128)}, u32[]{:S(2)}) copy-start(s32[1,8]{1,0:T(1,128)} %param.17) | copy-start | bytes 100
  116.7 89.4 %copy-start.11 = (s32[32]{0:T(128)S(1)}, s32[32]{0:T(128)}, u32[]{:S(2)}) copy-start(s32[32]{0:T(128)} %order.3) | copy-start | bytes 388
  206.1 1.0 copy-start.8
  207.0 16.9 %copy-start.12 = (bf16[4,4,32,1024]{3,2,1,0:T(8,128)(2,1)S(1)}, bf16[4,4,32,1024]{3,2,1,0:T(8,128)(2,1)}, u32[]{:S(2)}) copy-start(bf16[4,4,32,1024]{3,2,1,0:T(8,128)(2,1)} %get-tuple-element.97) | copy-start | bytes 3145732
  221.2 5.7 %copy-start.1 = (bf16[512,2048]{1,0:T(8,128)(2,1)S(1)}, bf16[512,2048]{1,0:T(8,128)(2,1)}, u32[]{:S(2)}) copy-start(bf16[512,2048]{1,0:T(8,128)(2,1)} %get-tuple-element.114.right) | copy-start | bytes 6291460
  221.2 5.7 %copy-start.3 = (bf16[2,4,64,1024]{3,2,1,0:T(8,128)(2,1)S(1)}, bf16[2,4,64,1024]{3,2,1,0:T(8,128)(2,1)}, u32[]{:S(2)}) copy-start(bf16[2,4,64,1024]{3,2,1,0:T(8,128)(2,1)} %get-tuple-element.113) | copy-start | bytes 3145732
  221.9 21.5 %collective-permute-start = (bf16[3,64,512]{2,1,0:T(8,128)(2,1)S(1)}, bf16[3,64,512]{2,1,0:T(8,128)(2,1)S(1)}, u32[]{:S(2)}, u32[]{:S(2)}) collective-permute-start(bf16[3,64,512]{2,1,0:T(8,128)(2,1)S(1)} %get-tuple-element.122), channel_id=1, source_target_pairs={{0,4},{1,5},{2,6},{3,7},{4,8},{5,9},{6,10},{7,11},{8,12},{9,13},{1... | collective-permute-start | bytes 589832 | tf_op jit(solution)/shard_map/ppermute | solution.py:2680
  223.2 20.3 %collective-permute-start.1 = (bf16[3,64,512]{2,1,0:T(8,128)(2,1)S(1)}, bf16[3,64,512]{2,1,0:T(8,128)(2,1)S(1)}, u32[]{:S(2)}, u32[]{:S(2)}) collective-permute-start(bf16[3,64,512]{2,1,0:T(8,128)(2,1)S(1)} %get-tuple-element.121), channel_id=1, source_target_pairs={{0,8},{1,9},{2,10},{3,11},{4,12},{5,13},{6,14},{7,15},{8,0},{9,1},... | collective-permute-start | bytes 589832 | tf_op jit(solution)/shard_map/ppermute | solution.py:2680
  224.0 15.7 %collective-permute-start.5 = (bf16[4,32,1024]{2,1,0:T(8,128)(2,1)S(1)}, bf16[4,32,1024]{2,1,0:T(8,128)(2,1)S(1)}, u32[]{:S(2)}, u32[]{:S(2)}) collective-permute-start(bf16[4,32,1024]{2,1,0:T(8,128)(2,1)S(1)} %get-tuple-element.118), channel_id=1, source_target_pairs={{0,3},{1,0},{2,1},{3,2},{4,7},{5,4},{6,5},{7,6},{8,11},{9,8},{10,9... | collective-permute-start | bytes 786440 | tf_op jit(solution)/shard_map/ppermute | solution.py:2680
  224.8 17.8 %collective-permute-start.4 = (bf16[4,32,1024]{2,1,0:T(8,128)(2,1)S(1)}, bf16[4,32,1024]{2,1,0:T(8,128)(2,1)S(1)}, u32[]{:S(2)}, u32[]{:S(2)}) collective-permute-start(bf16[4,32,1024]{2,1,0:T(8,128)(2,1)S(1)} %get-tuple-element.119), channel_id=1, source_target_pairs={{0,2},{1,3},{2,0},{3,1},{4,6},{5,7},{6,4},{7,5},{8,10},{9,11},{10,... | collective-permute-start | bytes 786440 | tf_op jit(solution)/shard_map/ppermute | solution.py:2680
  225.9 16.7 %collective-permute-start.3 = (bf16[4,32,1024]{2,1,0:T(8,128)(2,1)S(1)}, bf16[4,32,1024]{2,1,0:T(8,128)(2,1)S(1)}, u32[]{:S(2)}, u32[]{:S(2)}) collective-permute-start(bf16[4,32,1024]{2,1,0:T(8,128)(2,1)S(1)} %get-tuple-element.117), channel_id=1, source_target_pairs={{0,1},{1,2},{2,3},{3,0},{4,5},{5,6},{6,7},{7,4},{8,9},{9,10},{10,1... | collective-permute-start | bytes 786440 | tf_op jit(solution)/shard_map/ppermute | solution.py:2680
  226.8 6.5 %copy-start = (bf16[512,2048]{1,0:T(8,128)(2,1)S(1)}, bf16[512,2048]{1,0:T(8,128)(2,1)}, u32[]{:S(2)}) copy-start(bf16[512,2048]{1,0:T(8,128)(2,1)} %get-tuple-element.115.left) | copy-start | bytes 6291460
  226.8 6.5 %copy-start.2 = (bf16[2,4,64,1024]{3,2,1,0:T(8,128)(2,1)S(1)}, bf16[2,4,64,1024]{3,2,1,0:T(8,128)(2,1)}, u32[]{:S(2)}) copy-start(bf16[2,4,64,1024]{3,2,1,0:T(8,128)(2,1)} %get-tuple-element.116) | copy-start | bytes 3145732
  239.7 6.1 %collective-permute-start.2 = (bf16[3,64,512]{2,1,0:T(8,128)(2,1)S(1)}, bf16[3,64,512]{2,1,0:T(8,128)(2,1)S(1)}, u32[]{:S(2)}, u32[]{:S(2)}) collective-permute-start(bf16[3,64,512]{2,1,0:T(8,128)(2,1)S(1)} %get-tuple-element.120), channel_id=1, source_target_pairs={{0,12},{1,13},{2,14},{3,15},{4,0},{5,1},{6,2},{7,3},{8,4},{9,5},{1... | collective-permute-start | bytes 589832 | tf_op jit(solution)/shard_map/ppermute | solution.py:2680
  243.5 2.3 copy-start.13
  243.5 2.3 copy-start.14
  245.8 0.7 copy-start.15
Sparse Core Ops, SparseCore 0:
  58.4 58.2 all-gather.1
  206.0 31.7 reduce-scatter.1

commit v4 on v3

--- a/solution.py
+++ b/solution.py
@@ -522,7 +522,7 @@
 
 def mid_kernel(
     experts, team, member, att, wo, x, vec, rw, route, cot,
-    second, dgrad, send_s, send_g, sel, mixes, middle_own, prob_own, hot_own, second_own, att_own,
+    second, dgrad, send_s, send_g, sel, mixes, middle_own, prob_own, hot_own, second_own, att_own, sel_own,
     egrad,
 ):
     rows = middle_own.shape[0]
@@ -576,6 +576,8 @@
             hot_own[...] = jnp.where(hot, 1.0, 0.0)
             second_own[...] = low
             att_own[...] = part
+            place = lax.broadcasted_iota(jnp.int32, sel_own.shape, 1)
+            sel_own[...] = jnp.where(place == route_col * capacity + rank, 1.0, 0.0).astype(BF)
 
         return carry
 
@@ -600,6 +602,7 @@
         ((rows, 128), F32),
         ((rows, width), BF),
         ((width, rows), BF),
+        ((rows, experts * (slots // team)), BF),
     )
     inside = pl.BlockSpec(memory_space=pltpu.VMEM)
     return pl.pallas_call(
@@ -743,6 +746,24 @@
         self.started.append(copy)
         return copy
 
+    def other_group(self, bit, group=None):
+        group = self.g if group is None else group
+        return group + bit - 2 * bit * lax.rem(lax.div(group, bit), 2)
+
+    def send_group(self, src, dst, group):
+        k = len(self.started)
+        copy = pltpu.make_async_remote_copy(
+            src_ref=src,
+            dst_ref=dst,
+            send_sem=self.send_sem.at[k],
+            recv_sem=self.recv_sem.at[k],
+            device_id=(self.c, group * self.team + self.t),
+            device_id_type=MESH,
+        )
+        copy.start()
+        self.started.append(copy)
+        return copy
+
     def group_to(self, step):
         return lax.rem(self.g + step[1], self.groups)
 
@@ -784,11 +805,11 @@
 
 def start_kernel(sizes, *refs):
     tokens, cot, w_qkv, w_up, w_down, w_out, router, gains, biases, routes = refs[:10]
-    token_o, cot_o, heads_o, normed_o, weight_o, vec_o, out_o, ff_o, route_o = refs[10:19]
+    token_o, cot_o, heads_o, normed_o, weight_o, vec_o, out_o, ff_o, route_o, small_o = refs[10:20]
     (
         own, up, down, route, square, stage, weights, tokens_v, normed, mixed, heads, out_v,
         send_sem, recv_sem, local_sem,
-    ) = refs[19:]
+    ) = refs[20:]
     net, local = Net(sizes, send_sem, recv_sem), Local(local_sem)
     c, g, t = net.c, net.g, net.t
     two, groups, team = sizes
@@ -828,22 +849,33 @@
     later = [net.send(route, route_o.at[t], s) for s in net.team_steps]
     later += [net.send(up.at[net.team_to(s)], ff_o.at[0, t], s) for s in net.team_steps]
     arrive(staged)
-    spread = [net.send(stage, weights.at[c, g], s) for s in net.group_steps]
+    near, far = net.other_group(1), net.other_group(2)
+    last = net.other_group(2, near)
+    from_far = net.send_group(stage, weights.at[c, g], far)
+    from_near = net.send_group(stage, weights.at[c, g], near)
     swapped = [net.send(stage, weights.at[c, g], net.swap)]
     mine = local.copy(stage, weights.at[c, g])
     later += [net.send(cot, cot_o.at[t], s) for s in net.team_steps]
+    local.wait(mine)
+    from_far.wait_recv()
+    view = weights.at[c, far]
+    passed = net.send_group(view, view, near)
+    swapped.append(net.send(view, view, net.swap))
+    from_near.wait_recv()
+    view = weights.at[c, near]
+    swapped.append(net.send(view, view, net.swap))
+    passed.wait_recv()
+    view = weights.at[c, last]
+    swapped.append(net.send(view, view, net.swap))
     local.wait(own_tokens)
     arrive(told)
     local.copy(tokens_v, token_o)
-    local.wait(mine)
-    for copy, s in zip(spread, net.group_steps):
-        copy.wait_recv()
-        view = weights.at[c, net.group_from(s)]
-        swapped.append(net.send(view, view, net.swap))
     arrive(swapped)
     local.copy(weights, weight_o)
 
-    small = weights[:, :, :, :, used:].reshape(width, 128).astype(F32).T
+    small = weights[:, :, :, :, used:].reshape(width, 128)
+    small_o[...] = small
+    small = small.astype(F32).T
     vec_o[...] = small[120:, :]
 
     def norm(b, carry):
@@ -897,6 +929,7 @@
         ((two, groups, team, wr, width), BF),
         ((2,) + up, BF),
         ((team, 8, rows), jnp.int32),
+        ((width, 128), BF),
     )
     anywhere = pl.BlockSpec(memory_space=pl.ANY)
     inside = pl.BlockSpec(memory_space=pltpu.VMEM)
@@ -906,7 +939,7 @@
         name="start",
         out_shape=tuple(jax.ShapeDtypeStruct(s, d) for s, d in shapes),
         in_specs=[anywhere] * 2 + [inside] * 8,
-        out_specs=tuple(inside if n == 5 else anywhere for n in range(9)),
+        out_specs=tuple(inside if n in (5, 9) else anywhere for n in range(10)),
         scratch_shapes=[
             pltpu.VMEM((team, wr, cols), BF),
             pltpu.VMEM(up, BF),
@@ -994,11 +1027,13 @@
 
     lax.fori_loop(0, half // tile, keeping, 0)
     deep = half // groups
-    summed = [
-        net.send(zsend.at[span(net.group_to(s), deep), :], zrecv.at[g], s)
-        for s in net.group_steps
-    ]
-    zrecv[g] = zsend[span(g, deep), :]
+    near, far = net.other_group(1), net.other_group(2)
+    last = net.other_group(2, near)
+    for_far = net.send_group(zsend.at[span(last, deep), :], zrecv.at[0], near)
+    for_me = net.send_group(zsend.at[span(near, deep), :], zrecv.at[1], near)
+    for_far.wait_recv()
+    zrecv[3] = (zsend[span(far, deep), :].astype(F32) + zrecv[0].astype(F32)).astype(BF)
+    summed = [for_me, net.send_group(zrecv.at[3], zrecv.at[2], far)]
 
     arrive(owned)
     flow = jnp.sum(nrecv[...].astype(F32), axis=0)
@@ -1035,7 +1070,8 @@
     later += [net.send(small_d.at[t], small_d.at[t], s) for s in net.team_steps]
 
     arrive(summed)
-    qsend[...] = jnp.sum(zrecv[...].astype(F32), axis=0).astype(BF).reshape(qsend.shape)
+    total = zsend[span(g, deep), :].astype(F32) + zrecv[1].astype(F32) + zrecv[2].astype(F32)
+    qsend[...] = total.astype(BF).reshape(qsend.shape)
     later += [net.send(qsend.at[net.team_to(s)], qrecv.at[t], s) for s in net.team_steps]
     qrecv[t] = qsend[t]
     arrive(outed)
@@ -1767,6 +1803,7 @@
         hot_own,
         second_own,
         attended_own,
+        _,
     ) = between(
         experts,
         sizes,
@@ -2026,20 +2063,20 @@
 
 def whole_kernel(sizes, experts, copies_count, *refs):
     two, groups, team = sizes
-    (send_s, send_g, eup_h, edown_h, second_h, dgrad_h, ff_h, sel_h, cot_h, mix_h) = refs[:10]
-    (middle_h, prob_h, hot_h, own_h, att_h, rw_h, wo_h, vec_h) = refs[10:18]
+    (send_s, send_g, eup_h, edown_h, second_h, dgrad_h, ff_h, sel_h, cot_h) = refs[:9]
+    (middle_h, prob_h, hot_h, own_h, att_h, rw_h, wo_h, vec_h) = refs[9:17]
     (
         layer_o, middle_o, small_o, flow_o, out_o, down_o, up_o,
         active_o, hgrad_o, arr_s_o, arr_g_o,
-    ) = refs[18:29]
+    ) = refs[17:28]
     (
-        arr_s, arr_g, eup, edown, second, dgrad, upw, downw, sel, cot, mix,
+        arr_s, arr_g, eup, edown, second, dgrad, upw, downw, sel, cot,
         slope, active, hgrad, acc, give, got_s, got_g, ret_s, ret_g, back_s, back_g,
-        low, ugrad, dense, spart, lay, spa, sums, lay_r, spa_r, sums_r,
-        term_give, term_got, ffg, ff_r,
+        low, ugrad, lay, spa, lay_r, spa_r,
+        term_give, term_got, out_got, ffg, ff_r,
         middle, prob, hot, own, att, rw, wo, vec, flow_t, flow_1,
         send_sem, recv_sem, load_sem, out_sem,
-    ) = refs[29:]
+    ) = refs[28:]
     c = lax.axis_index("dp")
     i = lax.axis_index("ctx")
     g, t = lax.div(i, team), lax.rem(i, team)
@@ -2049,6 +2086,8 @@
     core = lax.rem(c + 1, two)
 
     def device(step):
+        if not isinstance(step, tuple):
+            return c, step * team + t
         dc, dg, dt = step
         return (
             lax.rem(c + dc, two),
@@ -2080,16 +2119,17 @@
 
     loads = []
     for k, (src, dst) in enumerate(
-        [
-            (second_h, second), (dgrad_h, dgrad), (eup_h, eup), (edown_h, edown), (sel_h, sel), (cot_h, cot), (mix_h, mix),
-            (send_s.at[g], arr_s.at[c, g]), (send_g.at[g], arr_g.at[c, g]),
+        [(second_h, second), (dgrad_h, dgrad)]
+        + [
+            (ff_h.at[k, n], weight.at[block_of(c, k), :])
+            for n, weight in enumerate((upw, downw))
+            for k in range(groups)
+        ]
+        + [
+            (send_s.at[g], arr_s.at[c, g]), (eup_h, eup), (edown_h, edown),
+            (send_g.at[g], arr_g.at[c, g]), (sel_h, sel), (cot_h, cot),
             (middle_h, middle), (prob_h, prob), (hot_h, hot), (own_h, own),
             (att_h, att), (rw_h, rw), (wo_h, wo), (vec_h, vec),
-        ]
-        + [
-            (ff_h.at[k, n], weight.at[block_of(c, k), :])
-            for k in range(groups)
-            for n, weight in enumerate((upw, downw))
         ]
     ):
         load = pltpu.make_async_copy(src, dst, load_sem.at[k])
@@ -2097,7 +2137,10 @@
         loads.append(load)
 
     barrier = pltpu.get_barrier_semaphore()
-    greet = group_steps + team_steps + [swap]
+    home_steps = [
+        (0, dg, dt) for dg in range(groups) for dt in range(team) if dg or dt
+    ]
+    greet = home_steps + [swap]
     for step in greet:
         pl.semaphore_signal(barrier, inc=1, device_id=device(step), device_id_type=MESH)
     pl.semaphore_wait(barrier, len(greet))
@@ -2109,10 +2152,16 @@
         every.append(copy)
         return copy
 
-    def to_groups(src, dst):
-        return [
-            launch(remote(src.at[lax.rem(g + s[1], groups)], dst.at[g], s)) for s in group_steps
-        ]
+    each = arr_s.shape[2] // team
+
+    def to_home(src, dst):
+        me = g * team + t
+        made = []
+        for s in home_steps:
+            to_g, to_t = lax.rem(g + s[1], groups), lax.rem(t + s[2], team)
+            made.append(launch(remote(src.at[to_g, span(to_t, each), :], dst.at[me], s)))
+        dst[me] = src[g, span(t, each), :]
+        return made
 
     def source(s):
         return lax.rem(g + groups - s[1], groups)
@@ -2127,13 +2176,8 @@
         for s in group_steps
     ]
     swap_s = [launch(remote(send_s.at[g], arr_s.at[c, g], swap))]
-    out_g = [
-        launch(remote(send_g.at[lax.rem(g + s[1], groups)], arr_g.at[c, g], s))
-        for s in group_steps
-    ]
-    swap_g = [launch(remote(send_g.at[g], arr_g.at[c, g], swap))]
-
-    for load in loads[:2] + loads[17:]:
+    dense_loads = 2 + 2 * groups
+    for load in loads[:dense_loads]:
         load.wait()
     for copy in swap_w:
         copy.wait_recv()
@@ -2146,49 +2190,30 @@
         return carry
 
     lax.fori_loop(0, hid // TILE, dense_in, 0)
+    out_g = [
+        launch(remote(send_g.at[lax.rem(g + s[1], groups)], arr_g.at[c, g], s))
+        for s in group_steps
+    ]
+    swap_g = [launch(remote(send_g.at[g], arr_g.at[c, g], swap))]
 
     def dense_out(n, carry):
         at = span(n, TILE)
-        dense[:, at] = dot_f32(low[...], downw[:, at])
-        spart[:, at] = contract_cols(ugrad[...], upw[at, :])
+        made = dot_f32(low[...], downw[:, at])
+        lay[:, :, at] = made.astype(BF).reshape(team, rows, TILE)
+        made = contract_cols(ugrad[...], upw[at, :])
+        spa[:, :, at] = made.astype(BF).reshape(team, rows, TILE)
         return carry
 
     lax.fori_loop(0, width // TILE, dense_out, 0)
 
-    half = hid // 2
-    term_tile = 128
-
-    def down_term(base, n):
-        at = pl.ds(pl.multiple_of(base + n * term_tile, term_tile), term_tile)
-        return contract_rows(low[:, at], dgrad[...])
-
-    def up_term(base, n):
-        at = pl.ds(pl.multiple_of(base + n * term_tile, term_tile), term_tile)
-        return contract_rows(second[:, at], ugrad[...])
-
-    terms = []
-    for k, (term, size) in enumerate(((down_term, half), (up_term, width // 2))):
-
-        def giving(n, carry, k=k, term=term, size=size):
-            term_give[k, span(n, term_tile), :] = term(core * size, n).astype(BF)
-            return carry
-
-        lax.fori_loop(0, size // term_tile, giving, 0)
-        terms.append(launch(remote(term_give.at[k], term_got.at[k], swap)))
-    for k, (term, size) in enumerate(((down_term, half), (up_term, width // 2))):
-        terms[k].wait_recv()
-
-        def keeping(n, carry, k=k, term=term, size=size):
-            at = span(n, term_tile)
-            total = term(c * size, n) + term_got[k, at, :].astype(F32)
-            ffg[k, at, :] = total.astype(BF)
-            return carry
-
-        lax.fori_loop(0, size // term_tile, keeping, 0)
-    up_copy = pltpu.make_async_copy(ffg.at[1], up_o, out_sem.at[4])
-    up_copy.start()
-
-    for load in loads[2:17]:
+    def to_team(src, dst):
+        made = [launch(remote(src.at[lax.rem(t + s[2], team)], dst.at[t], s)) for s in team_steps]
+        dst[t] = src[t]
+        return made
+
+    team_copies = to_team(lay, lay_r) + to_team(spa, spa_r)
+
+    for load in loads[dense_loads : dense_loads + 4]:
         load.wait()
     for copy, s in zip(out_s, group_steps):
         copy.wait_recv()
@@ -2226,8 +2251,7 @@
         swap_g.append(launch(remote(arr_g.at[c, source(s)], arr_g.at[c, source(s)], swap)))
     other_s.wait_recv()
     ret_s[...] = (acc[c] + got_s[...].astype(F32)).astype(BF).reshape(ret_s.shape)
-    home_s = to_groups(ret_s, back_s)
-    back_s[g] = ret_s[g]
+    home_s = to_home(ret_s, back_s)
     for copy in swap_g:
         copy.wait_recv()
 
@@ -2255,77 +2279,85 @@
     other_g = launch(remote(give.at[1], got_g, swap))
     other_g.wait_recv()
     ret_g[...] = (acc[c] + got_g[...].astype(F32)).astype(BF).reshape(ret_g.shape)
-    home_g = to_groups(ret_g, back_g)
-    back_g[g] = ret_g[g]
-
-    for copy in home_s:
+    home_g = to_home(ret_g, back_g)
+
+    half = hid // 2
+    term_tile = 128
+
+    def down_term(base, n):
+        at = pl.ds(pl.multiple_of(base + n * term_tile, term_tile), term_tile)
+        return contract_rows(low[:, at], dgrad[...])
+
+    def up_term(base, n):
+        at = pl.ds(pl.multiple_of(base + n * term_tile, term_tile), term_tile)
+        return contract_rows(second[:, at], ugrad[...])
+
+    terms = []
+    for k, (term, size) in enumerate(((down_term, half), (up_term, width // 2))):
+
+        def giving(n, carry, k=k, term=term, size=size):
+            term_give[k, span(n, term_tile), :] = term(core * size, n).astype(BF)
+            return carry
+
+        lax.fori_loop(0, size // term_tile, giving, 0)
+        terms.append(launch(remote(term_give.at[k], term_got.at[k], swap)))
+    for k, (term, size) in enumerate(((down_term, half), (up_term, width // 2))):
+        terms[k].wait_recv()
+
+        def keeping(n, carry, k=k, term=term, size=size):
+            at = span(n, term_tile)
+            total = term(c * size, n) + term_got[k, at, :].astype(F32)
+            ffg[k, at, :] = total.astype(BF)
+            return carry
+
+        lax.fori_loop(0, size // term_tile, keeping, 0)
+    up_copy = pltpu.make_async_copy(ffg.at[1], up_o, out_sem.at[4])
+    up_copy.start()
+
+    for load in loads[dense_loads + 4 :]:
+        load.wait()
+    for copy in team_copies + home_s:
         copy.wait_recv()
-    slots = groups * back_s.shape[1]
     lane = lax.broadcasted_iota(jnp.int32, (rows, 128), 1)
-
-    def join_layer(r, carry):
-        at = span(r, rows)
-        found = dot_f32(sel[at, :], back_s[...].reshape(slots, width))
-        own = dense[at, :]
-        flow = cot[at, :].astype(F32)
-        mixes = mix[at, :]
-        lay[r] = (mixes[:, 0:1] * own + mixes[:, 1:2] * found).astype(BF)
-        plain = jnp.sum(flow * own, axis=1, keepdims=True)
-        routed = jnp.sum(flow * found, axis=1, keepdims=True)
-        sums[r] = jnp.where(lane == 0, plain, jnp.where(lane == 1, routed, 0.0))
-        return carry
-
-    lax.fori_loop(0, team, join_layer, 0)
-
-    def to_team(src, dst):
-        made = [launch(remote(src.at[lax.rem(t + s[2], team)], dst.at[t], s)) for s in team_steps]
-        dst[t] = src[t]
-        return made
-
-    team_copies = to_team(lay, lay_r) + to_team(sums, sums_r)
-
-    for copy in home_g:
-        copy.wait_recv()
-    piece = half // groups
-    downs = [
-        launch(remote(ffg.at[0, span(lax.rem(g + s[1], groups), piece), :], ff_r.at[g], s))
-        for s in group_steps
-    ]
-    ff_r[g] = ffg[0, span(g, piece), :]
-
-    def join_grad(r, carry):
-        at = span(r, rows)
-        found = dot_f32(sel[at, :], back_g[...].reshape(slots, width))
-        spa[r] = (spart[at, :] + found).astype(BF)
-        return carry
-
-    lax.fori_loop(0, team, join_grad, 0)
-    team_copies += to_team(spa, spa_r)
-
-    for copy in team_copies:
-        copy.wait_recv()
-
-    sum_own = jnp.sum(sums_r[...], axis=0)
-    layer_o[...] = (middle[...] + jnp.sum(lay_r[...].astype(F32), axis=0)).astype(BF)
+    places = groups * team * each
     chances, chosen = prob[...], hot[...]
-    s0, s1 = sum_own[:, 0:1], sum_own[:, 1:2]
+    mix0 = jnp.sum(jnp.where(lane == experts, chances, 0.0), axis=1, keepdims=True)
     mix1 = jnp.sum(jnp.where(lane == experts + 1, chances, 0.0), axis=1, keepdims=True)
     gate = jnp.sum(chances * chosen, axis=1, keepdims=True)
+    flow = cot[...].astype(F32)
+    plain = jnp.sum(lay_r[...].astype(F32), axis=0)
+    found = dot_f32(sel[...], back_s[...].reshape(places, width))
+    layer_o[...] = (middle[...] + mix0 * plain + (mix1 * gate) * found).astype(BF)
+    s0 = jnp.sum(flow * plain, axis=1, keepdims=True)
+    s1 = jnp.sum(flow * found, axis=1, keepdims=True)
     pulls = jnp.where(lane == experts, s0, jnp.where(lane == experts + 1, s1 * gate, 0.0))
     mean_pull = jnp.sum(chances * pulls, axis=1, keepdims=True)
     logit_grad = chances * jnp.where(
         lane < experts, (s1 * mix1) * (chosen - gate), pulls - mean_pull
     )
     logit_grad = jnp.where(lane < experts + 2, logit_grad, 0.0).astype(BF)
-    second_grad = jnp.sum(spa_r[...].astype(F32), axis=0) + contract_cols(logit_grad, rw[...])
     hat, scale = normalize(middle[...])
+    early = jnp.sum(spa_r[...].astype(F32), axis=0) + contract_cols(logit_grad, rw[...])
+    for copy in home_g:
+        copy.wait_recv()
+    piece = half // groups
+
+    def other_group(bit, group):
+        return group + bit - 2 * bit * lax.rem(lax.div(group, bit), 2)
+
+    near, far = other_group(1, g), other_group(2, g)
+    last = other_group(2, near)
+    for_far = launch(remote(ffg.at[0, span(last, piece), :], ff_r.at[0], near))
+    downs = [launch(remote(ffg.at[0, span(near, piece), :], ff_r.at[1], near))]
+
+    second_grad = early + dot_f32(sel[...], back_g[...].reshape(places, width))
     pull = second_grad * vec[5:6, :]
     moved = scale * (
         pull
         - jnp.mean(pull, axis=-1, keepdims=True)
         - hat * jnp.mean(pull * hat, axis=-1, keepdims=True)
     )
-    middle_grad = cot[span(t, rows), :].astype(F32) + moved
+    middle_grad = flow + moved
     middle_o[...] = middle_grad
     branch = middle_grad.astype(BF)
 
@@ -2348,7 +2380,7 @@
     terms[0].wait_send()
     every[:] = [copy for copy in every if copy is not terms[0]]
     lax.fori_loop(0, width // 2 // term_tile, out_giving, 0)
-    out_cross = launch(remote(term_give.at[0], term_got.at[0], swap))
+    out_cross = launch(remote(term_give.at[0], out_got, swap))
     for copy in flowed:
         copy.wait_recv()
     flowed = [
@@ -2357,12 +2389,15 @@
     ]
     own_flow = pltpu.make_async_copy(flow_1.at[:, g], flow_o.at[g], out_sem.at[5])
     own_flow.start()
+    for_far.wait_recv()
+    ff_r[3] = (ffg[0, span(far, piece), :].astype(F32) + ff_r[0].astype(F32)).astype(BF)
+    downs.append(launch(remote(ff_r.at[3], ff_r.at[2], far)))
     out_cross.wait_recv()
     wr = out_o.shape[2]
 
     def out_keeping(n, carry):
         at = span(n, term_tile)
-        total = out_term(c * (width // 2), n) + term_got[0, at, :].astype(F32)
+        total = out_term(c * (width // 2), n) + out_got[at, :].astype(F32)
         out_o[:, n] = total.astype(BF).reshape(team, wr, width)
         return carry
 
@@ -2377,7 +2412,9 @@
     )
     for copy in downs:
         copy.wait_recv()
-    down_o[...] = jnp.sum(ff_r[...].astype(F32), axis=0)
+    down_o[...] = (
+        ffg[0, span(g, piece), :].astype(F32) + ff_r[1].astype(F32) + ff_r[2].astype(F32)
+    )
     for copy in flowed:
         copy.wait_recv()
     for copy in keeps + [up_copy, own_flow]:
@@ -2387,7 +2424,7 @@
 
 
 def whole(
-    sizes, rows, experts, wr, send_s, send_g, eup, edown, second, dgrad, ff, sel, cot, mix,
+    sizes, rows, experts, wr, send_s, send_g, eup, edown, second, dgrad, ff, sel, cot,
     middle, prob, hot, own, att, rw, wo, vec,
 ):
     two, groups, team = sizes
@@ -2396,7 +2433,9 @@
     hid, ehid = ff.shape[3], eup.shape[1]
     entries = 2 * groups * slots
     used = -(-(experts + 6) // 8) * 8
-    count = 6 * (groups - 1) + 2 * groups + 5 + 5 * (team - 1) + 2 * groups
+    homes = groups * team - 1
+    count = 3 * (groups - 1) + 4 * groups + 5 + 3 * (team - 1) + 2 * homes + 3
+    each = slots // team
     arrived = (two, groups, slots, width)
     anywhere = pl.BlockSpec(memory_space=pl.ANY)
     inside = pl.BlockSpec(memory_space=pltpu.VMEM)
@@ -2418,17 +2457,17 @@
     scratch = (
         (arrived, BF), (arrived, BF), (eup.shape, BF), (edown.shape, BF), (second.shape, BF),
         (dgrad.shape, BF), ((width, hid), BF), ((hid, width), BF), (sel.shape, BF),
-        (cot.shape, BF), (mix.shape, F32),
+        (cot.shape, BF),
         ((entries, ehid), F32), ((entries, ehid), BF), ((entries, ehid), BF),
         ((2, entries // 2, width), F32), ((2, entries // 2, width), BF),
         ((entries // 2, width), BF), ((entries // 2, width), BF),
         ((groups, slots, width), BF), ((groups, slots, width), BF),
-        ((groups, slots, width), BF), ((groups, slots, width), BF),
-        ((team_rows, hid), BF), ((team_rows, hid), BF), ((team_rows, width), F32),
-        ((team_rows, width), F32), ((team, rows, width), BF), ((team, rows, width), BF),
-        ((team, rows, 128), F32), ((team, rows, width), BF), ((team, rows, width), BF),
-        ((team, rows, 128), F32),
-        ((2, hid // 2, width), BF), ((2, hid // 2, width), BF), ((2, hid // 2, width), BF),
+        ((groups * team, each, width), BF), ((groups * team, each, width), BF),
+        ((team_rows, hid), BF), ((team_rows, hid), BF),
+        ((team, rows, width), BF), ((team, rows, width), BF),
+        ((team, rows, width), BF), ((team, rows, width), BF),
+        ((2, hid // 2, width), BF), ((2, hid // 2, width), BF), ((width // 2, width), BF),
+        ((2, hid // 2, width), BF),
         ((groups, hid // 2 // groups, width), BF),
         (middle.shape, F32), (prob.shape, F32), (hot.shape, F32), (own.shape, BF),
         (att.shape, BF), (rw.shape, BF), (wo.shape, BF), (vec.shape, F32),
@@ -2438,13 +2477,13 @@
         functools.partial(whole_kernel, sizes, experts, count),
         name="feed_forward",
         out_shape=tuple(jax.ShapeDtypeStruct(s, d) for s, d in shapes),
-        in_specs=[anywhere] * 18,
+        in_specs=[anywhere] * 17,
         out_specs=tuple(inside if n in (0, 1, 2, 4, 5) else anywhere for n in range(11)),
         scratch_shapes=[pltpu.VMEM(s, d) for s, d in scratch]
         + [
             pltpu.SemaphoreType.DMA((count,)),
             pltpu.SemaphoreType.DMA((count,)),
-            pltpu.SemaphoreType.DMA((17 + 2 * groups,)),
+            pltpu.SemaphoreType.DMA((16 + 2 * groups,)),
             pltpu.SemaphoreType.DMA((6,)),
         ],
         compiler_params=pltpu.CompilerParams(
@@ -2452,7 +2491,7 @@
         ),
         cost_estimate=pl.CostEstimate(flops=0, bytes_accessed=300_000_000, transcendentals=0),
     )(
-        send_s, send_g, eup, edown, second, dgrad, ff, sel, cot, mix,
+        send_s, send_g, eup, edown, second, dgrad, ff, sel, cot,
         middle, prob, hot, own, att, rw, wo, vec,
     )
 
@@ -2517,7 +2556,7 @@
     length = rows * ctx_count
     wr = w_qkv.shape[0]
     experts = ctx_count * expert_up.shape[0]
-    fits = groups * team == HEADS and team * wr == 128 and w_up.shape[1] == team * width
+    fits = groups == team == 4 and groups * team == HEADS and team * wr == 128 and w_up.shape[1] == team * width
     if not fits or length // block_order.shape[0] != BLOCK:
         return per_device_general(
             tokens, cotangent, block_order, doc_lengths, routes, w_qkv, w_out, w_up, w_down,
@@ -2528,7 +2567,6 @@
     slots = team * capacity
     hidden = w_up.shape[1]
     hidden_dev = w_down.shape[0]
-    qkv_cols = 3 * width // team
     up_cols = hidden // team
     ctx = lax.axis_index("ctx")
     core = lax.axis_index("dp")
@@ -2547,6 +2585,7 @@
         out_weight,
         ff_part,
         route_all,
+        router_weight,
     ) = start(
         sizes,
         tokens[0],
@@ -2560,7 +2599,6 @@
         norm_biases,
         routes[0].reshape(1, rows),
     )
-    router_weight = weights[:, :, :, :, qkv_cols:].reshape(width, 128)
     out_weight = out_weight.reshape(width, width)
     token_rows = token_rows.reshape(group_rows, width)
     cot_rows = cot_rows.reshape(group_rows, width)
@@ -2609,6 +2647,7 @@
         hot_own,
         second_own,
         attended_own,
+        select_own,
     ) = between(
         experts,
         sizes,
@@ -2646,9 +2685,8 @@
         second_low,
         dense_grad,
         ff_half,
-        select,
-        cot_rows,
-        mixes,
+        select_own,
+        cotangent[0],
         middle_own,
         prob_own,
         hot_own,

time: 294 us -> 281 us (0.956)
  Pallas kernels: 259 us -> 245 us
    pallas_call x1, Pallas kernels: 89.2 us -> 81.5 us  [whole(): pl.pallas_call(functools.partial(whole_kernel, sizes, experts, count), na...]
    pallas_call x1, Pallas kernels: 26.4 us -> 22.9 us  [exchange(): pl.pallas_call(kernel, name=name, out_shape=tuple((jax.ShapeDtypeStruct(s...]
where the time goes in v4:
time: 281 us
  Pallas kernels  245 us (87%)
  between operations  14.3 us (5%)
  waiting for transfers between devices  9.25 us (3%)
  starting transfers between devices  7.58 us (3%)
  local copies, waits for them, and re-layouts  3.79 us (1%)
    pallas_call x1, Pallas kernels, whole(): pl.pallas_call(functools.partial(whole_kernel, sizes, experts, count), na...  81.5 us
    pallas_call x1, Pallas kernels, start(): pl.pallas_call(functools.partial(start_kernel, sizes), name='start', out_...  51.1 us
    pallas_call x1, Pallas kernels, end(): pl.pallas_call(functools.partial(end_kernel, sizes, experts), name='end',...  33.6 us
    pallas_call x1, Pallas kernels, exchange(): pl.pallas_call(kernel, name=name, out_shape=tuple((jax.ShapeDtypeStruct(s...  22.9 us
    pallas_call x1, Pallas kernels, sorted_attend(): pl.pallas_call(sorted_attend_kernel, name='attend', grid=(length // TILE,...  16.1 us
    pallas_call x1, Pallas kernels, sorted_back(): pl.pallas_call(sorted_back_kernel, name='attend_back', grid=(length // TI...  14.1 us
    pallas_call x2, Pallas kernels, row_sum(): pl.pallas_call(row_sum_kernel, name='row_sum', grid=(high // tile,), in_s...  12.8 us
    pallas_call x1, Pallas kernels, between(): pl.pallas_call(functools.partial(mid_kernel, experts, team), name='betwee...  9.67 us
  transfers between devices with their start and end apart: 8, of which 2 were waited for; matrix products, arithmetic and copies ran while one was open for 1% of the time, Pallas kernels for 27%

profile of v4, /device:TPU:0, one launch (start us, length us, event | category | flops | bytes accessed | tf_op | source)
XLA Modules:
  0.0 281.2 jit_solution(12092844363815656592)
XLA Ops:
  7.2 51.1 %start.1 = (bf16[4,128,1024]{2,1,0:T(8,128)(2,1)}, bf16[4,128,1024]{2,1,0:T(8,128)(2,1)}, bf16[4,3,64,512]{3,2,1,0:T(8,128)(2,1)}, bf16[4,128,1024]{2,1,0:T(8,12...) custom-call(bf16[128,1024]{1,0:T(8,128)(2,1)} %bitcast.52, ...), custom_call_target="tpu_custom_call" | custom-call | bytes 150000000 | tf_op jit(solution)/shard_map/start/pallas_call | solution.py:937
  58.4 0.2 reduce-scatter.2.cloned.1.call-start
  58.6 16.1 %attend.1 = (bf16[4,64,512]{2,1,0:T(8,128)(2,1)}, f32[64,2048]{1,0:T(8,128)}, f32[1,2048]{1,0:T(1,128)}, bf16[128,2048]{1,0:T(8,128)(2,1)}, bf16[128,2048]{1,0:T(8,128)(2,1)}, /*index=5*/bf16[2048,128]{1,0:T(8,128)(2,1)}) custom-call(s32[8]{0:T(128)} %bitcast.41, s32[32]{0:T(128)} %order.3, bf16[4,192,512]{2,1,0:T(8,128)(2,1)} %bitcast.54), custom_call_target="tpu_custom_call" | custom-call | bytes 42000000 | tf_op jit(solution)/shard_map/attend/pallas_call | solution.py:477
  74.7 22.9 %attended.1 = bf16[4,4,64,512]{3,2,1,0:T(8,128)(2,1)} custom-call(bf16[4,64,512]{2,1,0:T(8,128)(2,1)} %get-tuple-element.65.refs_0_), custom_call_target="tpu_custom_call" | custom-call | bytes 60000000 | tf_op jit(solution)/shard_map/attended/pallas_call | solution.py:138
  97.6 9.7 %between.1 = (bf16[512,1024]{1,0:T(8,128)(2,1)}, bf16[512,1024]{1,0:T(8,128)(2,1)}, bf16[4,64,1024]{2,1,0:T(8,128)(2,1)}, bf16[4,64,1024]{2,1,0:T(8,128)(2,1)}, ...) custom-call(s32[1]{0:T(128)} %bitcast.member, ...), custom_call_target="tpu_custom_call" | custom-call | tf_op jit(solution)/shard_map/between/pallas_call | solution.py:608
  107.3 5.8 %all-gather.2.cloned.1.call-done.refs_6_ = bf16[4,2,128,1024]{3,2,1,0:T(8,128)(2,1)} async-done(((bf16[1,2,128,1024]{3,2,1,0:T(8,128)(2,1)}), bf16[4,2,128,1024]{3,2,1,0:T(8,128)(2,1)}) %all-gather.2.cloned.1.call-update) | async-done | bytes 2097168 | tf_op jit(solution)/shard_map/all_gather | solution.py:2606
  113.1 81.5 %feed_forward.1 = (bf16[128,1024]{1,0:T(8,128)(2,1)}, f32[128,1024]{1,0:T(8,128)}, f32[24,1024]{1,0:T(8,128)}, bf16[4,4,64,128]{3,2,1,0:T(8,128)(2,1)}, bf16[4,4...) custom-call(bf16[4,64,1024]{2,1,0:T(8,128)(2,1)} %get-tuple-element., ...), custom_call_target="tpu_custom_call" | custom-call | bytes 300000000 | tf_op jit(solution)/shard_map/feed_forward/pallas_call | solution.py:2476
  194.8 0.9 copy-done.8
  195.7 14.1 %attend_back.1 = bf16[4,3,64,512]{3,2,1,0:T(8,128)(2,1)S(1)} custom-call(s32[8]{0:T(128)S(1)} %bitcast.42, s32[32]{0:T(128)S(1)} %copy-done.11, bf16[16,64,128]{2,1,0:T(8,128)(2,1)S(1)} %bitcast.40, f32[64,2048]{1,0:T(8,128)S(1)} %copy-done.4, f32[1,2048]{1,0:T(1,128)S(1)} %copy-done.9, bf16[128,2048]{1,0:T(8,128)(2,1)S(1)} %copy-done.5, ...), custom_call_target="tpu_custom_call" | custom-call | bytes 42000000 | tf_op jit(solution)/shard_map/attend_back/pallas_call | solution.py:495
  209.9 0.8 dynamic-slice_bitcast_fusion.3
  210.7 1.4 collective-permute-start.1
  212.1 0.1 dynamic-slice_bitcast_fusion.2
  212.1 1.5 collective-permute-start.5
  213.7 1.8 collective-permute-start.4
  215.4 0.3 collective-permute-start.3
  215.7 6.4 %row_sum.2 = f32[1,1024,2048]{2,1,0:T(8,128)} custom-call(bf16[512,1024]{1,0:T(8,128)(2,1)S(1)} %bitcast.39, bf16[512,2048]{1,0:T(8,128)(2,1)S(1)} %copy-done.1), custom_call_target="tpu_custom_call" | custom-call | flops 2147483648 | bytes 8388608 | tf_op jit(solution)/shard_map/row_sum/pallas_call | solution.py:695
  222.2 6.4 %row_sum.3 = f32[1,2048,1024]{2,1,0:T(8,128)} custom-call(bf16[512,2048]{1,0:T(8,128)(2,1)S(1)} %copy-done, bf16[512,1024]{1,0:T(8,128)(2,1)S(1)} %bitcast.38), custom_call_target="tpu_custom_call" | custom-call | flops 2147483648 | bytes 8388608 | tf_op jit(solution)/shard_map/row_sum/pallas_call | solution.py:695
  228.6 2.3 collective-permute-start.2
  230.9 0.9 fusion.2.refs_11_
  231.8 3.4 %collective-permute-done.2.refs_3_ = bf16[3,64,512]{2,1,0:T(8,128)(2,1)S(1)} collective-permute-done((bf16[3,64,512]{2,1,0:T(8,128)(2,1)S(1)}, bf16[3,64,512]{2,1,0:T(8,128)(2,1)S(1)}, u32[]{:S(2)}, u32[]{:S(2)}) %collective-permute-start.2) | collective-permute-done | bytes 196640 | tf_op jit(solution)/shard_map/ppermute | solution.py:2718
  235.3 0.7 copy-done.15
  235.9 33.6 %end.1 = (bf16[128,1024]{1,0:T(8,128)(2,1)}, f32[32,3072]{1,0:T(8,128)}, f32[32,4096]{1,0:T(8,128)}, f32[32,1024]{1,0:T(8,128)}, f32[24,128]{1,0:T(8,128)}) custom-call(bf16[3,64,512]{2,1,0:T(8,128)(2,1)} %get-tuple-element.123.refs_0_, bf16[3,64,512]{2,1,0:T(8,128)(2,1)} %copy-done.13, bf16[3,64,512]{2,1,0:T(8,128)(2,1)} %copy-done.14, ...), custom_call_target="tpu_custom_call" | custom-call | bytes 120000000 | tf_op jit(solution)/shard_map/end/pallas_call | solution.py:1110
  269.6 3.5 %deliver.1 = (bf16[128,1024]{1,0:T(8,128)(2,1)}, bf16[128,1024]{1,0:T(8,128)(2,1)}, f32[32,3072]{1,0:T(8,128)}, f32[32,1024]{1,0:T(8,128)}, f32[32,4096]{1,0:T(8...) custom-call(s32[1]{0:T(128)S(6)} %mul.3.shift, f32[24,128]{1,0:T(8,128)} %get-tuple-element.98.small, ...), custom_call_target="tpu_custom_call" | custom-call | tf_op jit(solution)/shard_map/deliver/pallas_call | solution.py:2519
  273.1 1.3 fusion.3
  (40 shorter events, 0.2 us)
Async XLA Ops:
  7.2 105.8 %all-gather.2.cloned.1.call-start = ((), (), s32[]{:S(2)}) async-start(), calls=%async_computation.1 | async-start | bytes 2621440 | tf_op jit(solution)/shard_map/all_gather | solution.py:2606
  58.4 176.8 %reduce-scatter.2.cloned.1.call-start = ((), (), s32[]{:S(2)}) async-start(), calls=%async_computation.2 | async-start | bytes 1310720 | tf_op jit(solution)/shard_map/reduce_scatter | solution.py:2721
  113.0 81.7 %copy-start.4 = (f32[64,2048]{1,0:T(8,128)S(1)}, f32[64,2048]{1,0:T(8,128)}, u32[]{:S(2)}) copy-start(f32[64,2048]{1,0:T(8,128)} %get-tuple-element.84.out_ref) | copy-start | bytes 1572868
  113.0 81.7 %copy-start.5 = (bf16[128,2048]{1,0:T(8,128)(2,1)S(1)}, bf16[128,2048]{1,0:T(8,128)(2,1)}, u32[]{:S(2)}) copy-start(bf16[128,2048]{1,0:T(8,128)(2,1)} %get-tuple-element.86.q_ref) | copy-start | bytes 1572868
  113.0 81.7 %copy-start.6 = (bf16[128,2048]{1,0:T(8,128)(2,1)S(1)}, bf16[128,2048]{1,0:T(8,128)(2,1)}, u32[]{:S(2)}) copy-start(bf16[128,2048]{1,0:T(8,128)(2,1)} %get-tuple-element.87.kvt_ref) | copy-start | bytes 1572868
  113.0 81.7 %copy-start.7 = (bf16[2048,128]{1,0:T(8,128)(2,1)S(1)}, bf16[2048,128]{1,0:T(8,128)(2,1)}, u32[]{:S(2)}) copy-start(bf16[2048,128]{1,0:T(8,128)(2,1)} %get-tuple-element.88.rows_ref) | copy-start | bytes 1572868
  113.0 81.7 %copy-start.9 = (f32[1,2048]{1,0:T(1,128)S(1)}, f32[1,2048]{1,0:T(1,128)}, u32[]{:S(2)}) copy-start(f32[1,2048]{1,0:T(1,128)} %get-tuple-element.85.lse_ref) | copy-start | bytes 24580
  113.0 81.7 %copy-start.10 = (s32[1,8]{1,0:T(1,128)S(1)}, s32[1,8]{1,0:T(1,128)}, u32[]{:S(2)}) copy-start(s32[1,8]{1,0:T(1,128)} %param.17) | copy-start | bytes 100
  113.1 81.7 %copy-start.11 = (s32[32]{0:T(128)S(1)}, s32[32]{0:T(128)}, u32[]{:S(2)}) copy-start(s32[32]{0:T(128)} %order.3) | copy-start | bytes 388
  194.8 1.0 copy-start.8
  195.7 16.3 %copy-start.12 = (bf16[4,4,32,1024]{3,2,1,0:T(8,128)(2,1)S(1)}, bf16[4,4,32,1024]{3,2,1,0:T(8,128)(2,1)}, u32[]{:S(2)}) copy-start(bf16[4,4,32,1024]{3,2,1,0:T(8,128)(2,1)} %get-tuple-element.97) | copy-start | bytes 3145732
  209.9 5.8 %copy-start.1 = (bf16[512,2048]{1,0:T(8,128)(2,1)S(1)}, bf16[512,2048]{1,0:T(8,128)(2,1)}, u32[]{:S(2)}) copy-start(bf16[512,2048]{1,0:T(8,128)(2,1)} %get-tuple-element.114.right) | copy-start | bytes 6291460
  209.9 5.8 %copy-start.3 = (bf16[2,4,64,1024]{3,2,1,0:T(8,128)(2,1)S(1)}, bf16[2,4,64,1024]{3,2,1,0:T(8,128)(2,1)}, u32[]{:S(2)}) copy-start(bf16[2,4,64,1024]{3,2,1,0:T(8,128)(2,1)} %get-tuple-element.113) | copy-start | bytes 3145732
  210.7 21.1 %collective-permute-start = (bf16[3,64,512]{2,1,0:T(8,128)(2,1)S(1)}, bf16[3,64,512]{2,1,0:T(8,128)(2,1)S(1)}, u32[]{:S(2)}, u32[]{:S(2)}) collective-permute-start(bf16[3,64,512]{2,1,0:T(8,128)(2,1)S(1)} %get-tuple-element.122), channel_id=1, source_target_pairs={{0,4},{1,5},{2,6},{3,7},{4,8},{5,9},{6,10},{7,11},{8,12},{9,13},{1... | collective-permute-start | bytes 589832 | tf_op jit(solution)/shard_map/ppermute | solution.py:2718
  210.7 21.1 %collective-permute-start.1 = (bf16[3,64,512]{2,1,0:T(8,128)(2,1)S(1)}, bf16[3,64,512]{2,1,0:T(8,128)(2,1)S(1)}, u32[]{:S(2)}, u32[]{:S(2)}) collective-permute-start(bf16[3,64,512]{2,1,0:T(8,128)(2,1)S(1)} %get-tuple-element.121), channel_id=1, source_target_pairs={{0,8},{1,9},{2,10},{3,11},{4,12},{5,13},{6,14},{7,15},{8,0},{9,1},... | collective-permute-start | bytes 589832 | tf_op jit(solution)/shard_map/ppermute | solution.py:2718
  212.1 16.4 %collective-permute-start.5 = (bf16[4,32,1024]{2,1,0:T(8,128)(2,1)S(1)}, bf16[4,32,1024]{2,1,0:T(8,128)(2,1)S(1)}, u32[]{:S(2)}, u32[]{:S(2)}) collective-permute-start(bf16[4,32,1024]{2,1,0:T(8,128)(2,1)S(1)} %get-tuple-element.118), channel_id=1, source_target_pairs={{0,3},{1,0},{2,1},{3,2},{4,7},{5,4},{6,5},{7,6},{8,11},{9,8},{10,9... | collective-permute-start | bytes 786440 | tf_op jit(solution)/shard_map/ppermute | solution.py:2718
  213.7 17.2 %collective-permute-start.4 = (bf16[4,32,1024]{2,1,0:T(8,128)(2,1)S(1)}, bf16[4,32,1024]{2,1,0:T(8,128)(2,1)S(1)}, u32[]{:S(2)}, u32[]{:S(2)}) collective-permute-start(bf16[4,32,1024]{2,1,0:T(8,128)(2,1)S(1)} %get-tuple-element.119), channel_id=1, source_target_pairs={{0,2},{1,3},{2,0},{3,1},{4,6},{5,7},{6,4},{7,5},{8,10},{9,11},{10,... | collective-permute-start | bytes 786440 | tf_op jit(solution)/shard_map/ppermute | solution.py:2718
  215.4 15.5 %collective-permute-start.3 = (bf16[4,32,1024]{2,1,0:T(8,128)(2,1)S(1)}, bf16[4,32,1024]{2,1,0:T(8,128)(2,1)S(1)}, u32[]{:S(2)}, u32[]{:S(2)}) collective-permute-start(bf16[4,32,1024]{2,1,0:T(8,128)(2,1)S(1)} %get-tuple-element.117), channel_id=1, source_target_pairs={{0,1},{1,2},{2,3},{3,0},{4,5},{5,6},{6,7},{7,4},{8,9},{9,10},{10,1... | collective-permute-start | bytes 786440 | tf_op jit(solution)/shard_map/ppermute | solution.py:2718
  215.7 6.5 %copy-start = (bf16[512,2048]{1,0:T(8,128)(2,1)S(1)}, bf16[512,2048]{1,0:T(8,128)(2,1)}, u32[]{:S(2)}) copy-start(bf16[512,2048]{1,0:T(8,128)(2,1)} %get-tuple-element.115.left) | copy-start | bytes 6291460
  215.7 6.5 %copy-start.2 = (bf16[2,4,64,1024]{3,2,1,0:T(8,128)(2,1)S(1)}, bf16[2,4,64,1024]{3,2,1,0:T(8,128)(2,1)}, u32[]{:S(2)}) copy-start(bf16[2,4,64,1024]{3,2,1,0:T(8,128)(2,1)} %get-tuple-element.116) | copy-start | bytes 3145732
  228.6 6.7 %collective-permute-start.2 = (bf16[3,64,512]{2,1,0:T(8,128)(2,1)S(1)}, bf16[3,64,512]{2,1,0:T(8,128)(2,1)S(1)}, u32[]{:S(2)}, u32[]{:S(2)}) collective-permute-start(bf16[3,64,512]{2,1,0:T(8,128)(2,1)S(1)} %get-tuple-element.120), channel_id=1, source_target_pairs={{0,12},{1,13},{2,14},{3,15},{4,0},{5,1},{6,2},{7,3},{8,4},{9,5},{1... | collective-permute-start | bytes 589832 | tf_op jit(solution)/shard_map/ppermute | solution.py:2718
  231.8 3.5 %copy-start.13 = (bf16[3,64,512]{2,1,0:T(8,128)(2,1)}, bf16[3,64,512]{2,1,0:T(8,128)(2,1)S(1)}, u32[]{:S(2)}) copy-start(bf16[3,64,512]{2,1,0:T(8,128)(2,1)S(1)} %collective-permute-done.refs_1_) | copy-start | bytes 589828
  231.8 3.5 %copy-start.14 = (bf16[3,64,512]{2,1,0:T(8,128)(2,1)}, bf16[3,64,512]{2,1,0:T(8,128)(2,1)S(1)}, u32[]{:S(2)}) copy-start(bf16[3,64,512]{2,1,0:T(8,128)(2,1)S(1)} %collective-permute-done.1.refs_2_) | copy-start | bytes 589828
  235.2 0.7 copy-start.15
Sparse Core Ops, SparseCore 0:
  58.5 54.4 all-gather.1
  194.8 28.6 reduce-scatter.1

commit v5 on v4

--- a/solution.py
+++ b/solution.py
@@ -750,6 +750,23 @@
         group = self.g if group is None else group
         return group + bit - 2 * bit * lax.rem(lax.div(group, bit), 2)
 
+    def other_member(self, bit):
+        return self.t + bit - 2 * bit * lax.rem(lax.div(self.t, bit), 2)
+
+    def send_member(self, src, dst, member):
+        k = len(self.started)
+        copy = pltpu.make_async_remote_copy(
+            src_ref=src,
+            dst_ref=dst,
+            send_sem=self.send_sem.at[k],
+            recv_sem=self.recv_sem.at[k],
+            device_id=(self.c, self.g * self.team + member),
+            device_id_type=MESH,
+        )
+        copy.start()
+        self.started.append(copy)
+        return copy
+
     def send_group(self, src, dst, group):
         k = len(self.started)
         copy = pltpu.make_async_remote_copy(
@@ -833,7 +850,6 @@
     stage[t] = own[t]
     net.greet()
     staged = [net.send(own.at[net.team_to(s)], stage.at[t], s) for s in net.team_steps]
-    told = [net.send(tokens, tokens_v.at[t], s) for s in net.team_steps]
     out_v[g] = w_out[...].astype(BF)
     spread_out = [net.send(out_v.at[g], out_v.at[g], s) for s in net.group_steps]
     deep = w_down.shape[0]
@@ -846,8 +862,6 @@
     local.copy(up.at[t], ff_o.at[0, t])
     local.copy(down, ff_o.at[1])
     local.copy(route, route_o.at[t])
-    later = [net.send(route, route_o.at[t], s) for s in net.team_steps]
-    later += [net.send(up.at[net.team_to(s)], ff_o.at[0, t], s) for s in net.team_steps]
     arrive(staged)
     near, far = net.other_group(1), net.other_group(2)
     last = net.other_group(2, near)
@@ -855,8 +869,27 @@
     from_near = net.send_group(stage, weights.at[c, g], near)
     swapped = [net.send(stage, weights.at[c, g], net.swap)]
     mine = local.copy(stage, weights.at[c, g])
-    later += [net.send(cot, cot_o.at[t], s) for s in net.team_steps]
+
+    side, other = net.other_member(1), net.other_member(2)
+    part = rows // 2
+
+    def to_sides(src, dst):
+        return [net.send_member(src, dst.at[t], member) for member in (side, other)]
+
+    def pass_on(copies, dst):
+        made = []
+        for n, (copy, at, to) in enumerate(zip(copies, (side, other), (other, side))):
+            copy.wait_recv()
+            view = dst.at[at, pl.ds(n * part, part)]
+            made.append(net.send_member(view, view, to))
+        return made
+
+    told = to_sides(tokens, tokens_v)
+    later = [net.send(route, route_o.at[t], s) for s in net.team_steps]
     local.wait(mine)
+    told = pass_on(told, tokens_v)
+    turned = to_sides(cot, cot_o)
+    later += [net.send(up.at[net.team_to(s)], ff_o.at[0, t], s) for s in net.team_steps]
     from_far.wait_recv()
     view = weights.at[c, far]
     passed = net.send_group(view, view, near)
@@ -894,6 +927,7 @@
         at = (n % per) * pair
         mixed[n // per, at : at + pair] = made.reshape(pair, HEAD_DIM, group_rows)
     given = [net.send(mixed.at[:, net.group_to(s)], heads.at[g], s) for s in net.group_steps]
+    later += pass_on(turned, cot_o)
     local.wait(local.copy(mixed.at[:, g], heads.at[g]))
 
     arrive(spread_out)
@@ -933,7 +967,7 @@
     )
     anywhere = pl.BlockSpec(memory_space=pl.ANY)
     inside = pl.BlockSpec(memory_space=pltpu.VMEM)
-    count = 6 * (team - 1) + 4 * (groups - 1) + 2 + (team - 1)
+    count = 6 * (team - 1) + 4 * (groups - 1) + 4 + (team - 1)
     return pl.pallas_call(
         functools.partial(start_kernel, sizes),
         name="start",
@@ -2074,7 +2108,7 @@
         slope, active, hgrad, acc, give, got_s, got_g, ret_s, ret_g, back_s, back_g,
         low, ugrad, lay, spa, lay_r, spa_r,
         term_give, term_got, out_got, ffg, ff_r,
-        middle, prob, hot, own, att, rw, wo, vec, flow_t, flow_1,
+        middle, prob, hot, own, att, rw, wo, vec, flow_t, flow_1, wo_s, wo_r,
         send_sem, recv_sem, load_sem, out_sem,
     ) = refs[28:]
     c = lax.axis_index("dp")
@@ -2393,15 +2427,16 @@
     ff_r[3] = (ffg[0, span(far, piece), :].astype(F32) + ff_r[0].astype(F32)).astype(BF)
     downs.append(launch(remote(ff_r.at[3], ff_r.at[2], far)))
     out_cross.wait_recv()
-    wr = out_o.shape[2]
+    wr = wo_s.shape[2]
 
     def out_keeping(n, carry):
         at = span(n, term_tile)
         total = out_term(c * (width // 2), n) + out_got[at, :].astype(F32)
-        out_o[:, n] = total.astype(BF).reshape(team, wr, width)
+        wo_s[:, n] = total.astype(BF).reshape(team, wr, width)
         return carry
 
     lax.fori_loop(0, groups, out_keeping, 0)
+    outs = to_team(wo_s, wo_r)
 
     routed = contract_rows(logit_grad, own[...])[: small_o.shape[0], :]
     which = lax.broadcasted_iota(jnp.int32, routed.shape, 0)
@@ -2410,6 +2445,9 @@
     small_o[...] = jnp.where(
         which == experts + 3, gain, jnp.where(which == experts + 5, bias, routed)
     )
+    for copy in outs:
+        copy.wait_recv()
+    out_o[...] = jnp.sum(wo_r[...].astype(F32), axis=0).astype(BF)
     for copy in downs:
         copy.wait_recv()
     down_o[...] = (
@@ -2434,7 +2472,7 @@
     entries = 2 * groups * slots
     used = -(-(experts + 6) // 8) * 8
     homes = groups * team - 1
-    count = 3 * (groups - 1) + 4 * groups + 5 + 3 * (team - 1) + 2 * homes + 3
+    count = 3 * (groups - 1) + 4 * groups + 5 + 4 * (team - 1) + 2 * homes + 3
     each = slots // team
     arrived = (two, groups, slots, width)
     anywhere = pl.BlockSpec(memory_space=pl.ANY)
@@ -2446,7 +2484,7 @@
         ((rows, width), F32),
         ((used, width), F32),
         ((groups, team, HEAD_DIM, rows), BF),
-        ((team, groups, wr, width), BF),
+        ((groups, wr, width), BF),
         ((hid // 2 // groups, width), F32),
         ((width // 2, hid), BF),
         ((entries, ehid), BF),
@@ -2472,6 +2510,7 @@
         (middle.shape, F32), (prob.shape, F32), (hot.shape, F32), (own.shape, BF),
         (att.shape, BF), (rw.shape, BF), (wo.shape, BF), (vec.shape, F32),
         ((team,) + heads, BF), ((team,) + heads, BF),
+        ((team, groups, wr, width), BF), ((team, groups, wr, width), BF),
     )
     return pl.pallas_call(
         functools.partial(whole_kernel, sizes, experts, count),
@@ -2498,15 +2537,15 @@
 
 def deliver_kernel(experts, count, shift, small, *refs):
     ins, outs = refs[:count], refs[count : 2 * count]
-    router, vectors = refs[2 * count : 2 * count + 2]
-    sem = refs[2 * count + 2]
+    router, gains, biases, sem = refs[2 * count :]
     copies = [pltpu.make_async_copy(a, b, sem.at[n]) for n, (a, b) in enumerate(zip(ins, outs))]
     for copy in copies:
         copy.start()
     wr = router.shape[1]
     mine = pltpu.roll(small[...], lax.rem(128 - shift[0], 128), 1)[:, :wr]
     router[...] = mine[: experts + 2, :]
-    vectors[...] = mine[experts + 2 : experts + 6, :]
+    gains[...] = mine[experts + 2 : experts + 4, :]
+    biases[...] = mine[experts + 4 : experts + 6, :]
     for copy in copies:
         copy.wait()
 
@@ -2520,11 +2559,12 @@
         functools.partial(deliver_kernel, experts, count),
         name="deliver",
         in_specs=[pl.BlockSpec(memory_space=pltpu.SMEM)] + [inside] * (count + 1),
-        out_specs=tuple([anywhere] * count + [inside] * 2),
+        out_specs=tuple([anywhere] * count + [inside] * 3),
         out_shape=tuple(jax.ShapeDtypeStruct(a.shape, a.dtype) for a in arrays)
         + (
             jax.ShapeDtypeStruct((experts + 2, wr), F32),
-            jax.ShapeDtypeStruct((4, wr), F32),
+            jax.ShapeDtypeStruct((2, wr), F32),
+            jax.ShapeDtypeStruct((2, wr), F32),
         ),
         scratch_shapes=[pltpu.SemaphoreType.DMA((count,))],
         compiler_params=pltpu.CompilerParams(vmem_limit_bytes=60 * 2**20),
@@ -2666,7 +2706,7 @@
         middle_grad,
         small_t,
         flow_parts,
-        out_half,
+        out_sum,
         down_sum,
         up_half,
         expert_active,
@@ -2721,7 +2761,6 @@
     up_sum = lax.psum_scatter(
         up_half, "ctx", scatter_dimension=0, tiled=True, axis_index_groups=by_group
     ).reshape(team, wr, up_cols)
-    out_pieces = pieces_of(out_half, "t")
     grad_parts = sorted_back(
         doc_lengths[0],
         block_order,
@@ -2739,7 +2778,6 @@
     )
 
     pieces = pieces_of(grad_parts, "g")
-    out_sum = sum(piece.astype(F32) for piece in out_pieces).astype(BF)
     entries = two * groups * slots
     expert_down_grad = row_sum(expert_active, arrived_grad.reshape(entries, width), TILE)
     expert_up_grad = row_sum(arrived_in.reshape(entries, width), hidden_grad, 128)
@@ -2762,7 +2800,8 @@
         small_own,
         (layer_out, input_grad, qkv_own, out_own, up_own, down_sum),
     )
-    layer_out, input_grad, qkv_own, out_own, up_own, down_sum, router_own, vectors_own = delivered
+    layer_out, input_grad, qkv_own, out_own, up_own, down_sum = delivered[:6]
+    router_own, gains_own, biases_own = delivered[6:]
     return (
         layer_out[None],
         input_grad[None],
@@ -2771,8 +2810,8 @@
         up_own,
         down_sum,
         router_own.T,
-        vectors_own[:2],
-        vectors_own[2:],
+        gains_own,
+        biases_own,
         expert_up_grad,
         expert_down_grad,
     )

time: 281 us -> 279 us (level)
  Pallas kernels: 245 us -> 248 us
    ppermute x6 -> x3, starting transfers between devices: 7.32 us -> 5.45 us  [pieces_of(): found.append(lax.ppermute(chunk, 'ctx', pairs))]
  transfers between devices with their start and end apart: 8 -> 5, of which waited for: 2 -> 2; matrix products, arithmetic and copies ran while one was open for 1% -> 0% of each run, Pallas kernels for 27% -> 27%
where the time goes in v5:
time: 279 us
  Pallas kernels  248 us (89%)
  between operations  14.3 us (5%)
  waiting for transfers between devices  9.05 us (3%)
  starting transfers between devices  5.71 us (2%)
    pallas_call x1, Pallas kernels, whole(): pl.pallas_call(functools.partial(whole_kernel, sizes, experts, count), na...  79.7 us
    pallas_call x1, Pallas kernels, start(): pl.pallas_call(functools.partial(start_kernel, sizes), name='start', out_...  51.4 us
    pallas_call x1, Pallas kernels, end(): pl.pallas_call(functools.partial(end_kernel, sizes, experts), name='end',...  36.2 us
    pallas_call x1, Pallas kernels, exchange(): pl.pallas_call(kernel, name=name, out_shape=tuple((jax.ShapeDtypeStruct(s...  24.1 us
    pallas_call x1, Pallas kernels, sorted_attend(): pl.pallas_call(sorted_attend_kernel, name='attend', grid=(length // TILE,...  16.1 us
    pallas_call x1, Pallas kernels, sorted_back(): pl.pallas_call(sorted_back_kernel, name='attend_back', grid=(length // TI...  14.1 us
    pallas_call x2, Pallas kernels, row_sum(): pl.pallas_call(row_sum_kernel, name='row_sum', grid=(high // tile,), in_s...  12.8 us
    pallas_call x1, Pallas kernels, between(): pl.pallas_call(functools.partial(mid_kernel, experts, team), name='betwee...  9.64 us
  transfers between devices with their start and end apart: 5, of which 2 were waited for; matrix products, arithmetic and copies ran while one was open for 0% of the time, Pallas kernels for 27%

profile of v5, /device:TPU:0, one launch (start us, length us, event | category | flops | bytes accessed | tf_op | source)
XLA Modules:
  0.0 279.0 jit_solution(9508616078141847976)
XLA Ops:
  7.2 0.0 all-gather.2.cloned.1.call-start
  7.2 51.4 %start.1 = (bf16[4,128,1024]{2,1,0:T(8,128)(2,1)}, bf16[4,128,1024]{2,1,0:T(8,128)(2,1)}, bf16[4,3,64,512]{3,2,1,0:T(8,128)(2,1)}, bf16[4,128,1024]{2,1,0:T(8,12...) custom-call(bf16[128,1024]{1,0:T(8,128)(2,1)} %bitcast.43, ...), custom_call_target="tpu_custom_call" | custom-call | bytes 150000000 | tf_op jit(solution)/shard_map/start/pallas_call | solution.py:971
  58.7 0.0 all-gather.2.cloned.1.call-update
  58.7 0.2 reduce-scatter.2.cloned.1.call-start
  58.9 16.1 %attend.1 = (bf16[4,64,512]{2,1,0:T(8,128)(2,1)}, f32[64,2048]{1,0:T(8,128)}, f32[1,2048]{1,0:T(1,128)}, bf16[128,2048]{1,0:T(8,128)(2,1)}, bf16[128,2048]{1,0:T(8,128)(2,1)}, /*index=5*/bf16[2048,128]{1,0:T(8,128)(2,1)}) custom-call(s32[8]{0:T(128)} %bitcast.32, s32[32]{0:T(128)} %order.3, bf16[4,192,512]{2,1,0:T(8,128)(2,1)} %bitcast.45), custom_call_target="tpu_custom_call" | custom-call | bytes 42000000 | tf_op jit(solution)/shard_map/attend/pallas_call | solution.py:477
  75.0 24.1 %attended.1 = bf16[4,4,64,512]{3,2,1,0:T(8,128)(2,1)} custom-call(bf16[4,64,512]{2,1,0:T(8,128)(2,1)} %get-tuple-element.66.refs_0_), custom_call_target="tpu_custom_call" | custom-call | bytes 60000000 | tf_op jit(solution)/shard_map/attended/pallas_call | solution.py:138
  99.1 9.6 %between.1 = (bf16[512,1024]{1,0:T(8,128)(2,1)}, bf16[512,1024]{1,0:T(8,128)(2,1)}, bf16[4,64,1024]{2,1,0:T(8,128)(2,1)}, bf16[4,64,1024]{2,1,0:T(8,128)(2,1)}, ...) custom-call(s32[1]{0:T(128)} %bitcast.member, ...), custom_call_target="tpu_custom_call" | custom-call | tf_op jit(solution)/shard_map/between/pallas_call | solution.py:608
  108.7 4.0 %all-gather.2.cloned.1.call-done.refs_6_ = bf16[4,2,128,1024]{3,2,1,0:T(8,128)(2,1)} async-done(((bf16[1,2,128,1024]{3,2,1,0:T(8,128)(2,1)}), bf16[4,2,128,1024]{3,2,1,0:T(8,128)(2,1)}) %all-gather.2.cloned.1.call-update) | async-done | bytes 2097168 | tf_op jit(solution)/shard_map/all_gather | solution.py:2646
  112.8 79.7 %feed_forward.1 = (bf16[128,1024]{1,0:T(8,128)(2,1)}, f32[128,1024]{1,0:T(8,128)}, f32[24,1024]{1,0:T(8,128)}, bf16[4,4,64,128]{3,2,1,0:T(8,128)(2,1)}, bf16[4,3...) custom-call(bf16[4,64,1024]{2,1,0:T(8,128)(2,1)} %get-tuple-element., ...), custom_call_target="tpu_custom_call" | custom-call | bytes 300000000 | tf_op jit(solution)/shard_map/feed_forward/pallas_call | solution.py:2515
  192.5 0.0 reduce-scatter.2.cloned.1.call-update
  192.6 0.9 copy-done.8
  193.6 14.1 %attend_back.1 = bf16[4,3,64,512]{3,2,1,0:T(8,128)(2,1)S(1)} custom-call(s32[8]{0:T(128)S(1)} %bitcast.33, s32[32]{0:T(128)S(1)} %copy-done.11, bf16[16,64,128]{2,1,0:T(8,128)(2,1)S(1)} %bitcast.31, f32[64,2048]{1,0:T(8,128)S(1)} %copy-done.4, f32[1,2048]{1,0:T(1,128)S(1)} %copy-done.9, bf16[128,2048]{1,0:T(8,128)(2,1)S(1)} %copy-done.5, ...), custom_call_target="tpu_custom_call" | custom-call | bytes 42000000 | tf_op jit(solution)/shard_map/attend_back/pallas_call | solution.py:495
  207.7 0.8 dynamic-slice_bitcast_fusion
  208.5 3.1 %collective-permute-start = (bf16[3,64,512]{2,1,0:T(8,128)(2,1)S(1)}, bf16[3,64,512]{2,1,0:T(8,128)(2,1)S(1)}, u32[]{:S(2)}, u32[]{:S(2)}) collective-permute-start(bf16[3,64,512]{2,1,0:T(8,128)(2,1)S(1)} %get-tuple-element.121), channel_id=1, source_target_pairs={{0,4},{1,5},{2,6},{3,7},{4,8},{5,9},{6,10},{7,11},{8,12},{9,13},{1... | collective-permute-start | bytes 589832 | tf_op jit(solution)/shard_map/ppermute | solution.py:2758
  211.6 0.6 collective-permute-start.1
  212.2 1.8 collective-permute-start.2
  214.0 6.4 %row_sum.2 = f32[1,1024,2048]{2,1,0:T(8,128)} custom-call(bf16[512,1024]{1,0:T(8,128)(2,1)S(1)} %bitcast.30, bf16[512,2048]{1,0:T(8,128)(2,1)S(1)} %copy-done.1), custom_call_target="tpu_custom_call" | custom-call | flops 2147483648 | bytes 8388608 | tf_op jit(solution)/shard_map/row_sum/pallas_call | solution.py:695
  220.4 6.4 %row_sum.3 = f32[1,2048,1024]{2,1,0:T(8,128)} custom-call(bf16[512,2048]{1,0:T(8,128)(2,1)S(1)} %copy-done, bf16[512,1024]{1,0:T(8,128)(2,1)S(1)} %bitcast.29), custom_call_target="tpu_custom_call" | custom-call | flops 2147483648 | bytes 8388608 | tf_op jit(solution)/shard_map/row_sum/pallas_call | solution.py:695
  226.8 5.0 %collective-permute-done.1.refs_2_ = bf16[3,64,512]{2,1,0:T(8,128)(2,1)S(1)} collective-permute-done((bf16[3,64,512]{2,1,0:T(8,128)(2,1)S(1)}, bf16[3,64,512]{2,1,0:T(8,128)(2,1)S(1)}, u32[]{:S(2)}, u32[]{:S(2)}) %collective-permute-start.1) | collective-permute-done | bytes 196640 | tf_op jit(solution)/shard_map/ppermute | solution.py:2758
  231.8 0.0 reduce-scatter.2.cloned.1.call-done
  231.8 0.6 copy-done.13
  232.4 0.1 copy-done.14
  232.5 36.2 %end.1 = (bf16[128,1024]{1,0:T(8,128)(2,1)}, f32[32,3072]{1,0:T(8,128)}, f32[32,4096]{1,0:T(8,128)}, f32[32,1024]{1,0:T(8,128)}, f32[24,128]{1,0:T(8,128)}) custom-call(bf16[3,64,512]{2,1,0:T(8,128)(2,1)} %get-tuple-element.122.refs_0_, bf16[3,64,512]{2,1,0:T(8,128)(2,1)} %copy-done.12, bf16[3,64,512]{2,1,0:T(8,128)(2,1)} %copy-done.13, ...), custom_call_target="tpu_custom_call" | custom-call | bytes 120000000 | tf_op jit(solution)/shard_map/end/pallas_call | solution.py:1144
  268.7 3.5 %deliver.1 = (bf16[128,1024]{1,0:T(8,128)(2,1)}, bf16[128,1024]{1,0:T(8,128)(2,1)}, f32[32,3072]{1,0:T(8,128)}, f32[32,1024]{1,0:T(8,128)}, f32[32,4096]{1,0:T(8...) custom-call(s32[1]{0:T(128)S(6)} %mul.3.shift, ...), custom_call_target="tpu_custom_call" | custom-call | tf_op jit(solution)/shard_map/deliver/pallas_call | solution.py:2558
  (29 shorter events, 0.1 us)
Async XLA Ops:
  7.2 105.6 %all-gather.2.cloned.1.call-start = ((), (), s32[]{:S(2)}) async-start(), calls=%async_computation.1 | async-start | bytes 2621440 | tf_op jit(solution)/shard_map/all_gather | solution.py:2646
  58.7 173.1 %reduce-scatter.2.cloned.1.call-start = ((), (), s32[]{:S(2)}) async-start(), calls=%async_computation.2 | async-start | bytes 1310720 | tf_op jit(solution)/shard_map/reduce_scatter | solution.py:2761
  112.8 79.8 %copy-start.4 = (f32[64,2048]{1,0:T(8,128)S(1)}, f32[64,2048]{1,0:T(8,128)}, u32[]{:S(2)}) copy-start(f32[64,2048]{1,0:T(8,128)} %get-tuple-element.85.out_ref) | copy-start | bytes 1572868
  112.8 79.8 %copy-start.5 = (bf16[128,2048]{1,0:T(8,128)(2,1)S(1)}, bf16[128,2048]{1,0:T(8,128)(2,1)}, u32[]{:S(2)}) copy-start(bf16[128,2048]{1,0:T(8,128)(2,1)} %get-tuple-element.87.q_ref) | copy-start | bytes 1572868
  112.8 79.8 %copy-start.6 = (bf16[128,2048]{1,0:T(8,128)(2,1)S(1)}, bf16[128,2048]{1,0:T(8,128)(2,1)}, u32[]{:S(2)}) copy-start(bf16[128,2048]{1,0:T(8,128)(2,1)} %get-tuple-element.88.kvt_ref) | copy-start | bytes 1572868
  112.8 79.8 %copy-start.7 = (bf16[2048,128]{1,0:T(8,128)(2,1)S(1)}, bf16[2048,128]{1,0:T(8,128)(2,1)}, u32[]{:S(2)}) copy-start(bf16[2048,128]{1,0:T(8,128)(2,1)} %get-tuple-element.89.rows_ref) | copy-start | bytes 1572868
  112.8 79.8 %copy-start.9 = (f32[1,2048]{1,0:T(1,128)S(1)}, f32[1,2048]{1,0:T(1,128)}, u32[]{:S(2)}) copy-start(f32[1,2048]{1,0:T(1,128)} %get-tuple-element.86.lse_ref) | copy-start | bytes 24580
  112.8 79.8 %copy-start.10 = (s32[1,8]{1,0:T(1,128)S(1)}, s32[1,8]{1,0:T(1,128)}, u32[]{:S(2)}) copy-start(s32[1,8]{1,0:T(1,128)} %param.17) | copy-start | bytes 100
  112.8 79.8 %copy-start.11 = (s32[32]{0:T(128)S(1)}, s32[32]{0:T(128)}, u32[]{:S(2)}) copy-start(s32[32]{0:T(128)} %order.3) | copy-start | bytes 388
  192.6 1.0 copy-start.8
  193.6 20.4 %copy-start.1 = (bf16[512,2048]{1,0:T(8,128)(2,1)S(1)}, bf16[512,2048]{1,0:T(8,128)(2,1)}, u32[]{:S(2)}) copy-start(bf16[512,2048]{1,0:T(8,128)(2,1)} %get-tuple-element.116.right) | copy-start | bytes 6291460
  193.6 20.4 %copy-start.3 = (bf16[2,4,64,1024]{3,2,1,0:T(8,128)(2,1)S(1)}, bf16[2,4,64,1024]{3,2,1,0:T(8,128)(2,1)}, u32[]{:S(2)}) copy-start(bf16[2,4,64,1024]{3,2,1,0:T(8,128)(2,1)} %get-tuple-element.115) | copy-start | bytes 3145732
  208.5 18.3 %collective-permute-start = (bf16[3,64,512]{2,1,0:T(8,128)(2,1)S(1)}, bf16[3,64,512]{2,1,0:T(8,128)(2,1)S(1)}, u32[]{:S(2)}, u32[]{:S(2)}) collective-permute-start(bf16[3,64,512]{2,1,0:T(8,128)(2,1)S(1)} %get-tuple-element.121), channel_id=1, source_target_pairs={{0,4},{1,5},{2,6},{3,7},{4,8},{5,9},{6,10},{7,11},{8,12},{9,13},{1... | collective-permute-start | bytes 589832 | tf_op jit(solution)/shard_map/ppermute | solution.py:2758
  211.6 20.2 %collective-permute-start.1 = (bf16[3,64,512]{2,1,0:T(8,128)(2,1)S(1)}, bf16[3,64,512]{2,1,0:T(8,128)(2,1)S(1)}, u32[]{:S(2)}, u32[]{:S(2)}) collective-permute-start(bf16[3,64,512]{2,1,0:T(8,128)(2,1)S(1)} %get-tuple-element.120), channel_id=1, source_target_pairs={{0,8},{1,9},{2,10},{3,11},{4,12},{5,13},{6,14},{7,15},{8,0},{9,1},... | collective-permute-start | bytes 589832 | tf_op jit(solution)/shard_map/ppermute | solution.py:2758
  212.2 19.6 %collective-permute-start.2 = (bf16[3,64,512]{2,1,0:T(8,128)(2,1)S(1)}, bf16[3,64,512]{2,1,0:T(8,128)(2,1)S(1)}, u32[]{:S(2)}, u32[]{:S(2)}) collective-permute-start(bf16[3,64,512]{2,1,0:T(8,128)(2,1)S(1)} %get-tuple-element.119), channel_id=1, source_target_pairs={{0,12},{1,13},{2,14},{3,15},{4,0},{5,1},{6,2},{7,3},{8,4},{9,5},{1... | collective-permute-start | bytes 589832 | tf_op jit(solution)/shard_map/ppermute | solution.py:2758
  213.9 6.5 %copy-start = (bf16[512,2048]{1,0:T(8,128)(2,1)S(1)}, bf16[512,2048]{1,0:T(8,128)(2,1)}, u32[]{:S(2)}) copy-start(bf16[512,2048]{1,0:T(8,128)(2,1)} %get-tuple-element.117.left) | copy-start | bytes 6291460
  213.9 6.5 %copy-start.2 = (bf16[2,4,64,1024]{3,2,1,0:T(8,128)(2,1)S(1)}, bf16[2,4,64,1024]{3,2,1,0:T(8,128)(2,1)}, u32[]{:S(2)}) copy-start(bf16[2,4,64,1024]{3,2,1,0:T(8,128)(2,1)} %get-tuple-element.118) | copy-start | bytes 3145732
  226.8 5.0 %copy-start.12 = (bf16[3,64,512]{2,1,0:T(8,128)(2,1)}, bf16[3,64,512]{2,1,0:T(8,128)(2,1)S(1)}, u32[]{:S(2)}) copy-start(bf16[3,64,512]{2,1,0:T(8,128)(2,1)S(1)} %collective-permute-done.refs_1_) | copy-start | bytes 589828
  231.7 0.7 copy-start.13
  231.8 0.7 copy-start.14
Sparse Core Ops, SparseCore 0:
  58.8 53.8 all-gather.1
  192.6 33.7 reduce-scatter.1

commit v6 on v5

--- a/solution.py
+++ b/solution.py
@@ -824,7 +824,7 @@
     tokens, cot, w_qkv, w_up, w_down, w_out, router, gains, biases, routes = refs[:10]
     token_o, cot_o, heads_o, normed_o, weight_o, vec_o, out_o, ff_o, route_o, small_o = refs[10:20]
     (
-        own, up, down, route, square, stage, weights, tokens_v, normed, mixed, heads, out_v,
+        own, up, down, route, square, hats, stage, weights, tokens_v, normed, mixed, heads, out_v,
         send_sem, recv_sem, local_sem,
     ) = refs[20:]
     net, local = Net(sizes, send_sem, recv_sem), Local(local_sem)
@@ -897,12 +897,18 @@
     from_near.wait_recv()
     view = weights.at[c, near]
     swapped.append(net.send(view, view, net.swap))
+    local.wait(own_tokens)
+    arrive(told)
+    local.copy(tokens_v, token_o)
+
+    def center(b, carry):
+        hats[b] = normalize(tokens_v[b].astype(F32))[0]
+        return carry
+
+    lax.fori_loop(0, team, center, 0)
     passed.wait_recv()
     view = weights.at[c, last]
     swapped.append(net.send(view, view, net.swap))
-    local.wait(own_tokens)
-    arrive(told)
-    local.copy(tokens_v, token_o)
     arrive(swapped)
     local.copy(weights, weight_o)
 
@@ -912,8 +918,7 @@
     vec_o[...] = small[120:, :]
 
     def norm(b, carry):
-        hat, _ = normalize(tokens_v[b].astype(F32))
-        normed[b] = (hat * vec_o[4:5, :] + vec_o[6:7, :]).astype(BF)
+        normed[b] = (hats[b] * vec_o[4:5, :] + vec_o[6:7, :]).astype(BF)
         return carry
 
     lax.fori_loop(0, team, norm, 0)
@@ -980,6 +985,7 @@
             pltpu.VMEM(up, BF),
             pltpu.VMEM((8, rows), jnp.int32),
             pltpu.VMEM((128, 128), F32),
+            pltpu.VMEM((team, rows, width), F32),
             pltpu.VMEM((team, wr, cols), BF),
             pltpu.VMEM((two, groups, team, wr, cols), BF),
             pltpu.VMEM((team, rows, width), BF),

time: 279 us -> 278 us (level)
  no operation moved by 1% of the time
where the time goes in v6:
time: 278 us; the launch traced here: 277 us
  Pallas kernels  248 us (89%)
  between operations  14.3 us (5%)
  waiting for transfers between devices  8.72 us (3%)
  starting transfers between devices  4.09 us (1%)
    pallas_call x1, Pallas kernels, whole(): pl.pallas_call(functools.partial(whole_kernel, sizes, experts, count), na...  81.4 us
    pallas_call x1, Pallas kernels, start(): pl.pallas_call(functools.partial(start_kernel, sizes), name='start', out_...  50.6 us
    pallas_call x1, Pallas kernels, end(): pl.pallas_call(functools.partial(end_kernel, sizes, experts), name='end',...  36.1 us
    pallas_call x1, Pallas kernels, exchange(): pl.pallas_call(kernel, name=name, out_shape=tuple((jax.ShapeDtypeStruct(s...  23.4 us
    pallas_call x1, Pallas kernels, sorted_attend(): pl.pallas_call(sorted_attend_kernel, name='attend', grid=(length // TILE,...  16.1 us
    pallas_call x1, Pallas kernels, sorted_back(): pl.pallas_call(sorted_back_kernel, name='attend_back', grid=(length // TI...  14.1 us
    pallas_call x2, Pallas kernels, row_sum(): pl.pallas_call(row_sum_kernel, name='row_sum', grid=(high // tile,), in_s...  12.8 us
    pallas_call x1, Pallas kernels, between(): pl.pallas_call(functools.partial(mid_kernel, experts, team), name='betwee...  9.63 us
  transfers between devices with their start and end apart: 5, of which 2 were waited for; matrix products, arithmetic and copies ran while one was open for 0% of the time, Pallas kernels for 27%

profile of v6, /device:TPU:0, one launch (start us, length us, event | category | flops | bytes accessed | tf_op | source)
XLA Modules:
  0.0 277.2 jit_solution(12743845544544118708)
XLA Ops:
  7.2 0.0 all-gather.2.cloned.1.call-start
  7.2 50.6 %start.1 = (bf16[4,128,1024]{2,1,0:T(8,128)(2,1)}, bf16[4,128,1024]{2,1,0:T(8,128)(2,1)}, bf16[4,3,64,512]{3,2,1,0:T(8,128)(2,1)}, bf16[4,128,1024]{2,1,0:T(8,12...) custom-call(bf16[128,1024]{1,0:T(8,128)(2,1)} %bitcast.43, ...), custom_call_target="tpu_custom_call" | custom-call | bytes 150000000 | tf_op jit(solution)/shard_map/start/pallas_call | solution.py:976
  57.9 0.0 all-gather.2.cloned.1.call-update
  57.9 0.2 reduce-scatter.2.cloned.1.call-start
  58.1 16.1 %attend.1 = (bf16[4,64,512]{2,1,0:T(8,128)(2,1)}, f32[64,2048]{1,0:T(8,128)}, f32[1,2048]{1,0:T(1,128)}, bf16[128,2048]{1,0:T(8,128)(2,1)}, bf16[128,2048]{1,0:T(8,128)(2,1)}, /*index=5*/bf16[2048,128]{1,0:T(8,128)(2,1)}) custom-call(s32[8]{0:T(128)} %bitcast.32, s32[32]{0:T(128)} %order.3, bf16[4,192,512]{2,1,0:T(8,128)(2,1)} %bitcast.45), custom_call_target="tpu_custom_call" | custom-call | bytes 42000000 | tf_op jit(solution)/shard_map/attend/pallas_call | solution.py:477
  74.2 23.4 %attended.1 = bf16[4,4,64,512]{3,2,1,0:T(8,128)(2,1)} custom-call(bf16[4,64,512]{2,1,0:T(8,128)(2,1)} %get-tuple-element.66.refs_0_), custom_call_target="tpu_custom_call" | custom-call | bytes 60000000 | tf_op jit(solution)/shard_map/attended/pallas_call | solution.py:138
  97.6 9.6 %between.1 = (bf16[512,1024]{1,0:T(8,128)(2,1)}, bf16[512,1024]{1,0:T(8,128)(2,1)}, bf16[4,64,1024]{2,1,0:T(8,128)(2,1)}, bf16[4,64,1024]{2,1,0:T(8,128)(2,1)}, ...) custom-call(s32[1]{0:T(128)} %bitcast.member, ...), custom_call_target="tpu_custom_call" | custom-call | tf_op jit(solution)/shard_map/between/pallas_call | solution.py:608
  107.2 4.7 %all-gather.2.cloned.1.call-done.refs_6_ = bf16[4,2,128,1024]{3,2,1,0:T(8,128)(2,1)} async-done(((bf16[1,2,128,1024]{3,2,1,0:T(8,128)(2,1)}), bf16[4,2,128,1024]{3,2,1,0:T(8,128)(2,1)}) %all-gather.2.cloned.1.call-update) | async-done | bytes 2097168 | tf_op jit(solution)/shard_map/all_gather | solution.py:2652
  111.9 0.0 copy-start.10
  111.9 81.4 %feed_forward.1 = (bf16[128,1024]{1,0:T(8,128)(2,1)}, f32[128,1024]{1,0:T(8,128)}, f32[24,1024]{1,0:T(8,128)}, bf16[4,4,64,128]{3,2,1,0:T(8,128)(2,1)}, bf16[4,3...) custom-call(bf16[4,64,1024]{2,1,0:T(8,128)(2,1)} %get-tuple-element., ...), custom_call_target="tpu_custom_call" | custom-call | bytes 300000000 | tf_op jit(solution)/shard_map/feed_forward/pallas_call | solution.py:2521
  193.3 0.0 reduce-scatter.2.cloned.1.call-update
  193.5 0.9 copy-done.8
  194.4 14.1 %attend_back.1 = bf16[4,3,64,512]{3,2,1,0:T(8,128)(2,1)S(1)} custom-call(s32[8]{0:T(128)S(1)} %bitcast.33, s32[32]{0:T(128)S(1)} %copy-done.11, bf16[16,64,128]{2,1,0:T(8,128)(2,1)S(1)} %bitcast.31, f32[64,2048]{1,0:T(8,128)S(1)} %copy-done.4, f32[1,2048]{1,0:T(1,128)S(1)} %copy-done.9, bf16[128,2048]{1,0:T(8,128)(2,1)S(1)} %copy-done.5, ...), custom_call_target="tpu_custom_call" | custom-call | bytes 42000000 | tf_op jit(solution)/shard_map/attend_back/pallas_call | solution.py:495
  208.5 0.8 dynamic-slice_bitcast_fusion
  209.3 1.4 collective-permute-start.1
  210.8 2.4 collective-permute-start.2
  213.2 6.4 %row_sum.2 = f32[1,1024,2048]{2,1,0:T(8,128)} custom-call(bf16[512,1024]{1,0:T(8,128)(2,1)S(1)} %bitcast.30, bf16[512,2048]{1,0:T(8,128)(2,1)S(1)} %copy-done.1), custom_call_target="tpu_custom_call" | custom-call | flops 2147483648 | bytes 8388608 | tf_op jit(solution)/shard_map/row_sum/pallas_call | solution.py:695
  219.6 6.4 %row_sum.3 = f32[1,2048,1024]{2,1,0:T(8,128)} custom-call(bf16[512,2048]{1,0:T(8,128)(2,1)S(1)} %copy-done, bf16[512,1024]{1,0:T(8,128)(2,1)S(1)} %bitcast.29), custom_call_target="tpu_custom_call" | custom-call | flops 2147483648 | bytes 8388608 | tf_op jit(solution)/shard_map/row_sum/pallas_call | solution.py:695
  226.0 4.0 %collective-permute-done.1.refs_2_ = bf16[3,64,512]{2,1,0:T(8,128)(2,1)S(1)} collective-permute-done((bf16[3,64,512]{2,1,0:T(8,128)(2,1)S(1)}, bf16[3,64,512]{2,1,0:T(8,128)(2,1)S(1)}, u32[]{:S(2)}, u32[]{:S(2)}) %collective-permute-start.1) | collective-permute-done | bytes 196640 | tf_op jit(solution)/shard_map/ppermute | solution.py:2764
  230.0 0.0 reduce-scatter.2.cloned.1.call-done
  230.0 0.6 copy-done.13
  230.6 0.1 copy-done.14
  230.7 36.1 %end.1 = (bf16[128,1024]{1,0:T(8,128)(2,1)}, f32[32,3072]{1,0:T(8,128)}, f32[32,4096]{1,0:T(8,128)}, f32[32,1024]{1,0:T(8,128)}, f32[24,128]{1,0:T(8,128)}) custom-call(bf16[3,64,512]{2,1,0:T(8,128)(2,1)} %get-tuple-element.122.refs_0_, bf16[3,64,512]{2,1,0:T(8,128)(2,1)} %copy-done.12, bf16[3,64,512]{2,1,0:T(8,128)(2,1)} %copy-done.13, ...), custom_call_target="tpu_custom_call" | custom-call | bytes 120000000 | tf_op jit(solution)/shard_map/end/pallas_call | solution.py:1150
  266.8 3.5 %deliver.1 = (bf16[128,1024]{1,0:T(8,128)(2,1)}, bf16[128,1024]{1,0:T(8,128)(2,1)}, f32[32,3072]{1,0:T(8,128)}, f32[32,1024]{1,0:T(8,128)}, f32[32,4096]{1,0:T(8...) custom-call(s32[1]{0:T(128)S(6)} %mul.3.shift, ...), custom_call_target="tpu_custom_call" | custom-call | tf_op jit(solution)/shard_map/deliver/pallas_call | solution.py:2564
  (29 shorter events, 0.1 us)
Async XLA Ops:
  7.2 104.7 %all-gather.2.cloned.1.call-start = ((), (), s32[]{:S(2)}) async-start(), calls=%async_computation.1 | async-start | bytes 2621440 | tf_op jit(solution)/shard_map/all_gather | solution.py:2652
  57.9 172.1 %reduce-scatter.2.cloned.1.call-start = ((), (), s32[]{:S(2)}) async-start(), calls=%async_computation.2 | async-start | bytes 1310720 | tf_op jit(solution)/shard_map/reduce_scatter | solution.py:2767
  111.9 81.5 %copy-start.4 = (f32[64,2048]{1,0:T(8,128)S(1)}, f32[64,2048]{1,0:T(8,128)}, u32[]{:S(2)}) copy-start(f32[64,2048]{1,0:T(8,128)} %get-tuple-element.85.out_ref) | copy-start | bytes 1572868
  111.9 81.5 %copy-start.5 = (bf16[128,2048]{1,0:T(8,128)(2,1)S(1)}, bf16[128,2048]{1,0:T(8,128)(2,1)}, u32[]{:S(2)}) copy-start(bf16[128,2048]{1,0:T(8,128)(2,1)} %get-tuple-element.87.q_ref) | copy-start | bytes 1572868
  111.9 81.5 %copy-start.6 = (bf16[128,2048]{1,0:T(8,128)(2,1)S(1)}, bf16[128,2048]{1,0:T(8,128)(2,1)}, u32[]{:S(2)}) copy-start(bf16[128,2048]{1,0:T(8,128)(2,1)} %get-tuple-element.88.kvt_ref) | copy-start | bytes 1572868
  111.9 81.5 %copy-start.7 = (bf16[2048,128]{1,0:T(8,128)(2,1)S(1)}, bf16[2048,128]{1,0:T(8,128)(2,1)}, u32[]{:S(2)}) copy-start(bf16[2048,128]{1,0:T(8,128)(2,1)} %get-tuple-element.89.rows_ref) | copy-start | bytes 1572868
  111.9 81.5 %copy-start.9 = (f32[1,2048]{1,0:T(1,128)S(1)}, f32[1,2048]{1,0:T(1,128)}, u32[]{:S(2)}) copy-start(f32[1,2048]{1,0:T(1,128)} %get-tuple-element.86.lse_ref) | copy-start | bytes 24580
  111.9 81.5 %copy-start.10 = (s32[1,8]{1,0:T(1,128)S(1)}, s32[1,8]{1,0:T(1,128)}, u32[]{:S(2)}) copy-start(s32[1,8]{1,0:T(1,128)} %param.17) | copy-start | bytes 100
  111.9 81.5 %copy-start.11 = (s32[32]{0:T(128)S(1)}, s32[32]{0:T(128)}, u32[]{:S(2)}) copy-start(s32[32]{0:T(128)} %order.3) | copy-start | bytes 388
  193.5 1.0 copy-start.8
  194.4 18.7 %copy-start.1 = (bf16[512,2048]{1,0:T(8,128)(2,1)S(1)}, bf16[512,2048]{1,0:T(8,128)(2,1)}, u32[]{:S(2)}) copy-start(bf16[512,2048]{1,0:T(8,128)(2,1)} %get-tuple-element.116.right) | copy-start | bytes 6291460
  194.4 18.7 %copy-start.3 = (bf16[2,4,64,1024]{3,2,1,0:T(8,128)(2,1)S(1)}, bf16[2,4,64,1024]{3,2,1,0:T(8,128)(2,1)}, u32[]{:S(2)}) copy-start(bf16[2,4,64,1024]{3,2,1,0:T(8,128)(2,1)} %get-tuple-element.115) | copy-start | bytes 3145732
  209.3 16.7 %collective-permute-start = (bf16[3,64,512]{2,1,0:T(8,128)(2,1)S(1)}, bf16[3,64,512]{2,1,0:T(8,128)(2,1)S(1)}, u32[]{:S(2)}, u32[]{:S(2)}) collective-permute-start(bf16[3,64,512]{2,1,0:T(8,128)(2,1)S(1)} %get-tuple-element.121), channel_id=1, source_target_pairs={{0,4},{1,5},{2,6},{3,7},{4,8},{5,9},{6,10},{7,11},{8,12},{9,13},{1... | collective-permute-start | bytes 589832 | tf_op jit(solution)/shard_map/ppermute | solution.py:2764
  209.3 20.6 %collective-permute-start.1 = (bf16[3,64,512]{2,1,0:T(8,128)(2,1)S(1)}, bf16[3,64,512]{2,1,0:T(8,128)(2,1)S(1)}, u32[]{:S(2)}, u32[]{:S(2)}) collective-permute-start(bf16[3,64,512]{2,1,0:T(8,128)(2,1)S(1)} %get-tuple-element.120), channel_id=1, source_target_pairs={{0,8},{1,9},{2,10},{3,11},{4,12},{5,13},{6,14},{7,15},{8,0},{9,1},... | collective-permute-start | bytes 589832 | tf_op jit(solution)/shard_map/ppermute | solution.py:2764
  210.8 19.2 %collective-permute-start.2 = (bf16[3,64,512]{2,1,0:T(8,128)(2,1)S(1)}, bf16[3,64,512]{2,1,0:T(8,128)(2,1)S(1)}, u32[]{:S(2)}, u32[]{:S(2)}) collective-permute-start(bf16[3,64,512]{2,1,0:T(8,128)(2,1)S(1)} %get-tuple-element.119), channel_id=1, source_target_pairs={{0,12},{1,13},{2,14},{3,15},{4,0},{5,1},{6,2},{7,3},{8,4},{9,5},{1... | collective-permute-start | bytes 589832 | tf_op jit(solution)/shard_map/ppermute | solution.py:2764
  213.1 6.5 %copy-start = (bf16[512,2048]{1,0:T(8,128)(2,1)S(1)}, bf16[512,2048]{1,0:T(8,128)(2,1)}, u32[]{:S(2)}) copy-start(bf16[512,2048]{1,0:T(8,128)(2,1)} %get-tuple-element.117.left) | copy-start | bytes 6291460
  213.1 6.5 %copy-start.2 = (bf16[2,4,64,1024]{3,2,1,0:T(8,128)(2,1)S(1)}, bf16[2,4,64,1024]{3,2,1,0:T(8,128)(2,1)}, u32[]{:S(2)}) copy-start(bf16[2,4,64,1024]{3,2,1,0:T(8,128)(2,1)} %get-tuple-element.118) | copy-start | bytes 3145732
  226.0 4.0 %copy-start.12 = (bf16[3,64,512]{2,1,0:T(8,128)(2,1)}, bf16[3,64,512]{2,1,0:T(8,128)(2,1)S(1)}, u32[]{:S(2)}) copy-start(bf16[3,64,512]{2,1,0:T(8,128)(2,1)S(1)} %collective-permute-done.refs_1_) | copy-start | bytes 589828
  230.0 0.7 copy-start.13
  230.0 0.7 copy-start.14
Sparse Core Ops, SparseCore 0:
  58.0 53.8 all-gather.1
  193.5 30.2 reduce-scatter.1
